TPU v7x, 32 devices: a whole 2x2x4 slice. The times are simulated.
32 devices in a mesh: row: 8 (over z, x), col: 4 (over y, core).
Axes of the slice: x: 2, y: 2, z: 4, core: 2. Of those that a mesh axis runs over, the one named last changes fastest.
Arguments:
- positions: float32 [3, 65536], P(None, ('row', 'col')), may hold values from -6 to 6
- velocities: float32 [3, 65536], P(None, ('row', 'col')), may hold values from -4 to 4
- pair_lists: int32 [8, 4, 256, 2], P('row', 'col'), may hold values from 0 to 127, as said below
- pair_counts: int32 [8, 4], P('row', 'col'), may hold values from 64 to 256, as said below
Outputs:
- positions_out: float32 [3, 65536], P(None, ('row', 'col'))
- velocities_out: float32 [3, 65536], P(None, ('row', 'col'))
Inputs may be any that keep to these rules, and one draw needn't show every extreme that they name: `pair_lists`: entry [r, c, s] holds a row block in its first place and a column block in its second; slots at or past pair_counts[r, c] hold zeros. Blocks may repeat. `pair_counts`: the first entries of pair_lists are below 64. Some device lists exactly 256 pairs.
All inputs are finite; a program needn't handle non-finite values.
Results may differ from a plain program's by a relative error of at most 0.0003.
Values sent between devices are 32-bit elements; how exact they have to be, the bound alone decides.
No kernel may reach another device: no remote copies, remote signals or barrier semaphores. Data moves between devices by JAX's collectives and lax.ppermute only.
A program may use at most 128 MiB of HBM per device.

v0:
```python
import functools

import jax
import jax.numpy as jnp
from jax import lax
from jax.experimental import pallas as pl
from jax.experimental.pallas import tpu as pltpu
from jax.sharding import PartitionSpec as P

ATOM_DEV = 2048
PAIRS_MAX = 256
STEPS = 3
TIME_STEP = 0.5
STIFFNESS = ATOM_DEV / (2048.0 * PAIRS_MAX)

LANES = 128
LIST_ROWS = 8
UNROLL = 16
BASE_MASK = (1 << 14) - 1
FAR = 1.0e6
AXES = ("row", "col")


def stage_masks(devices):
    bits = devices.bit_length() - 1
    groups = [(0, 1)] if bits else []
    low = 1
    while low < bits:
        high = min(low + 2, bits)
        groups.append((low, high))
        low = high
    return [(lo, 1 << (hi - lo)) for lo, hi in reversed(groups)]


def gather(block, devices):
    for low, count in stage_masks(devices):
        parts = [block]
        for step in range(1, count):
            pairs = [(d, d ^ (step << low)) for d in range(devices)]
            parts.append(lax.ppermute(block, AXES, pairs))
        block = jnp.concatenate(parts, 0)
    return block


def slot_of(relative, devices):
    slot = jnp.zeros_like(relative)
    stride = 1
    for low, count in stage_masks(devices):
        slot = slot + ((relative >> low) & (count - 1)) * stride
        stride *= count
    return slot


def pack_list(pairs, total, span):
    valid = jnp.arange(pairs.shape[0], dtype=jnp.int32) < total
    code = jnp.where(valid, pairs[:, 0] * span + pairs[:, 1], -1).astype(jnp.float32)
    rows = code.reshape(-1, LANES)
    return jnp.pad(rows, ((0, LIST_ROWS - rows.shape[0]), (0, 0)))


def matmul(a, b):
    return jnp.dot(a, b, preferred_element_type=jnp.float32)


def split3(tile):
    high = tile.astype(jnp.bfloat16).astype(jnp.float32)
    rest = tile - high
    mid = rest.astype(jnp.bfloat16).astype(jnp.float32)
    return high, mid, rest - mid


def evaluate(size, gathered, rows, units, points, lefts, sums):
    devices, blocks = size
    stride = 4 * blocks
    dummy = devices * stride
    for slot in range(devices):
        norm = None
        for c in range(3):
            y = 0.5 * gathered[pl.ds(slot * rows + c * blocks, blocks), :]
            points[pl.ds(slot * stride + c * blocks, blocks), :] = y
            norm = y * y if norm is None else norm + y * y
        points[pl.ds(slot * stride + 3 * blocks, blocks), :] = norm
    points[pl.ds(dummy, 3 * blocks), :] = jnp.zeros((3 * blocks, LANES), jnp.float32)
    points[pl.ds(dummy + 3 * blocks, blocks), :] = jnp.full((blocks, LANES), FAR, jnp.float32)

    place = lax.broadcasted_iota(jnp.int32, (8, LANES), 0)
    for b in range(blocks):
        tile = points[pl.ds(b, 8, stride=blocks), :]
        moved = pltpu.roll(tile, 1, 0)
        tile = jnp.where(
            place < 3, 2.0 * tile, jnp.where(place == 3, -1.0, jnp.where(place == 4, 1.0 - moved, 0.0))
        )
        high, mid, low = split3(tile)
        lefts[b] = jnp.concatenate([high, high, high, mid, mid, low], 0).astype(jnp.bfloat16)
    sums[...] = jnp.zeros_like(sums)

    def right_tile(word):
        tile = points[pl.ds(dummy - (word & BASE_MASK), 8, stride=blocks), :]
        tile = jnp.where(place < 4, tile, jnp.where(place == 4, 1.0, 0.0))
        high, mid, low = split3(tile)
        return jnp.concatenate([high, mid, low, high, mid, high], 0).astype(jnp.bfloat16)

    def group(number, carry):
        staged = []
        for k in range(UNROLL):
            at = 2 * (number * UNROLL + k)
            words = [units[(at + n) // LANES, (at + n) % LANES] for n in range(2)]
            rights = [right_tile(word) for word in words]
            mine = words[0] // (BASE_MASK + 1)
            u = matmul(jnp.concatenate([r.T for r in rights], 0), lefts[mine])
            staged.append((mine, jnp.concatenate([r[:32] for r in rights], 1), u))
        parts = []
        for mine, right, u in staged:
            w = jnp.maximum(u, 0.0)
            high = w.astype(jnp.bfloat16)
            low = (w - high.astype(jnp.float32)).astype(jnp.bfloat16)
            part = matmul(right, jnp.concatenate([high, low], 1))
            parts.append(part[:, :LANES] + part[:, LANES:])
        for (mine, _, _), part in zip(staged, parts):
            at = pl.ds(pl.multiple_of(mine * 32, 32), 32)
            sums[at, :] = sums[at, :] + part
        return carry

    count = units[units.shape[0] - 1, LANES - 1]
    lax.fori_loop(0, (count + UNROLL - 1) // UNROLL, group, 0)

    total = sums[pl.ds(4, blocks, stride=32), :]
    forces = []
    for c in range(3):
        y = points[pl.ds(c * blocks, blocks), :]
        mix = (
            sums[pl.ds(c, blocks, stride=32), :]
            + sums[pl.ds(8 + c, blocks, stride=32), :]
            + sums[pl.ds(16 + c, blocks, stride=32), :]
        )
        forces.append((2.0 * STIFFNESS) * (y * total - mix))
    return forces


def build_units(size, shape, codes, out):
    devices, blocks = size
    nrow, ncol, span = shape
    row, col = lax.axis_index("row"), lax.axis_index("col")
    me = row * ncol + col
    shift = blocks.bit_length() - 1
    cshift = ncol.bit_length() - 1
    wide = (nrow * blocks).bit_length() - 1
    code = codes[...]
    height = code.shape[0]
    holder = lax.broadcasted_iota(jnp.int32, code.shape, 0) // span
    by_row = holder < ncol
    valid = (code >= 0) & (holder < ncol + nrow)
    left, right = code >> wide, code & (nrow * blocks - 1)
    left_owner = jnp.where(by_row, row, holder - ncol) * ncol + (left >> shift)
    right_owner = ((right >> shift) << cshift) + jnp.where(by_row, holder, col)
    left_place, right_place = left & (blocks - 1), right & (blocks - 1)
    distinct = (left_owner != right_owner) | (left_place != right_place)
    mine = jnp.where(by_row, left_place, right_place)
    owner = jnp.where(by_row, left_owner, right_owner)
    valid = valid & (owner == me) & (by_row | distinct)
    other = jnp.where(by_row, right_owner, left_owner)
    place = jnp.where(by_row, right_place, left_place)
    back = (devices - slot_of(other ^ me, devices)) * (4 * blocks) - place
    mine = jnp.where(valid, mine, -1)

    ones = jnp.bfloat16
    chosen = jnp.concatenate([(mine == b).astype(jnp.float32) for b in range(blocks)], 0)
    picked = chosen.astype(ones)
    one, two = lax.broadcasted_iota(jnp.int32, (LANES, LANES), 0), lax.broadcasted_iota(jnp.int32, (LANES, LANES), 1)
    before = matmul(picked, (one < two).astype(jnp.float32).astype(ones))
    totals = matmul(picked, jnp.ones((LANES, LANES), ones))
    many = blocks * height
    one, two = lax.broadcasted_iota(jnp.int32, (many, many), 0), lax.broadcasted_iota(jnp.int32, (many, many), 1)
    earlier = ((one // height == two // height) & (two < one)).astype(jnp.float32).astype(ones)
    above = matmul(earlier, totals.astype(ones))
    offset = jnp.zeros((1, LANES), jnp.float32)
    position = jnp.zeros(code.shape, jnp.float32)
    for b in range(blocks):
        part = slice(b * height, (b + 1) * height)
        position = position + chosen[part] * (before[part] + above[part] + offset)
        last = (b + 1) * height - 1
        filled = above[last : last + 1] + totals[last : last + 1]
        offset = offset + filled + (filled.astype(jnp.int32) & 1).astype(jnp.float32)
    position = position.astype(jnp.int32)
    high = jnp.where(valid, position >> 7, -1)
    low = position & (LANES - 1)

    rows = out.shape[0]
    pieces = [(back & 63).astype(jnp.float32), (back >> 6).astype(jnp.float32), mine.astype(jnp.float32)]
    lane = lax.broadcasted_iota(jnp.int32, (LANES, LANES), 0)
    place = lax.broadcasted_iota(jnp.int32, (rows, LANES), 0)
    found = jnp.zeros((3 * rows, LANES), jnp.float32)
    for r in range(height):
        here = high[r : r + 1] == place
        weights = jnp.concatenate([jnp.where(here, p[r : r + 1], 0.0) for p in pieces], 0)
        spots = (lane == low[r : r + 1]).astype(jnp.float32)
        found = found + lax.dot_general(
            weights.astype(ones), spots.astype(ones), (((1,), (1,)), ((), ())), preferred_element_type=jnp.float32
        )
    words = found.astype(jnp.int32)
    words = words[:rows] + words[rows : 2 * rows] * 64 + words[2 * rows :] * (BASE_MASK + 1)
    end = (place == rows - 1) & (lax.broadcasted_iota(jnp.int32, (rows, LANES), 1) == LANES - 1)
    out[...] = jnp.where(end, (offset * 0.5).astype(jnp.int32), words)


def first_kernel(size, shape, gathered, velocity, x_next, force_out, units, points, lefts, sums, codes, words, sem):
    devices, blocks = size
    nrow, ncol, span = shape
    rows = 3 * blocks + LIST_ROWS
    row, col = lax.axis_index("row"), lax.axis_index("col")
    me = row * ncol + col
    holders = [row * ncol + c for c in range(ncol)] + [r * ncol + col for r in range(nrow)]
    codes[...] = jnp.full_like(codes, -1)
    for n, holder in enumerate(holders):
        slot = slot_of(holder ^ me, devices)
        tile = gathered[pl.ds(pl.multiple_of(slot * rows + 3 * blocks, 8), LIST_ROWS), :]
        codes[pl.ds(n * span, span), :] = tile[:span].astype(jnp.int32)
    build_units(size, shape, codes, words)
    copy = pltpu.make_async_copy(words, units, sem)
    copy.start()
    copy.wait()
    forces = evaluate(size, gathered, rows, units, points, lefts, sums)
    for c in range(3):
        at = pl.ds(c * blocks, blocks)
        force_out[at, :] = forces[c]
        x_next[at, :] = gathered[at, :] + TIME_STEP * velocity[at, :] + (0.5 * TIME_STEP * TIME_STEP) * forces[c]


def next_kernel(size, last, gathered, velocity, force, units, x_next, v_next, *rest):
    devices, blocks = size
    if last:
        points, lefts, sums = rest
    else:
        force_out, points, lefts, sums = rest
    forces = evaluate(size, gathered, 3 * blocks, units, points, lefts, sums)
    for c in range(3):
        at = pl.ds(c * blocks, blocks)
        x = gathered[at, :]
        v = velocity[at, :] + (0.5 * TIME_STEP) * (force[at, :] + forces[c])
        v_next[at, :] = v
        if last:
            x_next[at, :] = x
        else:
            force_out[at, :] = forces[c]
            x_next[at, :] = x + TIME_STEP * v + (0.5 * TIME_STEP * TIME_STEP) * forces[c]


def body(positions, velocities, pair_lists, pair_counts):
    nrow, ncol = lax.axis_size("row"), lax.axis_size("col")
    devices = nrow * ncol
    blocks = positions.shape[1] // LANES
    pairs = pair_lists[0, 0]
    slots = pairs.shape[0]
    size = (devices, blocks)
    span = slots // LANES
    lists = pack_list(pairs, pair_counts[0, 0], nrow * blocks)
    entries = (nrow + ncol) * slots + blocks + 2 * UNROLL
    unit_rows = 8 * (entries // (8 * LANES) + 1)
    code_rows = 8 * (-(-(nrow + ncol) * span // 8))
    current = positions.reshape(3 * blocks, LANES)
    velocity = velocities.reshape(3 * blocks, LANES)

    flat = jax.ShapeDtypeStruct((3 * blocks, LANES), jnp.float32)
    unit_list = jax.ShapeDtypeStruct((unit_rows, LANES), jnp.int32)
    vmem = pl.BlockSpec(memory_space=pltpu.VMEM)
    smem = pl.BlockSpec(memory_space=pltpu.SMEM)
    scratch = [
        pltpu.VMEM(((devices + 3) * 4 * blocks, LANES), jnp.float32),
        pltpu.VMEM((blocks, 48, LANES), jnp.bfloat16),
        pltpu.VMEM((blocks * 32, LANES), jnp.float32),
    ]
    params = pltpu.CompilerParams(vmem_limit_bytes=48 * 1024 * 1024)

    gathered = gather(jnp.concatenate([current, lists], 0), devices)
    current, force, units = pl.pallas_call(
        functools.partial(first_kernel, size, (nrow, ncol, span)),
        out_shape=[flat, flat, unit_list],
        in_specs=[vmem, vmem],
        out_specs=[vmem, vmem, smem],
        scratch_shapes=scratch
        + [
            pltpu.VMEM((code_rows, LANES), jnp.int32),
            pltpu.VMEM((unit_rows, LANES), jnp.int32),
            pltpu.SemaphoreType.DMA,
        ],
        compiler_params=params,
        name="first_forces",
    )(gathered, velocity)
    for turn in range(STEPS):
        last = turn == STEPS - 1
        result = pl.pallas_call(
            functools.partial(next_kernel, size, last),
            out_shape=[flat] * (2 if last else 3),
            in_specs=[vmem, vmem, vmem, smem],
            out_specs=[vmem] * (2 if last else 3),
            scratch_shapes=scratch,
            compiler_params=params,
            name="last_forces" if last else "next_forces",
        )(gather(current, devices), velocity, force, units)
        if last:
            current, velocity = result
        else:
            current, velocity, force = result
    return current.reshape(positions.shape), velocity.reshape(velocities.shape)


def solution(mesh):
    placed = (
        P(None, ("row", "col")),
        P(None, ("row", "col")),
        P("row", "col", None, None),
        P("row", "col"),
    )
    return jax.shard_map(
        body,
        mesh=mesh,
        in_specs=placed,
        out_specs=(P(None, ("row", "col")), P(None, ("row", "col"))),
        check_vma=False,
    )
```

profile of v0, /device:TPU:0, one launch (start us, length us, event | category | flops | bytes accessed | tf_op | source)
XLA Modules:
  0.0 125.1 jit_solution(11914942554072610826)
XLA Ops:
  2.8 3.1 %collective-permute-start = (f32[56,128]{1,0:T(8,128)S(1)}, f32[56,128]{1,0:T(8,128)S(1)}, u32[]{:S(2)}, u32[]{:S(2)}) collective-permute-start(f32[56,128]{1,0:T(8,128)S(1)} %pad_maximum_fusion), channel_id=1, source_target_pairs={{0,8},{1,9},{2,10},{3,11},{4,12},{5,13},{6,14},{7,15},{8,0},{9,1},... | collective-permute-start | bytes 86024 | tf_op jit(solution)/shard_map/ppermute | solution.py:40
  5.9 2.6 %collective-permute-start.1 = (f32[56,128]{1,0:T(8,128)S(1)}, f32[56,128]{1,0:T(8,128)S(1)}, u32[]{:S(2)}, u32[]{:S(2)}) collective-permute-start(f32[56,128]{1,0:T(8,128)S(1)} %pad_maximum_fusion), channel_id=1, source_target_pairs={{0,16},{1,17},{2,18},{3,19},{4,20},{5,21},{6,22},{7,23},{8,24},{9,... | collective-permute-start | bytes 86024 | tf_op jit(solution)/shard_map/ppermute | solution.py:40
  8.5 2.6 %collective-permute-done.1 = f32[56,128]{1,0:T(8,128)S(1)} collective-permute-done((f32[56,128]{1,0:T(8,128)S(1)}, f32[56,128]{1,0:T(8,128)S(1)}, u32[]{:S(2)}, u32[]{:S(2)}) %collective-permute-start.1) | collective-permute-done | bytes 28704 | tf_op jit(solution)/shard_map/ppermute | solution.py:40
  11.1 3.0 %collective-permute-done.2 = f32[56,128]{1,0:T(8,128)S(1)} collective-permute-done((f32[56,128]{1,0:T(8,128)S(1)}, f32[56,128]{1,0:T(8,128)S(1)}, u32[]{:S(2)}, u32[]{:S(2)}) %collective-permute-start.2) | collective-permute-done | bytes 28704 | tf_op jit(solution)/shard_map/ppermute | solution.py:40
  17.7 2.5 %collective-permute-done.3 = f32[224,128]{1,0:T(8,128)S(1)} collective-permute-done((f32[224,128]{1,0:T(8,128)S(1)}, f32[224,128]{1,0:T(8,128)S(1)}, u32[]{:S(2)}, u32[]{:S(2)}) %collective-permute-start.3) | collective-permute-done | bytes 114720 | tf_op jit(solution)/shard_map/ppermute | solution.py:40
  20.5 2.4 %collective-permute-done.5 = f32[224,128]{1,0:T(8,128)S(1)} collective-permute-done((f32[224,128]{1,0:T(8,128)S(1)}, f32[224,128]{1,0:T(8,128)S(1)}, u32[]{:S(2)}, u32[]{:S(2)}) %collective-permute-start.5) | collective-permute-done | bytes 114720 | tf_op jit(solution)/shard_map/ppermute | solution.py:40
  24.8 13.9 %first_forces.1 = (f32[48,128]{1,0:T(8,128)S(1)}, f32[48,128]{1,0:T(8,128)S(1)}, s32[32,128]{1,0:T(8,128)S(1)}) custom-call(f32[1792,128]{1,0:T(8,128)S(1)} %constant_dynamic-update-slice_fusion.13.gathered, f32[48,128]{1,0:T(8,128)S(1)} %reshape.24.velocity), custom_call_target="tpu_custom_call" | custom-call | tf_op jit(solution)/shard_map/first_forces/pallas_call | solution.py:275
  38.9 4.3 %collective-permute-start.9 = (f32[48,128]{1,0:T(8,128)S(1)}, f32[48,128]{1,0:T(8,128)S(1)}, u32[]{:S(2)}, u32[]{:S(2)}) collective-permute-start(f32[48,128]{1,0:T(8,128)S(1)} %get-tuple-element.13), channel_id=1, source_target_pairs={{0,24},{1,25},{2,26},{3,27},{4,28},{5,29},{6,30},{7,31},{8,16},{9,... | collective-permute-start | bytes 73736 | tf_op jit(solution)/shard_map/ppermute | solution.py:40
  46.1 2.7 %collective-permute-start.12 = (f32[192,128]{1,0:T(8,128)S(1)}, f32[192,128]{1,0:T(8,128)S(1)}, u32[]{:S(2)}, u32[]{:S(2)}) collective-permute-start(f32[192,128]{1,0:T(8,128)S(1)} %get-tuple-element.83), channel_id=1, source_target_pairs={{0,6},{1,7},{2,4},{3,5},{4,2},{5,3},{6,0},{7,1},{8,14},{9,15},{10,... | collective-permute-start | bytes 294920 | tf_op jit(solution)/shard_map/ppermute | solution.py:40
  48.7 2.2 %collective-permute-done.10 = f32[192,128]{1,0:T(8,128)S(1)} collective-permute-done((f32[192,128]{1,0:T(8,128)S(1)}, f32[192,128]{1,0:T(8,128)S(1)}, u32[]{:S(2)}, u32[]{:S(2)}) %collective-permute-start.10) | collective-permute-done | bytes 98336 | tf_op jit(solution)/shard_map/ppermute | solution.py:40
  52.5 1.7 %collective-permute-done.13 = f32[768,128]{1,0:T(8,128)S(1)} collective-permute-done((f32[768,128]{1,0:T(8,128)S(1)}, f32[768,128]{1,0:T(8,128)S(1)}, u32[]{:S(2)}, u32[]{:S(2)}) %collective-permute-start.13) | collective-permute-done | bytes 393248 | tf_op jit(solution)/shard_map/ppermute | solution.py:40
  54.2 11.7 %next_forces.2 = (f32[48,128]{1,0:T(8,128)S(1)}, f32[48,128]{1,0:T(8,128)S(1)}, f32[48,128]{1,0:T(8,128)S(1)}) custom-call(f32[1536,128]{1,0:T(8,128)S(1)} %constant_dynamic-update-slice_fusion.33.gathered, f32[48,128]{1,0:T(8,128)S(1)} %reshape.24.velocity, f32[48,128]{1,0:T(8,128)S(1)} %get-tuple-element.14.force, s32[32,128]{1,0:T(8,128)S(1)} %get-tuple-element.15.units), custom_call_target="tpu_custom_call" | custom-call | tf_op jit(solution)/shard_map/next_forces/pallas_call | solution.py:291
  66.4 2.9 %collective-permute-start.15 = (f32[48,128]{1,0:T(8,128)S(1)}, f32[48,128]{1,0:T(8,128)S(1)}, u32[]{:S(2)}, u32[]{:S(2)}) collective-permute-start(f32[48,128]{1,0:T(8,128)S(1)} %get-tuple-element.16), channel_id=1, source_target_pairs={{0,16},{1,17},{2,18},{3,19},{4,20},{5,21},{6,22},{7,23},{8,24},{9,... | collective-permute-start | bytes 73736 | tf_op jit(solution)/shard_map/ppermute | solution.py:40
  71.2 3.7 %collective-permute-done.16 = f32[48,128]{1,0:T(8,128)S(1)} collective-permute-done((f32[48,128]{1,0:T(8,128)S(1)}, f32[48,128]{1,0:T(8,128)S(1)}, u32[]{:S(2)}, u32[]{:S(2)}) %collective-permute-start.16) | collective-permute-done | bytes 24608 | tf_op jit(solution)/shard_map/ppermute | solution.py:40
  76.5 1.9 %collective-permute-start.19 = (f32[192,128]{1,0:T(8,128)S(1)}, f32[192,128]{1,0:T(8,128)S(1)}, u32[]{:S(2)}, u32[]{:S(2)}) collective-permute-start(f32[192,128]{1,0:T(8,128)S(1)} %get-tuple-element.71), channel_id=1, source_target_pairs={{0,6},{1,7},{2,4},{3,5},{4,2},{5,3},{6,0},{7,1},{8,14},{9,15},{10,... | collective-permute-start | bytes 294920 | tf_op jit(solution)/shard_map/ppermute | solution.py:40
  78.4 1.9 %collective-permute-done.17 = f32[192,128]{1,0:T(8,128)S(1)} collective-permute-done((f32[192,128]{1,0:T(8,128)S(1)}, f32[192,128]{1,0:T(8,128)S(1)}, u32[]{:S(2)}, u32[]{:S(2)}) %collective-permute-start.17) | collective-permute-done | bytes 98336 | tf_op jit(solution)/shard_map/ppermute | solution.py:40
  82.1 1.7 %collective-permute-done.20 = f32[768,128]{1,0:T(8,128)S(1)} collective-permute-done((f32[768,128]{1,0:T(8,128)S(1)}, f32[768,128]{1,0:T(8,128)S(1)}, u32[]{:S(2)}, u32[]{:S(2)}) %collective-permute-start.20) | collective-permute-done | bytes 393248 | tf_op jit(solution)/shard_map/ppermute | solution.py:40
  83.9 11.7 %next_forces.3 = (f32[48,128]{1,0:T(8,128)S(1)}, f32[48,128]{1,0:T(8,128)S(1)}, f32[48,128]{1,0:T(8,128)S(1)}) custom-call(f32[1536,128]{1,0:T(8,128)S(1)} %constant_dynamic-update-slice_fusion.52.gathered, f32[48,128]{1,0:T(8,128)S(1)} %get-tuple-element.17.velocity, f32[48,128]{1,0:T(8,128)S(1)} %get-tuple-element.18.force, ...), custom_call_target="tpu_custom_call" | custom-call | tf_op jit(solution)/shard_map/next_forces/pallas_call | solution.py:291
  96.6 3.4 %collective-permute-start.23 = (f32[48,128]{1,0:T(8,128)S(1)}, f32[48,128]{1,0:T(8,128)S(1)}, u32[]{:S(2)}, u32[]{:S(2)}) collective-permute-start(f32[48,128]{1,0:T(8,128)S(1)} %get-tuple-element.19), channel_id=1, source_target_pairs={{0,24},{1,25},{2,26},{3,27},{4,28},{5,29},{6,30},{7,31},{8,16},{9,... | collective-permute-start | bytes 73736 | tf_op jit(solution)/shard_map/ppermute | solution.py:40
  100.5 1.8 %collective-permute-done.23 = f32[48,128]{1,0:T(8,128)S(1)} collective-permute-done((f32[48,128]{1,0:T(8,128)S(1)}, f32[48,128]{1,0:T(8,128)S(1)}, u32[]{:S(2)}, u32[]{:S(2)}) %collective-permute-start.23) | collective-permute-done | bytes 24608 | tf_op jit(solution)/shard_map/ppermute | solution.py:40
  102.3 2.5 %collective-permute-start.24 = (f32[192,128]{1,0:T(8,128)S(1)}, f32[192,128]{1,0:T(8,128)S(1)}, u32[]{:S(2)}, u32[]{:S(2)}) collective-permute-start(f32[192,128]{1,0:T(8,128)S(1)} %get-tuple-element.59), channel_id=1, source_target_pairs={{0,2},{1,3},{2,0},{3,1},{4,6},{5,7},{6,4},{7,5},{8,10},{9,11},{10,... | collective-permute-start | bytes 294920 | tf_op jit(solution)/shard_map/ppermute | solution.py:40
  106.3 2.1 %collective-permute-done.24 = f32[192,128]{1,0:T(8,128)S(1)} collective-permute-done((f32[192,128]{1,0:T(8,128)S(1)}, f32[192,128]{1,0:T(8,128)S(1)}, u32[]{:S(2)}, u32[]{:S(2)}) %collective-permute-start.24) | collective-permute-done | bytes 98336 | tf_op jit(solution)/shard_map/ppermute | solution.py:40
  110.4 1.7 %collective-permute-done.27 = f32[768,128]{1,0:T(8,128)S(1)} collective-permute-done((f32[768,128]{1,0:T(8,128)S(1)}, f32[768,128]{1,0:T(8,128)S(1)}, u32[]{:S(2)}, u32[]{:S(2)}) %collective-permute-start.27) | collective-permute-done | bytes 393248 | tf_op jit(solution)/shard_map/ppermute | solution.py:40
  112.1 11.7 %last_forces.1 = (f32[48,128]{1,0:T(8,128)S(1)}, f32[48,128]{1,0:T(8,128)S(1)}) custom-call(f32[1536,128]{1,0:T(8,128)S(1)} %constant_dynamic-update-slice_fusion.71.gathered, f32[48,128]{1,0:T(8,128)S(1)} %get-tuple-element.20.velocity, f32[48,128]{1,0:T(8,128)S(1)} %get-tuple-element.21.force, s32[32,128]{1,0:T(8,128)S(1)} %get-tuple-element.15.units), custom_call_target="tpu_custom_call" | custom-call | tf_op jit(solution)/shard_map/last_forces/pallas_call | solution.py:291
  (80 shorter events, 23.9 us)
Async XLA Ops:
  2.8 5.7 %collective-permute-start = (f32[56,128]{1,0:T(8,128)S(1)}, f32[56,128]{1,0:T(8,128)S(1)}, u32[]{:S(2)}, u32[]{:S(2)}) collective-permute-start(f32[56,128]{1,0:T(8,128)S(1)} %pad_maximum_fusion), channel_id=1, source_target_pairs={{0,8},{1,9},{2,10},{3,11},{4,12},{5,13},{6,14},{7,15},{8,0},{9,1},... | collective-permute-start | bytes 86024 | tf_op jit(solution)/shard_map/ppermute | solution.py:40
  5.9 5.2 %collective-permute-start.1 = (f32[56,128]{1,0:T(8,128)S(1)}, f32[56,128]{1,0:T(8,128)S(1)}, u32[]{:S(2)}, u32[]{:S(2)}) collective-permute-start(f32[56,128]{1,0:T(8,128)S(1)} %pad_maximum_fusion), channel_id=1, source_target_pairs={{0,16},{1,17},{2,18},{3,19},{4,20},{5,21},{6,22},{7,23},{8,24},{9,... | collective-permute-start | bytes 86024 | tf_op jit(solution)/shard_map/ppermute | solution.py:40
  8.5 5.7 %collective-permute-start.2 = (f32[56,128]{1,0:T(8,128)S(1)}, f32[56,128]{1,0:T(8,128)S(1)}, u32[]{:S(2)}, u32[]{:S(2)}) collective-permute-start(f32[56,128]{1,0:T(8,128)S(1)} %pad_maximum_fusion), channel_id=1, source_target_pairs={{0,24},{1,25},{2,26},{3,27},{4,28},{5,29},{6,30},{7,31},{8,16},{9,... | collective-permute-start | bytes 86024 | tf_op jit(solution)/shard_map/ppermute | solution.py:40
  14.1 6.1 %collective-permute-start.3 = (f32[224,128]{1,0:T(8,128)S(1)}, f32[224,128]{1,0:T(8,128)S(1)}, u32[]{:S(2)}, u32[]{:S(2)}) collective-permute-start(f32[224,128]{1,0:T(8,128)S(1)} %get-tuple-element.50), channel_id=1, source_target_pairs={{0,2},{1,3},{2,0},{3,1},{4,6},{5,7},{6,4},{7,5},{8,10},{9,11},{10,... | collective-permute-start | bytes 344072 | tf_op jit(solution)/shard_map/ppermute | solution.py:40
  15.7 4.8 %collective-permute-start.4 = (f32[224,128]{1,0:T(8,128)S(1)}, f32[224,128]{1,0:T(8,128)S(1)}, u32[]{:S(2)}, u32[]{:S(2)}) collective-permute-start(f32[224,128]{1,0:T(8,128)S(1)} %get-tuple-element.50), channel_id=1, source_target_pairs={{0,4},{1,5},{2,6},{3,7},{4,0},{5,1},{6,2},{7,3},{8,12},{9,13},{10,... | collective-permute-start | bytes 344072 | tf_op jit(solution)/shard_map/ppermute | solution.py:40
  17.2 5.7 %collective-permute-start.5 = (f32[224,128]{1,0:T(8,128)S(1)}, f32[224,128]{1,0:T(8,128)S(1)}, u32[]{:S(2)}, u32[]{:S(2)}) collective-permute-start(f32[224,128]{1,0:T(8,128)S(1)} %get-tuple-element.50), channel_id=1, source_target_pairs={{0,6},{1,7},{2,4},{3,5},{4,2},{5,3},{6,0},{7,1},{8,14},{9,15},{10,... | collective-permute-start | bytes 344072 | tf_op jit(solution)/shard_map/ppermute | solution.py:40
  38.7 4.5 %collective-permute-start.7 = (f32[48,128]{1,0:T(8,128)S(1)}, f32[48,128]{1,0:T(8,128)S(1)}, u32[]{:S(2)}, u32[]{:S(2)}) collective-permute-start(f32[48,128]{1,0:T(8,128)S(1)} %get-tuple-element.13), channel_id=1, source_target_pairs={{0,8},{1,9},{2,10},{3,11},{4,12},{5,13},{6,14},{7,15},{8,0},{9,1},... | collective-permute-start | bytes 73736 | tf_op jit(solution)/shard_map/ppermute | solution.py:40
  38.8 4.8 %collective-permute-start.8 = (f32[48,128]{1,0:T(8,128)S(1)}, f32[48,128]{1,0:T(8,128)S(1)}, u32[]{:S(2)}, u32[]{:S(2)}) collective-permute-start(f32[48,128]{1,0:T(8,128)S(1)} %get-tuple-element.13), channel_id=1, source_target_pairs={{0,16},{1,17},{2,18},{3,19},{4,20},{5,21},{6,22},{7,23},{8,24},{9,... | collective-permute-start | bytes 73736 | tf_op jit(solution)/shard_map/ppermute | solution.py:40
  38.9 6.3 %collective-permute-start.9 = (f32[48,128]{1,0:T(8,128)S(1)}, f32[48,128]{1,0:T(8,128)S(1)}, u32[]{:S(2)}, u32[]{:S(2)}) collective-permute-start(f32[48,128]{1,0:T(8,128)S(1)} %get-tuple-element.13), channel_id=1, source_target_pairs={{0,24},{1,25},{2,26},{3,27},{4,28},{5,29},{6,30},{7,31},{8,16},{9,... | collective-permute-start | bytes 73736 | tf_op jit(solution)/shard_map/ppermute | solution.py:40
  45.3 5.7 %collective-permute-start.10 = (f32[192,128]{1,0:T(8,128)S(1)}, f32[192,128]{1,0:T(8,128)S(1)}, u32[]{:S(2)}, u32[]{:S(2)}) collective-permute-start(f32[192,128]{1,0:T(8,128)S(1)} %get-tuple-element.83), channel_id=1, source_target_pairs={{0,2},{1,3},{2,0},{3,1},{4,6},{5,7},{6,4},{7,5},{8,10},{9,11},{10,... | collective-permute-start | bytes 294920 | tf_op jit(solution)/shard_map/ppermute | solution.py:40
  46.1 5.4 %collective-permute-start.11 = (f32[192,128]{1,0:T(8,128)S(1)}, f32[192,128]{1,0:T(8,128)S(1)}, u32[]{:S(2)}, u32[]{:S(2)}) collective-permute-start(f32[192,128]{1,0:T(8,128)S(1)} %get-tuple-element.83), channel_id=1, source_target_pairs={{0,4},{1,5},{2,6},{3,7},{4,0},{5,1},{6,2},{7,3},{8,12},{9,13},{10,... | collective-permute-start | bytes 294920 | tf_op jit(solution)/shard_map/ppermute | solution.py:40
  46.1 6.3 %collective-permute-start.12 = (f32[192,128]{1,0:T(8,128)S(1)}, f32[192,128]{1,0:T(8,128)S(1)}, u32[]{:S(2)}, u32[]{:S(2)}) collective-permute-start(f32[192,128]{1,0:T(8,128)S(1)} %get-tuple-element.83), channel_id=1, source_target_pairs={{0,6},{1,7},{2,4},{3,5},{4,2},{5,3},{6,0},{7,1},{8,14},{9,15},{10,... | collective-permute-start | bytes 294920 | tf_op jit(solution)/shard_map/ppermute | solution.py:40
  66.0 4.5 %collective-permute-start.14 = (f32[48,128]{1,0:T(8,128)S(1)}, f32[48,128]{1,0:T(8,128)S(1)}, u32[]{:S(2)}, u32[]{:S(2)}) collective-permute-start(f32[48,128]{1,0:T(8,128)S(1)} %get-tuple-element.16), channel_id=1, source_target_pairs={{0,8},{1,9},{2,10},{3,11},{4,12},{5,13},{6,14},{7,15},{8,0},{9,1},... | collective-permute-start | bytes 73736 | tf_op jit(solution)/shard_map/ppermute | solution.py:40
  66.4 4.7 %collective-permute-start.15 = (f32[48,128]{1,0:T(8,128)S(1)}, f32[48,128]{1,0:T(8,128)S(1)}, u32[]{:S(2)}, u32[]{:S(2)}) collective-permute-start(f32[48,128]{1,0:T(8,128)S(1)} %get-tuple-element.16), channel_id=1, source_target_pairs={{0,16},{1,17},{2,18},{3,19},{4,20},{5,21},{6,22},{7,23},{8,24},{9,... | collective-permute-start | bytes 73736 | tf_op jit(solution)/shard_map/ppermute | solution.py:40
  69.3 5.6 %collective-permute-start.16 = (f32[48,128]{1,0:T(8,128)S(1)}, f32[48,128]{1,0:T(8,128)S(1)}, u32[]{:S(2)}, u32[]{:S(2)}) collective-permute-start(f32[48,128]{1,0:T(8,128)S(1)} %get-tuple-element.16), channel_id=1, source_target_pairs={{0,24},{1,25},{2,26},{3,27},{4,28},{5,29},{6,30},{7,31},{8,16},{9,... | collective-permute-start | bytes 73736 | tf_op jit(solution)/shard_map/ppermute | solution.py:40
  74.9 5.4 %collective-permute-start.17 = (f32[192,128]{1,0:T(8,128)S(1)}, f32[192,128]{1,0:T(8,128)S(1)}, u32[]{:S(2)}, u32[]{:S(2)}) collective-permute-start(f32[192,128]{1,0:T(8,128)S(1)} %get-tuple-element.71), channel_id=1, source_target_pairs={{0,2},{1,3},{2,0},{3,1},{4,6},{5,7},{6,4},{7,5},{8,10},{9,11},{10,... | collective-permute-start | bytes 294920 | tf_op jit(solution)/shard_map/ppermute | solution.py:40
  76.5 4.6 %collective-permute-start.18 = (f32[192,128]{1,0:T(8,128)S(1)}, f32[192,128]{1,0:T(8,128)S(1)}, u32[]{:S(2)}, u32[]{:S(2)}) collective-permute-start(f32[192,128]{1,0:T(8,128)S(1)} %get-tuple-element.71), channel_id=1, source_target_pairs={{0,4},{1,5},{2,6},{3,7},{4,0},{5,1},{6,2},{7,3},{8,12},{9,13},{10,... | collective-permute-start | bytes 294920 | tf_op jit(solution)/shard_map/ppermute | solution.py:40
  76.5 5.5 %collective-permute-start.19 = (f32[192,128]{1,0:T(8,128)S(1)}, f32[192,128]{1,0:T(8,128)S(1)}, u32[]{:S(2)}, u32[]{:S(2)}) collective-permute-start(f32[192,128]{1,0:T(8,128)S(1)} %get-tuple-element.71), channel_id=1, source_target_pairs={{0,6},{1,7},{2,4},{3,5},{4,2},{5,3},{6,0},{7,1},{8,14},{9,15},{10,... | collective-permute-start | bytes 294920 | tf_op jit(solution)/shard_map/ppermute | solution.py:40
  95.6 4.5 %collective-permute-start.21 = (f32[48,128]{1,0:T(8,128)S(1)}, f32[48,128]{1,0:T(8,128)S(1)}, u32[]{:S(2)}, u32[]{:S(2)}) collective-permute-start(f32[48,128]{1,0:T(8,128)S(1)} %get-tuple-element.19), channel_id=1, source_target_pairs={{0,8},{1,9},{2,10},{3,11},{4,12},{5,13},{6,14},{7,15},{8,0},{9,1},... | collective-permute-start | bytes 73736 | tf_op jit(solution)/shard_map/ppermute | solution.py:40
  95.7 4.8 %collective-permute-start.22 = (f32[48,128]{1,0:T(8,128)S(1)}, f32[48,128]{1,0:T(8,128)S(1)}, u32[]{:S(2)}, u32[]{:S(2)}) collective-permute-start(f32[48,128]{1,0:T(8,128)S(1)} %get-tuple-element.19), channel_id=1, source_target_pairs={{0,16},{1,17},{2,18},{3,19},{4,20},{5,21},{6,22},{7,23},{8,24},{9,... | collective-permute-start | bytes 73736 | tf_op jit(solution)/shard_map/ppermute | solution.py:40
  96.6 5.6 %collective-permute-start.23 = (f32[48,128]{1,0:T(8,128)S(1)}, f32[48,128]{1,0:T(8,128)S(1)}, u32[]{:S(2)}, u32[]{:S(2)}) collective-permute-start(f32[48,128]{1,0:T(8,128)S(1)} %get-tuple-element.19), channel_id=1, source_target_pairs={{0,24},{1,25},{2,26},{3,27},{4,28},{5,29},{6,30},{7,31},{8,16},{9,... | collective-permute-start | bytes 73736 | tf_op jit(solution)/shard_map/ppermute | solution.py:40
  102.3 6.2 %collective-permute-start.24 = (f32[192,128]{1,0:T(8,128)S(1)}, f32[192,128]{1,0:T(8,128)S(1)}, u32[]{:S(2)}, u32[]{:S(2)}) collective-permute-start(f32[192,128]{1,0:T(8,128)S(1)} %get-tuple-element.59), channel_id=1, source_target_pairs={{0,2},{1,3},{2,0},{3,1},{4,6},{5,7},{6,4},{7,5},{8,10},{9,11},{10,... | collective-permute-start | bytes 294920 | tf_op jit(solution)/shard_map/ppermute | solution.py:40
  104.8 4.6 %collective-permute-start.25 = (f32[192,128]{1,0:T(8,128)S(1)}, f32[192,128]{1,0:T(8,128)S(1)}, u32[]{:S(2)}, u32[]{:S(2)}) collective-permute-start(f32[192,128]{1,0:T(8,128)S(1)} %get-tuple-element.59), channel_id=1, source_target_pairs={{0,4},{1,5},{2,6},{3,7},{4,0},{5,1},{6,2},{7,3},{8,12},{9,13},{10,... | collective-permute-start | bytes 294920 | tf_op jit(solution)/shard_map/ppermute | solution.py:40
  104.8 5.5 %collective-permute-start.26 = (f32[192,128]{1,0:T(8,128)S(1)}, f32[192,128]{1,0:T(8,128)S(1)}, u32[]{:S(2)}, u32[]{:S(2)}) collective-permute-start(f32[192,128]{1,0:T(8,128)S(1)} %get-tuple-element.59), channel_id=1, source_target_pairs={{0,6},{1,7},{2,4},{3,5},{4,2},{5,3},{6,0},{7,1},{8,14},{9,15},{10,... | collective-permute-start | bytes 294920 | tf_op jit(solution)/shard_map/ppermute | solution.py:40
  (6 other events, 8.7 us)
where the time goes:
time: 127 us; the launch traced here: 125 us
  Pallas kernels  49 us (39%)
  waiting for transfers between devices  36.9 us (29%)
  starting transfers between devices  33.9 us (27%)
  local copies, waits for them, and re-layouts  3.77 us (3%)
  between operations  1.52 us (1%)
    ppermute x28, waiting for transfers between devices, gather(): parts.append(lax.ppermute(block, AXES, pairs))  36.9 us
    pallas_call x3, Pallas kernels, body(): pl.pallas_call(functools.partial(next_kernel, size, last), out_shape=[fla...  35.1 us
    ppermute x28, starting transfers between devices, gather(): parts.append(lax.ppermute(block, AXES, pairs))  33.9 us
    pallas_call x1, Pallas kernels, body(): pl.pallas_call(functools.partial(first_kernel, size, (nrow, ncol, span)),...  13.9 us
  transfers between devices with their start and end apart: 28, of which 24 were waited for; matrix products, arithmetic and copies ran while one was open for 0% of the time, Pallas kernels for 0%

commit v1 on v0

--- a/solution.py
+++ b/solution.py
@@ -15,7 +15,9 @@
 
 LANES = 128
 LIST_ROWS = 8
-UNROLL = 16
+UNROLL = 24
+AHEAD = 6
+BEHIND = 2
 BASE_MASK = (1 << 14) - 1
 FAR = 1.0e6
 AXES = ("row", "col")
@@ -101,24 +103,33 @@
         return jnp.concatenate([high, mid, low, high, mid, high], 0).astype(jnp.bfloat16)
 
     def group(number, carry):
-        staged = []
-        for k in range(UNROLL):
+        def weigh(k):
             at = 2 * (number * UNROLL + k)
             words = [units[(at + n) // LANES, (at + n) % LANES] for n in range(2)]
             rights = [right_tile(word) for word in words]
             mine = words[0] // (BASE_MASK + 1)
             u = matmul(jnp.concatenate([r.T for r in rights], 0), lefts[mine])
-            staged.append((mine, jnp.concatenate([r[:32] for r in rights], 1), u))
-        parts = []
-        for mine, right, u in staged:
+            return mine, jnp.concatenate([r[:32] for r in rights], 1), u
+
+        def halve(u):
             w = jnp.maximum(u, 0.0)
             high = w.astype(jnp.bfloat16)
-            low = (w - high.astype(jnp.float32)).astype(jnp.bfloat16)
-            part = matmul(right, jnp.concatenate([high, low], 1))
-            parts.append(part[:, :LANES] + part[:, LANES:])
-        for (mine, _, _), part in zip(staged, parts):
+            return jnp.concatenate([high, (w - high.astype(jnp.float32)).astype(jnp.bfloat16)], 1)
+
+        def add(mine, right, w):
+            part = matmul(right, w)
             at = pl.ds(pl.multiple_of(mine * 32, 32), 32)
-            sums[at, :] = sums[at, :] + part
+            sums[at, :] = sums[at, :] + (part[:, :LANES] + part[:, LANES:])
+
+        staged, halved = [], []
+        for k in range(UNROLL + AHEAD + BEHIND):
+            if k < UNROLL:
+                staged.append(weigh(k))
+            if 0 <= k - AHEAD < UNROLL:
+                halved.append(halve(staged[k - AHEAD][2]))
+            if k >= AHEAD + BEHIND:
+                mine, right, _ = staged[k - AHEAD - BEHIND]
+                add(mine, right, halved[k - AHEAD - BEHIND])
         return carry
 
     count = units[units.shape[0] - 1, LANES - 1]

time: 127 us -> 118 us (0.929)
  Pallas kernels: 49 us -> 37.9 us
  waiting for transfers between devices: 36.9 us -> 40.1 us
    pallas_call x3, Pallas kernels: 35.1 us -> 26.8 us  [body(): pl.pallas_call(functools.partial(next_kernel, size, last), out_shape=[fla...]
    ppermute x28, waiting for transfers between devices: 36.9 us -> 40.1 us  [gather(): parts.append(lax.ppermute(block, AXES, pairs))]
    pallas_call x1, Pallas kernels: 13.9 us -> 11.1 us  [body(): pl.pallas_call(functools.partial(first_kernel, size, (nrow, ncol, span)),...]
  transfers between devices with their start and end apart: 28 -> 28, of which waited for: 24 -> 23; matrix products, arithmetic and copies ran while one was open for 0% -> 0% of each run, Pallas kernels for 0% -> 0%
where the time goes in v1:
time: 118 us; the launch traced here: 117 us
  waiting for transfers between devices  40.1 us (34%)
  Pallas kernels  37.9 us (32%)
  starting transfers between devices  33.3 us (28%)
  local copies, waits for them, and re-layouts  3.78 us (3%)
  between operations  1.52 us (1%)
    ppermute x28, waiting for transfers between devices, gather(): parts.append(lax.ppermute(block, AXES, pairs))  40.1 us
    ppermute x28, starting transfers between devices, gather(): parts.append(lax.ppermute(block, AXES, pairs))  33.3 us
    pallas_call x3, Pallas kernels, body(): pl.pallas_call(functools.partial(next_kernel, size, last), out_shape=[fla...  26.8 us
    pallas_call x1, Pallas kernels, body(): pl.pallas_call(functools.partial(first_kernel, size, (nrow, ncol, span)),...  11.1 us
  transfers between devices with their start and end apart: 28, of which 23 were waited for; matrix products, arithmetic and copies ran while one was open for 0% of the time, Pallas kernels for 0%

profile of v1, /device:TPU:0, one launch (start us, length us, event | category | flops | bytes accessed | tf_op | source)
XLA Modules:
  0.0 116.6 jit_solution(12594922423084670806)
XLA Ops:
  2.8 3.1 %collective-permute-start = (f32[56,128]{1,0:T(8,128)S(1)}, f32[56,128]{1,0:T(8,128)S(1)}, u32[]{:S(2)}, u32[]{:S(2)}) collective-permute-start(f32[56,128]{1,0:T(8,128)S(1)} %pad_maximum_fusion), channel_id=1, source_target_pairs={{0,8},{1,9},{2,10},{3,11},{4,12},{5,13},{6,14},{7,15},{8,0},{9,1},... | collective-permute-start | bytes 86024 | tf_op jit(solution)/shard_map/ppermute | solution.py:42
  5.9 2.6 %collective-permute-start.1 = (f32[56,128]{1,0:T(8,128)S(1)}, f32[56,128]{1,0:T(8,128)S(1)}, u32[]{:S(2)}, u32[]{:S(2)}) collective-permute-start(f32[56,128]{1,0:T(8,128)S(1)} %pad_maximum_fusion), channel_id=1, source_target_pairs={{0,16},{1,17},{2,18},{3,19},{4,20},{5,21},{6,22},{7,23},{8,24},{9,... | collective-permute-start | bytes 86024 | tf_op jit(solution)/shard_map/ppermute | solution.py:42
  8.5 2.6 %collective-permute-done.1 = f32[56,128]{1,0:T(8,128)S(1)} collective-permute-done((f32[56,128]{1,0:T(8,128)S(1)}, f32[56,128]{1,0:T(8,128)S(1)}, u32[]{:S(2)}, u32[]{:S(2)}) %collective-permute-start.1) | collective-permute-done | bytes 28704 | tf_op jit(solution)/shard_map/ppermute | solution.py:42
  11.1 3.0 %collective-permute-done.2 = f32[56,128]{1,0:T(8,128)S(1)} collective-permute-done((f32[56,128]{1,0:T(8,128)S(1)}, f32[56,128]{1,0:T(8,128)S(1)}, u32[]{:S(2)}, u32[]{:S(2)}) %collective-permute-start.2) | collective-permute-done | bytes 28704 | tf_op jit(solution)/shard_map/ppermute | solution.py:42
  17.7 2.5 %collective-permute-done.3 = f32[224,128]{1,0:T(8,128)S(1)} collective-permute-done((f32[224,128]{1,0:T(8,128)S(1)}, f32[224,128]{1,0:T(8,128)S(1)}, u32[]{:S(2)}, u32[]{:S(2)}) %collective-permute-start.3) | collective-permute-done | bytes 114720 | tf_op jit(solution)/shard_map/ppermute | solution.py:42
  20.5 2.4 %collective-permute-done.5 = f32[224,128]{1,0:T(8,128)S(1)} collective-permute-done((f32[224,128]{1,0:T(8,128)S(1)}, f32[224,128]{1,0:T(8,128)S(1)}, u32[]{:S(2)}, u32[]{:S(2)}) %collective-permute-start.5) | collective-permute-done | bytes 114720 | tf_op jit(solution)/shard_map/ppermute | solution.py:42
  24.8 11.1 %first_forces.1 = (f32[48,128]{1,0:T(8,128)S(1)}, f32[48,128]{1,0:T(8,128)S(1)}, s32[32,128]{1,0:T(8,128)S(1)}) custom-call(f32[1792,128]{1,0:T(8,128)S(1)} %constant_dynamic-update-slice_fusion.13.gathered, f32[48,128]{1,0:T(8,128)S(1)} %reshape.24.velocity), custom_call_target="tpu_custom_call" | custom-call | tf_op jit(solution)/shard_map/first_forces/pallas_call | solution.py:286
  36.1 1.8 %collective-permute-start.8 = (f32[48,128]{1,0:T(8,128)S(1)}, f32[48,128]{1,0:T(8,128)S(1)}, u32[]{:S(2)}, u32[]{:S(2)}) collective-permute-start(f32[48,128]{1,0:T(8,128)S(1)} %get-tuple-element.13), channel_id=1, source_target_pairs={{0,16},{1,17},{2,18},{3,19},{4,20},{5,21},{6,22},{7,23},{8,24},{9,... | collective-permute-start | bytes 73736 | tf_op jit(solution)/shard_map/ppermute | solution.py:42
  37.9 2.5 %collective-permute-start.9 = (f32[48,128]{1,0:T(8,128)S(1)}, f32[48,128]{1,0:T(8,128)S(1)}, u32[]{:S(2)}, u32[]{:S(2)}) collective-permute-start(f32[48,128]{1,0:T(8,128)S(1)} %get-tuple-element.13), channel_id=1, source_target_pairs={{0,24},{1,25},{2,26},{3,27},{4,28},{5,29},{6,30},{7,31},{8,16},{9,... | collective-permute-start | bytes 73736 | tf_op jit(solution)/shard_map/ppermute | solution.py:42
  40.9 2.6 %collective-permute-done.9 = f32[48,128]{1,0:T(8,128)S(1)} collective-permute-done((f32[48,128]{1,0:T(8,128)S(1)}, f32[48,128]{1,0:T(8,128)S(1)}, u32[]{:S(2)}, u32[]{:S(2)}) %collective-permute-start.9) | collective-permute-done | bytes 24608 | tf_op jit(solution)/shard_map/ppermute | solution.py:42
  44.1 2.9 %collective-permute-start.12 = (f32[192,128]{1,0:T(8,128)S(1)}, f32[192,128]{1,0:T(8,128)S(1)}, u32[]{:S(2)}, u32[]{:S(2)}) collective-permute-start(f32[192,128]{1,0:T(8,128)S(1)} %get-tuple-element.83), channel_id=1, source_target_pairs={{0,6},{1,7},{2,4},{3,5},{4,2},{5,3},{6,0},{7,1},{8,14},{9,15},{10,... | collective-permute-start | bytes 294920 | tf_op jit(solution)/shard_map/ppermute | solution.py:42
  47.0 2.0 %collective-permute-done.10 = f32[192,128]{1,0:T(8,128)S(1)} collective-permute-done((f32[192,128]{1,0:T(8,128)S(1)}, f32[192,128]{1,0:T(8,128)S(1)}, u32[]{:S(2)}, u32[]{:S(2)}) %collective-permute-start.10) | collective-permute-done | bytes 98336 | tf_op jit(solution)/shard_map/ppermute | solution.py:42
  52.5 8.9 %next_forces.2 = (f32[48,128]{1,0:T(8,128)S(1)}, f32[48,128]{1,0:T(8,128)S(1)}, f32[48,128]{1,0:T(8,128)S(1)}) custom-call(f32[1536,128]{1,0:T(8,128)S(1)} %constant_dynamic-update-slice_fusion.33.gathered, f32[48,128]{1,0:T(8,128)S(1)} %reshape.24.velocity, f32[48,128]{1,0:T(8,128)S(1)} %get-tuple-element.14.force, s32[32,128]{1,0:T(8,128)S(1)} %get-tuple-element.15.units), custom_call_target="tpu_custom_call" | custom-call | tf_op jit(solution)/shard_map/next_forces/pallas_call | solution.py:302
  62.0 3.6 %collective-permute-start.15 = (f32[48,128]{1,0:T(8,128)S(1)}, f32[48,128]{1,0:T(8,128)S(1)}, u32[]{:S(2)}, u32[]{:S(2)}) collective-permute-start(f32[48,128]{1,0:T(8,128)S(1)} %get-tuple-element.16), channel_id=1, source_target_pairs={{0,16},{1,17},{2,18},{3,19},{4,20},{5,21},{6,22},{7,23},{8,24},{9,... | collective-permute-start | bytes 73736 | tf_op jit(solution)/shard_map/ppermute | solution.py:42
  67.4 3.8 %collective-permute-done.16 = f32[48,128]{1,0:T(8,128)S(1)} collective-permute-done((f32[48,128]{1,0:T(8,128)S(1)}, f32[48,128]{1,0:T(8,128)S(1)}, u32[]{:S(2)}, u32[]{:S(2)}) %collective-permute-start.16) | collective-permute-done | bytes 24608 | tf_op jit(solution)/shard_map/ppermute | solution.py:42
  71.2 1.9 %collective-permute-start.17 = (f32[192,128]{1,0:T(8,128)S(1)}, f32[192,128]{1,0:T(8,128)S(1)}, u32[]{:S(2)}, u32[]{:S(2)}) collective-permute-start(f32[192,128]{1,0:T(8,128)S(1)} %get-tuple-element.71), channel_id=1, source_target_pairs={{0,2},{1,3},{2,0},{3,1},{4,6},{5,7},{6,4},{7,5},{8,10},{9,11},{10,... | collective-permute-start | bytes 294920 | tf_op jit(solution)/shard_map/ppermute | solution.py:42
  74.7 1.9 %collective-permute-done.17 = f32[192,128]{1,0:T(8,128)S(1)} collective-permute-done((f32[192,128]{1,0:T(8,128)S(1)}, f32[192,128]{1,0:T(8,128)S(1)}, u32[]{:S(2)}, u32[]{:S(2)}) %collective-permute-start.17) | collective-permute-done | bytes 98336 | tf_op jit(solution)/shard_map/ppermute | solution.py:42
  80.5 8.9 %next_forces.3 = (f32[48,128]{1,0:T(8,128)S(1)}, f32[48,128]{1,0:T(8,128)S(1)}, f32[48,128]{1,0:T(8,128)S(1)}) custom-call(f32[1536,128]{1,0:T(8,128)S(1)} %constant_dynamic-update-slice_fusion.52.gathered, f32[48,128]{1,0:T(8,128)S(1)} %get-tuple-element.17.velocity, f32[48,128]{1,0:T(8,128)S(1)} %get-tuple-element.18.force, ...), custom_call_target="tpu_custom_call" | custom-call | tf_op jit(solution)/shard_map/next_forces/pallas_call | solution.py:302
  89.5 1.9 %collective-permute-start.22 = (f32[48,128]{1,0:T(8,128)S(1)}, f32[48,128]{1,0:T(8,128)S(1)}, u32[]{:S(2)}, u32[]{:S(2)}) collective-permute-start(f32[48,128]{1,0:T(8,128)S(1)} %get-tuple-element.19), channel_id=1, source_target_pairs={{0,16},{1,17},{2,18},{3,19},{4,20},{5,21},{6,22},{7,23},{8,24},{9,... | collective-permute-start | bytes 73736 | tf_op jit(solution)/shard_map/ppermute | solution.py:42
  91.4 2.5 %collective-permute-start.23 = (f32[48,128]{1,0:T(8,128)S(1)}, f32[48,128]{1,0:T(8,128)S(1)}, u32[]{:S(2)}, u32[]{:S(2)}) collective-permute-start(f32[48,128]{1,0:T(8,128)S(1)} %get-tuple-element.19), channel_id=1, source_target_pairs={{0,24},{1,25},{2,26},{3,27},{4,28},{5,29},{6,30},{7,31},{8,16},{9,... | collective-permute-start | bytes 73736 | tf_op jit(solution)/shard_map/ppermute | solution.py:42
  94.3 2.7 %collective-permute-done.23 = f32[48,128]{1,0:T(8,128)S(1)} collective-permute-done((f32[48,128]{1,0:T(8,128)S(1)}, f32[48,128]{1,0:T(8,128)S(1)}, u32[]{:S(2)}, u32[]{:S(2)}) %collective-permute-start.23) | collective-permute-done | bytes 24608 | tf_op jit(solution)/shard_map/ppermute | solution.py:42
  97.0 1.9 %collective-permute-start.24 = (f32[192,128]{1,0:T(8,128)S(1)}, f32[192,128]{1,0:T(8,128)S(1)}, u32[]{:S(2)}, u32[]{:S(2)}) collective-permute-start(f32[192,128]{1,0:T(8,128)S(1)} %get-tuple-element.59), channel_id=1, source_target_pairs={{0,2},{1,3},{2,0},{3,1},{4,6},{5,7},{6,4},{7,5},{8,10},{9,11},{10,... | collective-permute-start | bytes 294920 | tf_op jit(solution)/shard_map/ppermute | solution.py:42
  100.5 2.2 %collective-permute-done.24 = f32[192,128]{1,0:T(8,128)S(1)} collective-permute-done((f32[192,128]{1,0:T(8,128)S(1)}, f32[192,128]{1,0:T(8,128)S(1)}, u32[]{:S(2)}, u32[]{:S(2)}) %collective-permute-start.24) | collective-permute-done | bytes 98336 | tf_op jit(solution)/shard_map/ppermute | solution.py:42
  106.4 8.9 %last_forces.1 = (f32[48,128]{1,0:T(8,128)S(1)}, f32[48,128]{1,0:T(8,128)S(1)}) custom-call(f32[1536,128]{1,0:T(8,128)S(1)} %constant_dynamic-update-slice_fusion.71.gathered, f32[48,128]{1,0:T(8,128)S(1)} %get-tuple-element.20.velocity, f32[48,128]{1,0:T(8,128)S(1)} %get-tuple-element.21.force, s32[32,128]{1,0:T(8,128)S(1)} %get-tuple-element.15.units), custom_call_target="tpu_custom_call" | custom-call | tf_op jit(solution)/shard_map/last_forces/pallas_call | solution.py:302
  (80 shorter events, 26.6 us)
Async XLA Ops:
  2.8 5.7 %collective-permute-start = (f32[56,128]{1,0:T(8,128)S(1)}, f32[56,128]{1,0:T(8,128)S(1)}, u32[]{:S(2)}, u32[]{:S(2)}) collective-permute-start(f32[56,128]{1,0:T(8,128)S(1)} %pad_maximum_fusion), channel_id=1, source_target_pairs={{0,8},{1,9},{2,10},{3,11},{4,12},{5,13},{6,14},{7,15},{8,0},{9,1},... | collective-permute-start | bytes 86024 | tf_op jit(solution)/shard_map/ppermute | solution.py:42
  5.9 5.2 %collective-permute-start.1 = (f32[56,128]{1,0:T(8,128)S(1)}, f32[56,128]{1,0:T(8,128)S(1)}, u32[]{:S(2)}, u32[]{:S(2)}) collective-permute-start(f32[56,128]{1,0:T(8,128)S(1)} %pad_maximum_fusion), channel_id=1, source_target_pairs={{0,16},{1,17},{2,18},{3,19},{4,20},{5,21},{6,22},{7,23},{8,24},{9,... | collective-permute-start | bytes 86024 | tf_op jit(solution)/shard_map/ppermute | solution.py:42
  8.5 5.7 %collective-permute-start.2 = (f32[56,128]{1,0:T(8,128)S(1)}, f32[56,128]{1,0:T(8,128)S(1)}, u32[]{:S(2)}, u32[]{:S(2)}) collective-permute-start(f32[56,128]{1,0:T(8,128)S(1)} %pad_maximum_fusion), channel_id=1, source_target_pairs={{0,24},{1,25},{2,26},{3,27},{4,28},{5,29},{6,30},{7,31},{8,16},{9,... | collective-permute-start | bytes 86024 | tf_op jit(solution)/shard_map/ppermute | solution.py:42
  14.1 6.1 %collective-permute-start.3 = (f32[224,128]{1,0:T(8,128)S(1)}, f32[224,128]{1,0:T(8,128)S(1)}, u32[]{:S(2)}, u32[]{:S(2)}) collective-permute-start(f32[224,128]{1,0:T(8,128)S(1)} %get-tuple-element.50), channel_id=1, source_target_pairs={{0,2},{1,3},{2,0},{3,1},{4,6},{5,7},{6,4},{7,5},{8,10},{9,11},{10,... | collective-permute-start | bytes 344072 | tf_op jit(solution)/shard_map/ppermute | solution.py:42
  15.7 4.8 %collective-permute-start.4 = (f32[224,128]{1,0:T(8,128)S(1)}, f32[224,128]{1,0:T(8,128)S(1)}, u32[]{:S(2)}, u32[]{:S(2)}) collective-permute-start(f32[224,128]{1,0:T(8,128)S(1)} %get-tuple-element.50), channel_id=1, source_target_pairs={{0,4},{1,5},{2,6},{3,7},{4,0},{5,1},{6,2},{7,3},{8,12},{9,13},{10,... | collective-permute-start | bytes 344072 | tf_op jit(solution)/shard_map/ppermute | solution.py:42
  17.2 5.7 %collective-permute-start.5 = (f32[224,128]{1,0:T(8,128)S(1)}, f32[224,128]{1,0:T(8,128)S(1)}, u32[]{:S(2)}, u32[]{:S(2)}) collective-permute-start(f32[224,128]{1,0:T(8,128)S(1)} %get-tuple-element.50), channel_id=1, source_target_pairs={{0,6},{1,7},{2,4},{3,5},{4,2},{5,3},{6,0},{7,1},{8,14},{9,15},{10,... | collective-permute-start | bytes 344072 | tf_op jit(solution)/shard_map/ppermute | solution.py:42
  36.0 4.5 %collective-permute-start.7 = (f32[48,128]{1,0:T(8,128)S(1)}, f32[48,128]{1,0:T(8,128)S(1)}, u32[]{:S(2)}, u32[]{:S(2)}) collective-permute-start(f32[48,128]{1,0:T(8,128)S(1)} %get-tuple-element.13), channel_id=1, source_target_pairs={{0,8},{1,9},{2,10},{3,11},{4,12},{5,13},{6,14},{7,15},{8,0},{9,1},... | collective-permute-start | bytes 73736 | tf_op jit(solution)/shard_map/ppermute | solution.py:42
  36.1 4.8 %collective-permute-start.8 = (f32[48,128]{1,0:T(8,128)S(1)}, f32[48,128]{1,0:T(8,128)S(1)}, u32[]{:S(2)}, u32[]{:S(2)}) collective-permute-start(f32[48,128]{1,0:T(8,128)S(1)} %get-tuple-element.13), channel_id=1, source_target_pairs={{0,16},{1,17},{2,18},{3,19},{4,20},{5,21},{6,22},{7,23},{8,24},{9,... | collective-permute-start | bytes 73736 | tf_op jit(solution)/shard_map/ppermute | solution.py:42
  37.9 5.6 %collective-permute-start.9 = (f32[48,128]{1,0:T(8,128)S(1)}, f32[48,128]{1,0:T(8,128)S(1)}, u32[]{:S(2)}, u32[]{:S(2)}) collective-permute-start(f32[48,128]{1,0:T(8,128)S(1)} %get-tuple-element.13), channel_id=1, source_target_pairs={{0,24},{1,25},{2,26},{3,27},{4,28},{5,29},{6,30},{7,31},{8,16},{9,... | collective-permute-start | bytes 73736 | tf_op jit(solution)/shard_map/ppermute | solution.py:42
  43.5 5.5 %collective-permute-start.10 = (f32[192,128]{1,0:T(8,128)S(1)}, f32[192,128]{1,0:T(8,128)S(1)}, u32[]{:S(2)}, u32[]{:S(2)}) collective-permute-start(f32[192,128]{1,0:T(8,128)S(1)} %get-tuple-element.83), channel_id=1, source_target_pairs={{0,2},{1,3},{2,0},{3,1},{4,6},{5,7},{6,4},{7,5},{8,10},{9,11},{10,... | collective-permute-start | bytes 294920 | tf_op jit(solution)/shard_map/ppermute | solution.py:42
  44.0 5.0 %collective-permute-start.11 = (f32[192,128]{1,0:T(8,128)S(1)}, f32[192,128]{1,0:T(8,128)S(1)}, u32[]{:S(2)}, u32[]{:S(2)}) collective-permute-start(f32[192,128]{1,0:T(8,128)S(1)} %get-tuple-element.83), channel_id=1, source_target_pairs={{0,4},{1,5},{2,6},{3,7},{4,0},{5,1},{6,2},{7,3},{8,12},{9,13},{10,... | collective-permute-start | bytes 294920 | tf_op jit(solution)/shard_map/ppermute | solution.py:42
  44.1 6.6 %collective-permute-start.12 = (f32[192,128]{1,0:T(8,128)S(1)}, f32[192,128]{1,0:T(8,128)S(1)}, u32[]{:S(2)}, u32[]{:S(2)}) collective-permute-start(f32[192,128]{1,0:T(8,128)S(1)} %get-tuple-element.83), channel_id=1, source_target_pairs={{0,6},{1,7},{2,4},{3,5},{4,2},{5,3},{6,0},{7,1},{8,14},{9,15},{10,... | collective-permute-start | bytes 294920 | tf_op jit(solution)/shard_map/ppermute | solution.py:42
  61.4 4.5 %collective-permute-start.14 = (f32[48,128]{1,0:T(8,128)S(1)}, f32[48,128]{1,0:T(8,128)S(1)}, u32[]{:S(2)}, u32[]{:S(2)}) collective-permute-start(f32[48,128]{1,0:T(8,128)S(1)} %get-tuple-element.16), channel_id=1, source_target_pairs={{0,8},{1,9},{2,10},{3,11},{4,12},{5,13},{6,14},{7,15},{8,0},{9,1},... | collective-permute-start | bytes 73736 | tf_op jit(solution)/shard_map/ppermute | solution.py:42
  62.0 5.4 %collective-permute-start.15 = (f32[48,128]{1,0:T(8,128)S(1)}, f32[48,128]{1,0:T(8,128)S(1)}, u32[]{:S(2)}, u32[]{:S(2)}) collective-permute-start(f32[48,128]{1,0:T(8,128)S(1)} %get-tuple-element.16), channel_id=1, source_target_pairs={{0,16},{1,17},{2,18},{3,19},{4,20},{5,21},{6,22},{7,23},{8,24},{9,... | collective-permute-start | bytes 73736 | tf_op jit(solution)/shard_map/ppermute | solution.py:42
  65.6 5.6 %collective-permute-start.16 = (f32[48,128]{1,0:T(8,128)S(1)}, f32[48,128]{1,0:T(8,128)S(1)}, u32[]{:S(2)}, u32[]{:S(2)}) collective-permute-start(f32[48,128]{1,0:T(8,128)S(1)} %get-tuple-element.16), channel_id=1, source_target_pairs={{0,24},{1,25},{2,26},{3,27},{4,28},{5,29},{6,30},{7,31},{8,16},{9,... | collective-permute-start | bytes 73736 | tf_op jit(solution)/shard_map/ppermute | solution.py:42
  71.2 5.3 %collective-permute-start.17 = (f32[192,128]{1,0:T(8,128)S(1)}, f32[192,128]{1,0:T(8,128)S(1)}, u32[]{:S(2)}, u32[]{:S(2)}) collective-permute-start(f32[192,128]{1,0:T(8,128)S(1)} %get-tuple-element.71), channel_id=1, source_target_pairs={{0,2},{1,3},{2,0},{3,1},{4,6},{5,7},{6,4},{7,5},{8,10},{9,11},{10,... | collective-permute-start | bytes 294920 | tf_op jit(solution)/shard_map/ppermute | solution.py:42
  73.1 4.6 %collective-permute-start.18 = (f32[192,128]{1,0:T(8,128)S(1)}, f32[192,128]{1,0:T(8,128)S(1)}, u32[]{:S(2)}, u32[]{:S(2)}) collective-permute-start(f32[192,128]{1,0:T(8,128)S(1)} %get-tuple-element.71), channel_id=1, source_target_pairs={{0,4},{1,5},{2,6},{3,7},{4,0},{5,1},{6,2},{7,3},{8,12},{9,13},{10,... | collective-permute-start | bytes 294920 | tf_op jit(solution)/shard_map/ppermute | solution.py:42
  73.1 5.5 %collective-permute-start.19 = (f32[192,128]{1,0:T(8,128)S(1)}, f32[192,128]{1,0:T(8,128)S(1)}, u32[]{:S(2)}, u32[]{:S(2)}) collective-permute-start(f32[192,128]{1,0:T(8,128)S(1)} %get-tuple-element.71), channel_id=1, source_target_pairs={{0,6},{1,7},{2,4},{3,5},{4,2},{5,3},{6,0},{7,1},{8,14},{9,15},{10,... | collective-permute-start | bytes 294920 | tf_op jit(solution)/shard_map/ppermute | solution.py:42
  89.4 4.5 %collective-permute-start.21 = (f32[48,128]{1,0:T(8,128)S(1)}, f32[48,128]{1,0:T(8,128)S(1)}, u32[]{:S(2)}, u32[]{:S(2)}) collective-permute-start(f32[48,128]{1,0:T(8,128)S(1)} %get-tuple-element.19), channel_id=1, source_target_pairs={{0,8},{1,9},{2,10},{3,11},{4,12},{5,13},{6,14},{7,15},{8,0},{9,1},... | collective-permute-start | bytes 73736 | tf_op jit(solution)/shard_map/ppermute | solution.py:42
  89.5 4.8 %collective-permute-start.22 = (f32[48,128]{1,0:T(8,128)S(1)}, f32[48,128]{1,0:T(8,128)S(1)}, u32[]{:S(2)}, u32[]{:S(2)}) collective-permute-start(f32[48,128]{1,0:T(8,128)S(1)} %get-tuple-element.19), channel_id=1, source_target_pairs={{0,16},{1,17},{2,18},{3,19},{4,20},{5,21},{6,22},{7,23},{8,24},{9,... | collective-permute-start | bytes 73736 | tf_op jit(solution)/shard_map/ppermute | solution.py:42
  91.4 5.6 %collective-permute-start.23 = (f32[48,128]{1,0:T(8,128)S(1)}, f32[48,128]{1,0:T(8,128)S(1)}, u32[]{:S(2)}, u32[]{:S(2)}) collective-permute-start(f32[48,128]{1,0:T(8,128)S(1)} %get-tuple-element.19), channel_id=1, source_target_pairs={{0,24},{1,25},{2,26},{3,27},{4,28},{5,29},{6,30},{7,31},{8,16},{9,... | collective-permute-start | bytes 73736 | tf_op jit(solution)/shard_map/ppermute | solution.py:42
  97.0 5.7 %collective-permute-start.24 = (f32[192,128]{1,0:T(8,128)S(1)}, f32[192,128]{1,0:T(8,128)S(1)}, u32[]{:S(2)}, u32[]{:S(2)}) collective-permute-start(f32[192,128]{1,0:T(8,128)S(1)} %get-tuple-element.59), channel_id=1, source_target_pairs={{0,2},{1,3},{2,0},{3,1},{4,6},{5,7},{6,4},{7,5},{8,10},{9,11},{10,... | collective-permute-start | bytes 294920 | tf_op jit(solution)/shard_map/ppermute | solution.py:42
  99.0 4.6 %collective-permute-start.25 = (f32[192,128]{1,0:T(8,128)S(1)}, f32[192,128]{1,0:T(8,128)S(1)}, u32[]{:S(2)}, u32[]{:S(2)}) collective-permute-start(f32[192,128]{1,0:T(8,128)S(1)} %get-tuple-element.59), channel_id=1, source_target_pairs={{0,4},{1,5},{2,6},{3,7},{4,0},{5,1},{6,2},{7,3},{8,12},{9,13},{10,... | collective-permute-start | bytes 294920 | tf_op jit(solution)/shard_map/ppermute | solution.py:42
  99.0 5.5 %collective-permute-start.26 = (f32[192,128]{1,0:T(8,128)S(1)}, f32[192,128]{1,0:T(8,128)S(1)}, u32[]{:S(2)}, u32[]{:S(2)}) collective-permute-start(f32[192,128]{1,0:T(8,128)S(1)} %get-tuple-element.59), channel_id=1, source_target_pairs={{0,6},{1,7},{2,4},{3,5},{4,2},{5,3},{6,0},{7,1},{8,14},{9,15},{10,... | collective-permute-start | bytes 294920 | tf_op jit(solution)/shard_map/ppermute | solution.py:42
  (6 other events, 8.7 us)

commit v2 on v0

--- a/solution.py
+++ b/solution.py
@@ -15,8 +15,11 @@
 
 LANES = 128
 LIST_ROWS = 8
-UNROLL = 16
-BASE_MASK = (1 << 14) - 1
+UNROLL = 32
+LEAD = 4
+LAG = 8
+BASE_BITS = 14
+BASE_MASK = (1 << BASE_BITS) - 1
 FAR = 1.0e6
 AXES = ("row", "col")
 
@@ -69,7 +72,7 @@
     return high, mid, rest - mid
 
 
-def evaluate(size, gathered, rows, units, points, lefts, sums):
+def evaluate(size, gathered, rows, units, points, lefts, sums, turned_kept, right_kept, weights_kept, partner_kept):
     devices, blocks = size
     stride = 4 * blocks
     dummy = devices * stride
@@ -100,29 +103,52 @@
         high, mid, low = split3(tile)
         return jnp.concatenate([high, mid, low, high, mid, high], 0).astype(jnp.bfloat16)
 
+    def word(unit, n):
+        at = 2 * unit + n
+        return units[at >> 7, at & (LANES - 1)]
+
+    def block_of(unit):
+        return word(unit, 0) >> BASE_BITS
+
+    def fetch(unit):
+        rights = [right_tile(word(unit, n)) for n in range(2)]
+        return jnp.concatenate([r.T for r in rights], 0), jnp.concatenate([r[:32] for r in rights], 1)
+
+    def weigh(unit, turned):
+        w = jnp.maximum(matmul(turned, lefts[block_of(unit)]), 0.0)
+        high = w.astype(jnp.bfloat16)
+        return jnp.concatenate([high, (w - high.astype(jnp.float32)).astype(jnp.bfloat16)], 1)
+
+    def add(unit, right, w):
+        part = matmul(right, w)
+        at = pl.ds(pl.multiple_of(block_of(unit) * 32, 32), 32)
+        sums[at, :] = sums[at, :] + (part[:, :LANES] + part[:, LANES:])
+
+    for k in range(LEAD):
+        turned_kept[k], right_kept[k] = fetch(k)
+    weights_kept[...] = jnp.zeros_like(weights_kept)
+    partner_kept[...] = jnp.zeros_like(partner_kept)
+
     def group(number, carry):
-        staged = []
+        first = number * UNROLL
+        fetched = [(turned_kept[k], right_kept[k]) for k in range(LEAD)]
+        weighed = [(partner_kept[k], weights_kept[k]) for k in range(LAG)]
         for k in range(UNROLL):
-            at = 2 * (number * UNROLL + k)
-            words = [units[(at + n) // LANES, (at + n) % LANES] for n in range(2)]
-            rights = [right_tile(word) for word in words]
-            mine = words[0] // (BASE_MASK + 1)
-            u = matmul(jnp.concatenate([r.T for r in rights], 0), lefts[mine])
-            staged.append((mine, jnp.concatenate([r[:32] for r in rights], 1), u))
-        parts = []
-        for mine, right, u in staged:
-            w = jnp.maximum(u, 0.0)
-            high = w.astype(jnp.bfloat16)
-            low = (w - high.astype(jnp.float32)).astype(jnp.bfloat16)
-            part = matmul(right, jnp.concatenate([high, low], 1))
-            parts.append(part[:, :LANES] + part[:, LANES:])
-        for (mine, _, _), part in zip(staged, parts):
-            at = pl.ds(pl.multiple_of(mine * 32, 32), 32)
-            sums[at, :] = sums[at, :] + part
+            add(jnp.maximum(first + k - LAG, 0), *weighed[k])
+            turned, right = fetched[k]
+            weighed.append((right, weigh(first + k, turned)))
+            fetched.append(fetch(first + k + LEAD))
+        for k in range(LEAD):
+            turned_kept[k], right_kept[k] = fetched[UNROLL + k]
+        for k in range(LAG):
+            partner_kept[k], weights_kept[k] = weighed[UNROLL + k]
         return carry
 
     count = units[units.shape[0] - 1, LANES - 1]
-    lax.fori_loop(0, (count + UNROLL - 1) // UNROLL, group, 0)
+    steps = (count + UNROLL - 1) >> (UNROLL.bit_length() - 1)
+    lax.fori_loop(0, steps, group, 0)
+    for k in range(LAG):
+        add(jnp.maximum(steps * UNROLL - LAG + k, 0), partner_kept[k], weights_kept[k])
 
     total = sums[pl.ds(4, blocks, stride=32), :]
     forces = []
@@ -203,7 +229,7 @@
     out[...] = jnp.where(end, (offset * 0.5).astype(jnp.int32), words)
 
 
-def first_kernel(size, shape, gathered, velocity, x_next, force_out, units, points, lefts, sums, codes, words, sem):
+def first_kernel(size, shape, gathered, velocity, x_next, force_out, units, codes, words, sem, *scratch):
     devices, blocks = size
     nrow, ncol, span = shape
     rows = 3 * blocks + LIST_ROWS
@@ -219,7 +245,7 @@
     copy = pltpu.make_async_copy(words, units, sem)
     copy.start()
     copy.wait()
-    forces = evaluate(size, gathered, rows, units, points, lefts, sums)
+    forces = evaluate(size, gathered, rows, units, *scratch)
     for c in range(3):
         at = pl.ds(c * blocks, blocks)
         force_out[at, :] = forces[c]
@@ -229,10 +255,10 @@
 def next_kernel(size, last, gathered, velocity, force, units, x_next, v_next, *rest):
     devices, blocks = size
     if last:
-        points, lefts, sums = rest
+        scratch = rest
     else:
-        force_out, points, lefts, sums = rest
-    forces = evaluate(size, gathered, 3 * blocks, units, points, lefts, sums)
+        force_out, *scratch = rest
+    forces = evaluate(size, gathered, 3 * blocks, units, *scratch)
     for c in range(3):
         at = pl.ds(c * blocks, blocks)
         x = gathered[at, :]
@@ -254,7 +280,7 @@
     size = (devices, blocks)
     span = slots // LANES
     lists = pack_list(pairs, pair_counts[0, 0], nrow * blocks)
-    entries = (nrow + ncol) * slots + blocks + 2 * UNROLL
+    entries = (nrow + ncol) * slots + blocks + 2 * (UNROLL + LEAD)
     unit_rows = 8 * (entries // (8 * LANES) + 1)
     code_rows = 8 * (-(-(nrow + ncol) * span // 8))
     current = positions.reshape(3 * blocks, LANES)
@@ -268,6 +294,10 @@
         pltpu.VMEM(((devices + 3) * 4 * blocks, LANES), jnp.float32),
         pltpu.VMEM((blocks, 48, LANES), jnp.bfloat16),
         pltpu.VMEM((blocks * 32, LANES), jnp.float32),
+        pltpu.VMEM((LEAD, 2 * LANES, 48), jnp.bfloat16),
+        pltpu.VMEM((LEAD, 32, 2 * LANES), jnp.bfloat16),
+        pltpu.VMEM((LAG, 2 * LANES, 2 * LANES), jnp.bfloat16),
+        pltpu.VMEM((LAG, 32, 2 * LANES), jnp.bfloat16),
     ]
     params = pltpu.CompilerParams(vmem_limit_bytes=48 * 1024 * 1024)
 
@@ -277,12 +307,12 @@
         out_shape=[flat, flat, unit_list],
         in_specs=[vmem, vmem],
         out_specs=[vmem, vmem, smem],
-        scratch_shapes=scratch
-        + [
+        scratch_shapes=[
             pltpu.VMEM((code_rows, LANES), jnp.int32),
             pltpu.VMEM((unit_rows, LANES), jnp.int32),
             pltpu.SemaphoreType.DMA,
-        ],
+        ]
+        + scratch,
         compiler_params=params,
         name="first_forces",
     )(gathered, velocity)

time: 127 us -> 111 us (0.87); the launches traced: 125 us -> 112 us
  Pallas kernels: 49 us -> 32.2 us
  waiting for transfers between devices: 36.9 us -> 40.6 us
    pallas_call x3, Pallas kernels: 35.1 us -> 22.5 us  [body(): pl.pallas_call(functools.partial(next_kernel, size, last), out_shape=[fla...]
    pallas_call x1, Pallas kernels: 13.9 us -> 9.7 us  [body(): pl.pallas_call(functools.partial(first_kernel, size, (nrow, ncol, span)),...]
    ppermute x28, waiting for transfers between devices: 36.9 us -> 40.6 us  [gather(): parts.append(lax.ppermute(block, AXES, pairs))]
where the time goes in v2:
time: 111 us; the launch traced here: 112 us
  waiting for transfers between devices  40.6 us (37%)
  starting transfers between devices  34.1 us (31%)
  Pallas kernels  32.2 us (29%)
  local copies, waits for them, and re-layouts  3.77 us (3%)
  between operations  1.52 us (1%)
    ppermute x28, waiting for transfers between devices, gather(): parts.append(lax.ppermute(block, AXES, pairs))  40.6 us
    ppermute x28, starting transfers between devices, gather(): parts.append(lax.ppermute(block, AXES, pairs))  34.1 us
    pallas_call x3, Pallas kernels, body(): pl.pallas_call(functools.partial(next_kernel, size, last), out_shape=[fla...  22.5 us
    pallas_call x1, Pallas kernels, body(): pl.pallas_call(functools.partial(first_kernel, size, (nrow, ncol, span)),...  9.7 us
  transfers between devices with their start and end apart: 28, of which 24 were waited for; matrix products, arithmetic and copies ran while one was open for 0% of the time, Pallas kernels for 0%

profile of v2, /device:TPU:0, one launch (start us, length us, event | category | flops | bytes accessed | tf_op | source)
XLA Modules:
  0.0 112.2 jit_solution(10721079101482167660)
XLA Ops:
  2.8 3.1 %collective-permute-start = (f32[56,128]{1,0:T(8,128)S(1)}, f32[56,128]{1,0:T(8,128)S(1)}, u32[]{:S(2)}, u32[]{:S(2)}) collective-permute-start(f32[56,128]{1,0:T(8,128)S(1)} %pad_maximum_fusion), channel_id=1, source_target_pairs={{0,8},{1,9},{2,10},{3,11},{4,12},{5,13},{6,14},{7,15},{8,0},{9,1},... | collective-permute-start | bytes 86024 | tf_op jit(solution)/shard_map/ppermute | solution.py:43
  5.9 2.6 %collective-permute-start.1 = (f32[56,128]{1,0:T(8,128)S(1)}, f32[56,128]{1,0:T(8,128)S(1)}, u32[]{:S(2)}, u32[]{:S(2)}) collective-permute-start(f32[56,128]{1,0:T(8,128)S(1)} %pad_maximum_fusion), channel_id=1, source_target_pairs={{0,16},{1,17},{2,18},{3,19},{4,20},{5,21},{6,22},{7,23},{8,24},{9,... | collective-permute-start | bytes 86024 | tf_op jit(solution)/shard_map/ppermute | solution.py:43
  8.5 2.6 %collective-permute-done.1 = f32[56,128]{1,0:T(8,128)S(1)} collective-permute-done((f32[56,128]{1,0:T(8,128)S(1)}, f32[56,128]{1,0:T(8,128)S(1)}, u32[]{:S(2)}, u32[]{:S(2)}) %collective-permute-start.1) | collective-permute-done | bytes 28704 | tf_op jit(solution)/shard_map/ppermute | solution.py:43
  11.1 3.0 %collective-permute-done.2 = f32[56,128]{1,0:T(8,128)S(1)} collective-permute-done((f32[56,128]{1,0:T(8,128)S(1)}, f32[56,128]{1,0:T(8,128)S(1)}, u32[]{:S(2)}, u32[]{:S(2)}) %collective-permute-start.2) | collective-permute-done | bytes 28704 | tf_op jit(solution)/shard_map/ppermute | solution.py:43
  17.7 2.5 %collective-permute-done.3 = f32[224,128]{1,0:T(8,128)S(1)} collective-permute-done((f32[224,128]{1,0:T(8,128)S(1)}, f32[224,128]{1,0:T(8,128)S(1)}, u32[]{:S(2)}, u32[]{:S(2)}) %collective-permute-start.3) | collective-permute-done | bytes 114720 | tf_op jit(solution)/shard_map/ppermute | solution.py:43
  20.5 2.4 %collective-permute-done.5 = f32[224,128]{1,0:T(8,128)S(1)} collective-permute-done((f32[224,128]{1,0:T(8,128)S(1)}, f32[224,128]{1,0:T(8,128)S(1)}, u32[]{:S(2)}, u32[]{:S(2)}) %collective-permute-start.5) | collective-permute-done | bytes 114720 | tf_op jit(solution)/shard_map/ppermute | solution.py:43
  24.8 9.7 %first_forces.1 = (f32[48,128]{1,0:T(8,128)S(1)}, f32[48,128]{1,0:T(8,128)S(1)}, s32[32,128]{1,0:T(8,128)S(1)}) custom-call(f32[1792,128]{1,0:T(8,128)S(1)} %constant_dynamic-update-slice_fusion.13.gathered, f32[48,128]{1,0:T(8,128)S(1)} %reshape.24.velocity), custom_call_target="tpu_custom_call" | custom-call | tf_op jit(solution)/shard_map/first_forces/pallas_call | solution.py:305
  34.6 1.9 %collective-permute-start.8 = (f32[48,128]{1,0:T(8,128)S(1)}, f32[48,128]{1,0:T(8,128)S(1)}, u32[]{:S(2)}, u32[]{:S(2)}) collective-permute-start(f32[48,128]{1,0:T(8,128)S(1)} %get-tuple-element.13), channel_id=1, source_target_pairs={{0,16},{1,17},{2,18},{3,19},{4,20},{5,21},{6,22},{7,23},{8,24},{9,... | collective-permute-start | bytes 73736 | tf_op jit(solution)/shard_map/ppermute | solution.py:43
  36.5 2.5 %collective-permute-start.9 = (f32[48,128]{1,0:T(8,128)S(1)}, f32[48,128]{1,0:T(8,128)S(1)}, u32[]{:S(2)}, u32[]{:S(2)}) collective-permute-start(f32[48,128]{1,0:T(8,128)S(1)} %get-tuple-element.13), channel_id=1, source_target_pairs={{0,24},{1,25},{2,26},{3,27},{4,28},{5,29},{6,30},{7,31},{8,16},{9,... | collective-permute-start | bytes 73736 | tf_op jit(solution)/shard_map/ppermute | solution.py:43
  39.5 2.7 %collective-permute-done.9 = f32[48,128]{1,0:T(8,128)S(1)} collective-permute-done((f32[48,128]{1,0:T(8,128)S(1)}, f32[48,128]{1,0:T(8,128)S(1)}, u32[]{:S(2)}, u32[]{:S(2)}) %collective-permute-start.9) | collective-permute-done | bytes 24608 | tf_op jit(solution)/shard_map/ppermute | solution.py:43
  45.6 2.1 %collective-permute-done.10 = f32[192,128]{1,0:T(8,128)S(1)} collective-permute-done((f32[192,128]{1,0:T(8,128)S(1)}, f32[192,128]{1,0:T(8,128)S(1)}, u32[]{:S(2)}, u32[]{:S(2)}) %collective-permute-start.10) | collective-permute-done | bytes 98336 | tf_op jit(solution)/shard_map/ppermute | solution.py:43
  51.3 7.5 %next_forces.2 = (f32[48,128]{1,0:T(8,128)S(1)}, f32[48,128]{1,0:T(8,128)S(1)}, f32[48,128]{1,0:T(8,128)S(1)}) custom-call(f32[1536,128]{1,0:T(8,128)S(1)} %constant_dynamic-update-slice_fusion.33.gathered, f32[48,128]{1,0:T(8,128)S(1)} %reshape.24.velocity, f32[48,128]{1,0:T(8,128)S(1)} %get-tuple-element.14.force, s32[32,128]{1,0:T(8,128)S(1)} %get-tuple-element.15.units), custom_call_target="tpu_custom_call" | custom-call | tf_op jit(solution)/shard_map/next_forces/pallas_call | solution.py:321
  59.2 4.8 %collective-permute-start.15 = (f32[48,128]{1,0:T(8,128)S(1)}, f32[48,128]{1,0:T(8,128)S(1)}, u32[]{:S(2)}, u32[]{:S(2)}) collective-permute-start(f32[48,128]{1,0:T(8,128)S(1)} %get-tuple-element.16), channel_id=1, source_target_pairs={{0,16},{1,17},{2,18},{3,19},{4,20},{5,21},{6,22},{7,23},{8,24},{9,... | collective-permute-start | bytes 73736 | tf_op jit(solution)/shard_map/ppermute | solution.py:43
  64.0 1.8 %collective-permute-done.15 = f32[48,128]{1,0:T(8,128)S(1)} collective-permute-done((f32[48,128]{1,0:T(8,128)S(1)}, f32[48,128]{1,0:T(8,128)S(1)}, u32[]{:S(2)}, u32[]{:S(2)}) %collective-permute-start.15) | collective-permute-done | bytes 24608 | tf_op jit(solution)/shard_map/ppermute | solution.py:43
  65.8 3.8 %collective-permute-done.16 = f32[48,128]{1,0:T(8,128)S(1)} collective-permute-done((f32[48,128]{1,0:T(8,128)S(1)}, f32[48,128]{1,0:T(8,128)S(1)}, u32[]{:S(2)}, u32[]{:S(2)}) %collective-permute-start.16) | collective-permute-done | bytes 24608 | tf_op jit(solution)/shard_map/ppermute | solution.py:43
  70.9 2.2 %collective-permute-start.19 = (f32[192,128]{1,0:T(8,128)S(1)}, f32[192,128]{1,0:T(8,128)S(1)}, u32[]{:S(2)}, u32[]{:S(2)}) collective-permute-start(f32[192,128]{1,0:T(8,128)S(1)} %get-tuple-element.71), channel_id=1, source_target_pairs={{0,6},{1,7},{2,4},{3,5},{4,2},{5,3},{6,0},{7,1},{8,14},{9,15},{10,... | collective-permute-start | bytes 294920 | tf_op jit(solution)/shard_map/ppermute | solution.py:43
  73.1 1.9 %collective-permute-done.17 = f32[192,128]{1,0:T(8,128)S(1)} collective-permute-done((f32[192,128]{1,0:T(8,128)S(1)}, f32[192,128]{1,0:T(8,128)S(1)}, u32[]{:S(2)}, u32[]{:S(2)}) %collective-permute-start.17) | collective-permute-done | bytes 98336 | tf_op jit(solution)/shard_map/ppermute | solution.py:43
  78.6 7.5 %next_forces.3 = (f32[48,128]{1,0:T(8,128)S(1)}, f32[48,128]{1,0:T(8,128)S(1)}, f32[48,128]{1,0:T(8,128)S(1)}) custom-call(f32[1536,128]{1,0:T(8,128)S(1)} %constant_dynamic-update-slice_fusion.52.gathered, f32[48,128]{1,0:T(8,128)S(1)} %get-tuple-element.17.velocity, f32[48,128]{1,0:T(8,128)S(1)} %get-tuple-element.18.force, ...), custom_call_target="tpu_custom_call" | custom-call | tf_op jit(solution)/shard_map/next_forces/pallas_call | solution.py:321
  86.2 2.5 %collective-permute-start.22 = (f32[48,128]{1,0:T(8,128)S(1)}, f32[48,128]{1,0:T(8,128)S(1)}, u32[]{:S(2)}, u32[]{:S(2)}) collective-permute-start(f32[48,128]{1,0:T(8,128)S(1)} %get-tuple-element.19), channel_id=1, source_target_pairs={{0,16},{1,17},{2,18},{3,19},{4,20},{5,21},{6,22},{7,23},{8,24},{9,... | collective-permute-start | bytes 73736 | tf_op jit(solution)/shard_map/ppermute | solution.py:43
  88.7 1.9 %collective-permute-start.23 = (f32[48,128]{1,0:T(8,128)S(1)}, f32[48,128]{1,0:T(8,128)S(1)}, u32[]{:S(2)}, u32[]{:S(2)}) collective-permute-start(f32[48,128]{1,0:T(8,128)S(1)} %get-tuple-element.19), channel_id=1, source_target_pairs={{0,24},{1,25},{2,26},{3,27},{4,28},{5,29},{6,30},{7,31},{8,16},{9,... | collective-permute-start | bytes 73736 | tf_op jit(solution)/shard_map/ppermute | solution.py:43
  91.4 2.9 %collective-permute-done.23 = f32[48,128]{1,0:T(8,128)S(1)} collective-permute-done((f32[48,128]{1,0:T(8,128)S(1)}, f32[48,128]{1,0:T(8,128)S(1)}, u32[]{:S(2)}, u32[]{:S(2)}) %collective-permute-start.23) | collective-permute-done | bytes 24608 | tf_op jit(solution)/shard_map/ppermute | solution.py:43
  96.1 1.7 %collective-permute-start.26 = (f32[192,128]{1,0:T(8,128)S(1)}, f32[192,128]{1,0:T(8,128)S(1)}, u32[]{:S(2)}, u32[]{:S(2)}) collective-permute-start(f32[192,128]{1,0:T(8,128)S(1)} %get-tuple-element.59), channel_id=1, source_target_pairs={{0,6},{1,7},{2,4},{3,5},{4,2},{5,3},{6,0},{7,1},{8,14},{9,15},{10,... | collective-permute-start | bytes 294920 | tf_op jit(solution)/shard_map/ppermute | solution.py:43
  97.8 2.2 %collective-permute-done.24 = f32[192,128]{1,0:T(8,128)S(1)} collective-permute-done((f32[192,128]{1,0:T(8,128)S(1)}, f32[192,128]{1,0:T(8,128)S(1)}, u32[]{:S(2)}, u32[]{:S(2)}) %collective-permute-start.24) | collective-permute-done | bytes 98336 | tf_op jit(solution)/shard_map/ppermute | solution.py:43
  103.4 7.5 %last_forces.1 = (f32[48,128]{1,0:T(8,128)S(1)}, f32[48,128]{1,0:T(8,128)S(1)}) custom-call(f32[1536,128]{1,0:T(8,128)S(1)} %constant_dynamic-update-slice_fusion.71.gathered, f32[48,128]{1,0:T(8,128)S(1)} %get-tuple-element.20.velocity, f32[48,128]{1,0:T(8,128)S(1)} %get-tuple-element.21.force, s32[32,128]{1,0:T(8,128)S(1)} %get-tuple-element.15.units), custom_call_target="tpu_custom_call" | custom-call | tf_op jit(solution)/shard_map/last_forces/pallas_call | solution.py:321
  (80 shorter events, 27.6 us)
Async XLA Ops:
  2.8 5.7 %collective-permute-start = (f32[56,128]{1,0:T(8,128)S(1)}, f32[56,128]{1,0:T(8,128)S(1)}, u32[]{:S(2)}, u32[]{:S(2)}) collective-permute-start(f32[56,128]{1,0:T(8,128)S(1)} %pad_maximum_fusion), channel_id=1, source_target_pairs={{0,8},{1,9},{2,10},{3,11},{4,12},{5,13},{6,14},{7,15},{8,0},{9,1},... | collective-permute-start | bytes 86024 | tf_op jit(solution)/shard_map/ppermute | solution.py:43
  5.9 5.2 %collective-permute-start.1 = (f32[56,128]{1,0:T(8,128)S(1)}, f32[56,128]{1,0:T(8,128)S(1)}, u32[]{:S(2)}, u32[]{:S(2)}) collective-permute-start(f32[56,128]{1,0:T(8,128)S(1)} %pad_maximum_fusion), channel_id=1, source_target_pairs={{0,16},{1,17},{2,18},{3,19},{4,20},{5,21},{6,22},{7,23},{8,24},{9,... | collective-permute-start | bytes 86024 | tf_op jit(solution)/shard_map/ppermute | solution.py:43
  8.5 5.7 %collective-permute-start.2 = (f32[56,128]{1,0:T(8,128)S(1)}, f32[56,128]{1,0:T(8,128)S(1)}, u32[]{:S(2)}, u32[]{:S(2)}) collective-permute-start(f32[56,128]{1,0:T(8,128)S(1)} %pad_maximum_fusion), channel_id=1, source_target_pairs={{0,24},{1,25},{2,26},{3,27},{4,28},{5,29},{6,30},{7,31},{8,16},{9,... | collective-permute-start | bytes 86024 | tf_op jit(solution)/shard_map/ppermute | solution.py:43
  14.1 6.1 %collective-permute-start.3 = (f32[224,128]{1,0:T(8,128)S(1)}, f32[224,128]{1,0:T(8,128)S(1)}, u32[]{:S(2)}, u32[]{:S(2)}) collective-permute-start(f32[224,128]{1,0:T(8,128)S(1)} %get-tuple-element.50), channel_id=1, source_target_pairs={{0,2},{1,3},{2,0},{3,1},{4,6},{5,7},{6,4},{7,5},{8,10},{9,11},{10,... | collective-permute-start | bytes 344072 | tf_op jit(solution)/shard_map/ppermute | solution.py:43
  15.7 4.8 %collective-permute-start.4 = (f32[224,128]{1,0:T(8,128)S(1)}, f32[224,128]{1,0:T(8,128)S(1)}, u32[]{:S(2)}, u32[]{:S(2)}) collective-permute-start(f32[224,128]{1,0:T(8,128)S(1)} %get-tuple-element.50), channel_id=1, source_target_pairs={{0,4},{1,5},{2,6},{3,7},{4,0},{5,1},{6,2},{7,3},{8,12},{9,13},{10,... | collective-permute-start | bytes 344072 | tf_op jit(solution)/shard_map/ppermute | solution.py:43
  17.2 5.7 %collective-permute-start.5 = (f32[224,128]{1,0:T(8,128)S(1)}, f32[224,128]{1,0:T(8,128)S(1)}, u32[]{:S(2)}, u32[]{:S(2)}) collective-permute-start(f32[224,128]{1,0:T(8,128)S(1)} %get-tuple-element.50), channel_id=1, source_target_pairs={{0,6},{1,7},{2,4},{3,5},{4,2},{5,3},{6,0},{7,1},{8,14},{9,15},{10,... | collective-permute-start | bytes 344072 | tf_op jit(solution)/shard_map/ppermute | solution.py:43
  34.6 4.5 %collective-permute-start.7 = (f32[48,128]{1,0:T(8,128)S(1)}, f32[48,128]{1,0:T(8,128)S(1)}, u32[]{:S(2)}, u32[]{:S(2)}) collective-permute-start(f32[48,128]{1,0:T(8,128)S(1)} %get-tuple-element.13), channel_id=1, source_target_pairs={{0,8},{1,9},{2,10},{3,11},{4,12},{5,13},{6,14},{7,15},{8,0},{9,1},... | collective-permute-start | bytes 73736 | tf_op jit(solution)/shard_map/ppermute | solution.py:43
  34.6 4.8 %collective-permute-start.8 = (f32[48,128]{1,0:T(8,128)S(1)}, f32[48,128]{1,0:T(8,128)S(1)}, u32[]{:S(2)}, u32[]{:S(2)}) collective-permute-start(f32[48,128]{1,0:T(8,128)S(1)} %get-tuple-element.13), channel_id=1, source_target_pairs={{0,16},{1,17},{2,18},{3,19},{4,20},{5,21},{6,22},{7,23},{8,24},{9,... | collective-permute-start | bytes 73736 | tf_op jit(solution)/shard_map/ppermute | solution.py:43
  36.5 5.6 %collective-permute-start.9 = (f32[48,128]{1,0:T(8,128)S(1)}, f32[48,128]{1,0:T(8,128)S(1)}, u32[]{:S(2)}, u32[]{:S(2)}) collective-permute-start(f32[48,128]{1,0:T(8,128)S(1)} %get-tuple-element.13), channel_id=1, source_target_pairs={{0,24},{1,25},{2,26},{3,27},{4,28},{5,29},{6,30},{7,31},{8,16},{9,... | collective-permute-start | bytes 73736 | tf_op jit(solution)/shard_map/ppermute | solution.py:43
  42.2 5.6 %collective-permute-start.10 = (f32[192,128]{1,0:T(8,128)S(1)}, f32[192,128]{1,0:T(8,128)S(1)}, u32[]{:S(2)}, u32[]{:S(2)}) collective-permute-start(f32[192,128]{1,0:T(8,128)S(1)} %get-tuple-element.83), channel_id=1, source_target_pairs={{0,2},{1,3},{2,0},{3,1},{4,6},{5,7},{6,4},{7,5},{8,10},{9,11},{10,... | collective-permute-start | bytes 294920 | tf_op jit(solution)/shard_map/ppermute | solution.py:43
  43.7 4.6 %collective-permute-start.11 = (f32[192,128]{1,0:T(8,128)S(1)}, f32[192,128]{1,0:T(8,128)S(1)}, u32[]{:S(2)}, u32[]{:S(2)}) collective-permute-start(f32[192,128]{1,0:T(8,128)S(1)} %get-tuple-element.83), channel_id=1, source_target_pairs={{0,4},{1,5},{2,6},{3,7},{4,0},{5,1},{6,2},{7,3},{8,12},{9,13},{10,... | collective-permute-start | bytes 294920 | tf_op jit(solution)/shard_map/ppermute | solution.py:43
  43.9 5.5 %collective-permute-start.12 = (f32[192,128]{1,0:T(8,128)S(1)}, f32[192,128]{1,0:T(8,128)S(1)}, u32[]{:S(2)}, u32[]{:S(2)}) collective-permute-start(f32[192,128]{1,0:T(8,128)S(1)} %get-tuple-element.83), channel_id=1, source_target_pairs={{0,6},{1,7},{2,4},{3,5},{4,2},{5,3},{6,0},{7,1},{8,14},{9,15},{10,... | collective-permute-start | bytes 294920 | tf_op jit(solution)/shard_map/ppermute | solution.py:43
  58.8 5.2 %collective-permute-start.14 = (f32[48,128]{1,0:T(8,128)S(1)}, f32[48,128]{1,0:T(8,128)S(1)}, u32[]{:S(2)}, u32[]{:S(2)}) collective-permute-start(f32[48,128]{1,0:T(8,128)S(1)} %get-tuple-element.16), channel_id=1, source_target_pairs={{0,8},{1,9},{2,10},{3,11},{4,12},{5,13},{6,14},{7,15},{8,0},{9,1},... | collective-permute-start | bytes 73736 | tf_op jit(solution)/shard_map/ppermute | solution.py:43
  59.2 6.6 %collective-permute-start.15 = (f32[48,128]{1,0:T(8,128)S(1)}, f32[48,128]{1,0:T(8,128)S(1)}, u32[]{:S(2)}, u32[]{:S(2)}) collective-permute-start(f32[48,128]{1,0:T(8,128)S(1)} %get-tuple-element.16), channel_id=1, source_target_pairs={{0,16},{1,17},{2,18},{3,19},{4,20},{5,21},{6,22},{7,23},{8,24},{9,... | collective-permute-start | bytes 73736 | tf_op jit(solution)/shard_map/ppermute | solution.py:43
  64.0 5.6 %collective-permute-start.16 = (f32[48,128]{1,0:T(8,128)S(1)}, f32[48,128]{1,0:T(8,128)S(1)}, u32[]{:S(2)}, u32[]{:S(2)}) collective-permute-start(f32[48,128]{1,0:T(8,128)S(1)} %get-tuple-element.16), channel_id=1, source_target_pairs={{0,24},{1,25},{2,26},{3,27},{4,28},{5,29},{6,30},{7,31},{8,16},{9,... | collective-permute-start | bytes 73736 | tf_op jit(solution)/shard_map/ppermute | solution.py:43
  69.6 5.3 %collective-permute-start.17 = (f32[192,128]{1,0:T(8,128)S(1)}, f32[192,128]{1,0:T(8,128)S(1)}, u32[]{:S(2)}, u32[]{:S(2)}) collective-permute-start(f32[192,128]{1,0:T(8,128)S(1)} %get-tuple-element.71), channel_id=1, source_target_pairs={{0,2},{1,3},{2,0},{3,1},{4,6},{5,7},{6,4},{7,5},{8,10},{9,11},{10,... | collective-permute-start | bytes 294920 | tf_op jit(solution)/shard_map/ppermute | solution.py:43
  70.9 4.6 %collective-permute-start.18 = (f32[192,128]{1,0:T(8,128)S(1)}, f32[192,128]{1,0:T(8,128)S(1)}, u32[]{:S(2)}, u32[]{:S(2)}) collective-permute-start(f32[192,128]{1,0:T(8,128)S(1)} %get-tuple-element.71), channel_id=1, source_target_pairs={{0,4},{1,5},{2,6},{3,7},{4,0},{5,1},{6,2},{7,3},{8,12},{9,13},{10,... | collective-permute-start | bytes 294920 | tf_op jit(solution)/shard_map/ppermute | solution.py:43
  70.9 5.8 %collective-permute-start.19 = (f32[192,128]{1,0:T(8,128)S(1)}, f32[192,128]{1,0:T(8,128)S(1)}, u32[]{:S(2)}, u32[]{:S(2)}) collective-permute-start(f32[192,128]{1,0:T(8,128)S(1)} %get-tuple-element.71), channel_id=1, source_target_pairs={{0,6},{1,7},{2,4},{3,5},{4,2},{5,3},{6,0},{7,1},{8,14},{9,15},{10,... | collective-permute-start | bytes 294920 | tf_op jit(solution)/shard_map/ppermute | solution.py:43
  86.1 4.5 %collective-permute-start.21 = (f32[48,128]{1,0:T(8,128)S(1)}, f32[48,128]{1,0:T(8,128)S(1)}, u32[]{:S(2)}, u32[]{:S(2)}) collective-permute-start(f32[48,128]{1,0:T(8,128)S(1)} %get-tuple-element.19), channel_id=1, source_target_pairs={{0,8},{1,9},{2,10},{3,11},{4,12},{5,13},{6,14},{7,15},{8,0},{9,1},... | collective-permute-start | bytes 73736 | tf_op jit(solution)/shard_map/ppermute | solution.py:43
  86.2 5.2 %collective-permute-start.22 = (f32[48,128]{1,0:T(8,128)S(1)}, f32[48,128]{1,0:T(8,128)S(1)}, u32[]{:S(2)}, u32[]{:S(2)}) collective-permute-start(f32[48,128]{1,0:T(8,128)S(1)} %get-tuple-element.19), channel_id=1, source_target_pairs={{0,16},{1,17},{2,18},{3,19},{4,20},{5,21},{6,22},{7,23},{8,24},{9,... | collective-permute-start | bytes 73736 | tf_op jit(solution)/shard_map/ppermute | solution.py:43
  88.7 5.6 %collective-permute-start.23 = (f32[48,128]{1,0:T(8,128)S(1)}, f32[48,128]{1,0:T(8,128)S(1)}, u32[]{:S(2)}, u32[]{:S(2)}) collective-permute-start(f32[48,128]{1,0:T(8,128)S(1)} %get-tuple-element.19), channel_id=1, source_target_pairs={{0,24},{1,25},{2,26},{3,27},{4,28},{5,29},{6,30},{7,31},{8,16},{9,... | collective-permute-start | bytes 73736 | tf_op jit(solution)/shard_map/ppermute | solution.py:43
  94.3 5.7 %collective-permute-start.24 = (f32[192,128]{1,0:T(8,128)S(1)}, f32[192,128]{1,0:T(8,128)S(1)}, u32[]{:S(2)}, u32[]{:S(2)}) collective-permute-start(f32[192,128]{1,0:T(8,128)S(1)} %get-tuple-element.59), channel_id=1, source_target_pairs={{0,2},{1,3},{2,0},{3,1},{4,6},{5,7},{6,4},{7,5},{8,10},{9,11},{10,... | collective-permute-start | bytes 294920 | tf_op jit(solution)/shard_map/ppermute | solution.py:43
  96.0 4.6 %collective-permute-start.25 = (f32[192,128]{1,0:T(8,128)S(1)}, f32[192,128]{1,0:T(8,128)S(1)}, u32[]{:S(2)}, u32[]{:S(2)}) collective-permute-start(f32[192,128]{1,0:T(8,128)S(1)} %get-tuple-element.59), channel_id=1, source_target_pairs={{0,4},{1,5},{2,6},{3,7},{4,0},{5,1},{6,2},{7,3},{8,12},{9,13},{10,... | collective-permute-start | bytes 294920 | tf_op jit(solution)/shard_map/ppermute | solution.py:43
  96.1 5.5 %collective-permute-start.26 = (f32[192,128]{1,0:T(8,128)S(1)}, f32[192,128]{1,0:T(8,128)S(1)}, u32[]{:S(2)}, u32[]{:S(2)}) collective-permute-start(f32[192,128]{1,0:T(8,128)S(1)} %get-tuple-element.59), channel_id=1, source_target_pairs={{0,6},{1,7},{2,4},{3,5},{4,2},{5,3},{6,0},{7,1},{8,14},{9,15},{10,... | collective-permute-start | bytes 294920 | tf_op jit(solution)/shard_map/ppermute | solution.py:43
  (6 other events, 8.7 us)

commit v3 on v2

--- a/solution.py
+++ b/solution.py
@@ -35,30 +35,58 @@
     return [(lo, 1 << (hi - lo)) for lo, hi in reversed(groups)]
 
 
+def send(block, devices, mask):
+    return lax.ppermute(block, AXES, [(d, d ^ mask(d)) for d in range(devices)])
+
+
 def gather(block, devices):
-    for low, count in stage_masks(devices):
-        parts = [block]
-        for step in range(1, count):
-            pairs = [(d, d ^ (step << low)) for d in range(devices)]
-            parts.append(lax.ppermute(block, AXES, pairs))
-        block = jnp.concatenate(parts, 0)
-    return block
-
-
-def slot_of(relative, devices):
-    slot = jnp.zeros_like(relative)
-    stride = 1
-    for low, count in stage_masks(devices):
-        slot = slot + ((relative >> low) & (count - 1)) * stride
-        stride *= count
-    return slot
-
-
-def pack_list(pairs, total, span):
-    valid = jnp.arange(pairs.shape[0], dtype=jnp.int32) < total
-    code = jnp.where(valid, pairs[:, 0] * span + pairs[:, 1], -1).astype(jnp.float32)
-    rows = code.reshape(-1, LANES)
-    return jnp.pad(rows, ((0, LIST_ROWS - rows.shape[0]), (0, 0)))
+    stages = stage_masks(devices)[:-1]
+    near, far, missing = block, None, [block]
+    for number, (low, count) in enumerate(stages):
+        if number == 0 and count == 4:
+            far = send(block, devices, lambda d: 1)
+            both = jnp.concatenate([near, far], 0)
+            third = send(near, devices, lambda d: 3 << low)
+            whole = send(both, devices, lambda d: (1 + d % 2) << low)
+            missing = [whole, third]
+            near = jnp.concatenate([near] + missing, 0)
+        else:
+            parts = [send(near, devices, lambda d: step << low) for step in range(1, count)]
+            missing = missing + parts
+            near = jnp.concatenate([near] + parts, 0)
+    rest = send(jnp.concatenate(missing, 0), devices, lambda d: 1)
+    return jnp.concatenate([near, rest] if far is None else [near, far, rest], 0)
+
+
+def slot_of(owner, me, devices):
+    relative = owner ^ me
+    holder = owner & 1
+    place = jnp.zeros_like(relative)
+    size = 1
+    for number, (low, count) in enumerate(stage_masks(devices)[:-1]):
+        step = (relative >> low) & (count - 1)
+        if number == 0 and count == 4:
+            fetcher = jnp.where((step == 1) | (step == 2), step - 1, holder)
+            place = jnp.where(step == 0, place, jnp.where(step == 3, 3, 1 + (holder ^ fetcher)))
+            holder = fetcher
+        else:
+            place = place + step * size
+        size *= count
+    return place + (holder ^ (me & 1)) * size
+
+
+def prepare_kernel(blocks, span, positions, velocities, pairs, total, out, velocity):
+    slots = pairs.shape[1]
+    for c in range(3):
+        for b in range(blocks):
+            at, lanes = pl.ds(c * blocks + b, 1), pl.ds(b * LANES, LANES)
+            out[at, :] = positions[pl.ds(c, 1), lanes]
+            velocity[at, :] = velocities[pl.ds(c, 1), lanes]
+    live = lax.broadcasted_iota(jnp.int32, (1, slots), 1) < total[0, 0]
+    code = jnp.where(live, pairs[0:1, :] * span + pairs[1:2, :], -1).astype(jnp.float32)
+    out[pl.ds(3 * blocks, LIST_ROWS), :] = jnp.zeros((LIST_ROWS, LANES), jnp.float32)
+    for r in range(slots // LANES):
+        out[pl.ds(3 * blocks + r, 1), :] = code[:, r * LANES : (r + 1) * LANES]
 
 
 def matmul(a, b):
@@ -186,7 +214,7 @@
     valid = valid & (owner == me) & (by_row | distinct)
     other = jnp.where(by_row, right_owner, left_owner)
     place = jnp.where(by_row, right_place, left_place)
-    back = (devices - slot_of(other ^ me, devices)) * (4 * blocks) - place
+    back = (devices - slot_of(other, me, devices)) * (4 * blocks) - place
     mine = jnp.where(valid, mine, -1)
 
     ones = jnp.bfloat16
@@ -238,7 +266,7 @@
     holders = [row * ncol + c for c in range(ncol)] + [r * ncol + col for r in range(nrow)]
     codes[...] = jnp.full_like(codes, -1)
     for n, holder in enumerate(holders):
-        slot = slot_of(holder ^ me, devices)
+        slot = slot_of(holder, me, devices)
         tile = gathered[pl.ds(pl.multiple_of(slot * rows + 3 * blocks, 8), LIST_ROWS), :]
         codes[pl.ds(n * span, span), :] = tile[:span].astype(jnp.int32)
     build_units(size, shape, codes, words)
@@ -263,10 +291,13 @@
         at = pl.ds(c * blocks, blocks)
         x = gathered[at, :]
         v = velocity[at, :] + (0.5 * TIME_STEP) * (force[at, :] + forces[c])
-        v_next[at, :] = v
         if last:
-            x_next[at, :] = x
+            for b in range(blocks):
+                lanes = pl.ds(b * LANES, LANES)
+                x_next[pl.ds(c, 1), lanes] = x[b : b + 1]
+                v_next[pl.ds(c, 1), lanes] = v[b : b + 1]
         else:
+            v_next[at, :] = v
             force_out[at, :] = forces[c]
             x_next[at, :] = x + TIME_STEP * v + (0.5 * TIME_STEP * TIME_STEP) * forces[c]
 
@@ -279,14 +310,11 @@
     slots = pairs.shape[0]
     size = (devices, blocks)
     span = slots // LANES
-    lists = pack_list(pairs, pair_counts[0, 0], nrow * blocks)
     entries = (nrow + ncol) * slots + blocks + 2 * (UNROLL + LEAD)
     unit_rows = 8 * (entries // (8 * LANES) + 1)
     code_rows = 8 * (-(-(nrow + ncol) * span // 8))
-    current = positions.reshape(3 * blocks, LANES)
-    velocity = velocities.reshape(3 * blocks, LANES)
-
     flat = jax.ShapeDtypeStruct((3 * blocks, LANES), jnp.float32)
+    whole = jax.ShapeDtypeStruct(positions.shape, jnp.float32)
     unit_list = jax.ShapeDtypeStruct((unit_rows, LANES), jnp.int32)
     vmem = pl.BlockSpec(memory_space=pltpu.VMEM)
     smem = pl.BlockSpec(memory_space=pltpu.SMEM)
@@ -301,7 +329,14 @@
     ]
     params = pltpu.CompilerParams(vmem_limit_bytes=48 * 1024 * 1024)
 
-    gathered = gather(jnp.concatenate([current, lists], 0), devices)
+    packed, velocity = pl.pallas_call(
+        functools.partial(prepare_kernel, blocks, nrow * blocks),
+        out_shape=[jax.ShapeDtypeStruct((3 * blocks + LIST_ROWS, LANES), jnp.float32), flat],
+        in_specs=[vmem, vmem, vmem, smem],
+        out_specs=[vmem, vmem],
+        name="prepare",
+    )(positions, velocities, pairs.T, pair_counts)
+    gathered = gather(packed, devices)
     current, force, units = pl.pallas_call(
         functools.partial(first_kernel, size, (nrow, ncol, span)),
         out_shape=[flat, flat, unit_list],
@@ -320,7 +355,7 @@
         last = turn == STEPS - 1
         result = pl.pallas_call(
             functools.partial(next_kernel, size, last),
-            out_shape=[flat] * (2 if last else 3),
+            out_shape=[whole] * 2 if last else [flat] * 3,
             in_specs=[vmem, vmem, vmem, smem],
             out_specs=[vmem] * (2 if last else 3),
             scratch_shapes=scratch,
@@ -331,7 +366,7 @@
             current, velocity = result
         else:
             current, velocity, force = result
-    return current.reshape(positions.shape), velocity.reshape(velocities.shape)
+    return current, velocity
 
 
 def solution(mesh):

time: 111 us -> 106 us (0.955); the launches traced: 112 us -> 106 us
  starting transfers between devices: 34.1 us -> 30.4 us
  local copies, waits for them, and re-layouts: 3.77 us -> 0.4 us
  Pallas kernels: 32.2 us -> 30.2 us
  waiting for transfers between devices: 40.6 us -> 42.4 us
    ppermute x28, starting transfers between devices: 34.1 us -> 30.4 us  [send(): return lax.ppermute(block, AXES, [(d, d ^ mask(d)) for d in range(devices)])]
    reshape x4 -> x0, local copies, waits for them, and re-layouts: 2.05 us -> none  [the longest x1 0.78 us: body(): current = positions.reshape(3 * blocks, LANES)]
    ppermute x28, waiting for transfers between devices: 40.6 us -> 42.4 us  [send(): return lax.ppermute(block, AXES, [(d, d ^ mask(d)) for d in range(devices)])]
    unnamed x29 -> x28, local copies, waits for them, and re-layouts: 1.55 us -> 0.24 us
    pallas_call x3 -> x4, Pallas kernels: 22.5 us -> 21.5 us  [the longest x3 20 us: body(): pl.pallas_call(functools.partial(next_kernel, size, last), out_shape=[who...]
  transfers between devices with their start and end apart: 28 -> 28, of which waited for: 24 -> 26; matrix products, arithmetic and copies ran while one was open for 0% -> 1% of each run, Pallas kernels for 0% -> 0%
where the time goes in v3:
time: 106 us
  waiting for transfers between devices  42.4 us (40%)
  starting transfers between devices  30.4 us (29%)
  Pallas kernels  30.2 us (28%)
  between operations  1.52 us (1%)
    ppermute x28, waiting for transfers between devices, send(): return lax.ppermute(block, AXES, [(d, d ^ mask(d)) for d in range(devices)])  42.4 us
    ppermute x28, starting transfers between devices, send(): return lax.ppermute(block, AXES, [(d, d ^ mask(d)) for d in range(devices)])  30.4 us
    pallas_call x3, Pallas kernels, body(): pl.pallas_call(functools.partial(next_kernel, size, last), out_shape=[who...  20 us
    pallas_call x1, Pallas kernels, body(): pl.pallas_call(functools.partial(first_kernel, size, (nrow, ncol, span)),...  8.71 us
  transfers between devices with their start and end apart: 28, of which 26 were waited for; matrix products, arithmetic and copies ran while one was open for 1% of the time, Pallas kernels for 0%

profile of v3, /device:TPU:0, one launch (start us, length us, event | category | flops | bytes accessed | tf_op | source)
XLA Modules:
  0.0 105.7 jit_solution(17508068375444219376)
XLA Ops:
  3.2 4.7 %collective-permute-start.2 = (f32[56,128]{1,0:T(8,128)}, f32[56,128]{1,0:T(8,128)S(1)}, u32[]{:S(2)}, u32[]{:S(2)}) collective-permute-start(f32[56,128]{1,0:T(8,128)} %get-tuple-element.13), channel_id=1, source_target_pairs={{0,24},{1,25},{2,26},{3,27},{4,28},{5,29},{6,30},{7,31},{8,16},{9,... | collective-permute-start | bytes 86024 | tf_op jit(solution)/shard_map/ppermute | solution.py:39
  8.6 4.8 %collective-permute-done.1 = f32[112,128]{1,0:T(8,128)S(1)} collective-permute-done((f32[112,128]{1,0:T(8,128)S(1)}, f32[112,128]{1,0:T(8,128)S(1)}, u32[]{:S(2)}, u32[]{:S(2)}) %collective-permute-start.1) | collective-permute-done | bytes 57376 | tf_op jit(solution)/shard_map/ppermute | solution.py:39
  13.4 1.6 %collective-permute-start.3 = (f32[224,128]{1,0:T(8,128)S(1)}, f32[224,128]{1,0:T(8,128)S(1)}, u32[]{:S(2)}, u32[]{:S(2)}) collective-permute-start(f32[224,128]{1,0:T(8,128)S(1)} %get-tuple-element.62), channel_id=1, source_target_pairs={{0,2},{1,3},{2,0},{3,1},{4,6},{5,7},{6,4},{7,5},{8,10},{9,11},{10,... | collective-permute-start | bytes 344072 | tf_op jit(solution)/shard_map/ppermute | solution.py:39
  18.3 2.1 %collective-permute-done.4 = f32[224,128]{1,0:T(8,128)S(1)} collective-permute-done((f32[224,128]{1,0:T(8,128)S(1)}, f32[224,128]{1,0:T(8,128)S(1)}, u32[]{:S(2)}, u32[]{:S(2)}) %collective-permute-start.4) | collective-permute-done | bytes 114720 | tf_op jit(solution)/shard_map/ppermute | solution.py:39
  20.5 1.8 %collective-permute-done.5 = f32[224,128]{1,0:T(8,128)S(1)} collective-permute-done((f32[224,128]{1,0:T(8,128)S(1)}, f32[224,128]{1,0:T(8,128)S(1)}, u32[]{:S(2)}, u32[]{:S(2)}) %collective-permute-start.5) | collective-permute-done | bytes 114720 | tf_op jit(solution)/shard_map/ppermute | solution.py:39
  22.3 1.7 %collective-permute-done.6 = f32[840,128]{1,0:T(8,128)S(1)} collective-permute-done((f32[840,128]{1,0:T(8,128)S(1)}, f32[840,128]{1,0:T(8,128)S(1)}, u32[]{:S(2)}, u32[]{:S(2)}) %collective-permute-start.6) | collective-permute-done | bytes 430112 | tf_op jit(solution)/shard_map/ppermute | solution.py:39
  24.1 8.7 %first_forces.1 = (f32[48,128]{1,0:T(8,128)S(1)}, f32[48,128]{1,0:T(8,128)S(1)}, s32[32,128]{1,0:T(8,128)S(1)}) custom-call(f32[1792,128]{1,0:T(8,128)S(1)} %constant_dynamic-update-slice_fusion.8.gathered, f32[48,128]{1,0:T(8,128)S(1)} %copy-done), custom_call_target="tpu_custom_call" | custom-call | tf_op jit(solution)/shard_map/first_forces/pallas_call | solution.py:340
  34.1 2.4 %collective-permute-start.9 = (f32[48,128]{1,0:T(8,128)S(1)}, f32[48,128]{1,0:T(8,128)S(1)}, u32[]{:S(2)}, u32[]{:S(2)}) collective-permute-start(f32[48,128]{1,0:T(8,128)S(1)} %get-tuple-element.15), channel_id=1, source_target_pairs={{0,24},{1,25},{2,26},{3,27},{4,28},{5,29},{6,30},{7,31},{8,16},{9,... | collective-permute-start | bytes 73736 | tf_op jit(solution)/shard_map/ppermute | solution.py:39
  36.6 2.2 %collective-permute-done.8 = f32[96,128]{1,0:T(8,128)S(1)} collective-permute-done((f32[96,128]{1,0:T(8,128)S(1)}, f32[96,128]{1,0:T(8,128)S(1)}, u32[]{:S(2)}, u32[]{:S(2)}) %collective-permute-start.8) | collective-permute-done | bytes 49184 | tf_op jit(solution)/shard_map/ppermute | solution.py:39
  39.8 1.9 %collective-permute-start.10 = (f32[192,128]{1,0:T(8,128)S(1)}, f32[192,128]{1,0:T(8,128)S(1)}, u32[]{:S(2)}, u32[]{:S(2)}) collective-permute-start(f32[192,128]{1,0:T(8,128)S(1)} %get-tuple-element.77), channel_id=1, source_target_pairs={{0,2},{1,3},{2,0},{3,1},{4,6},{5,7},{6,4},{7,5},{8,10},{9,11},{10,... | collective-permute-start | bytes 294920 | tf_op jit(solution)/shard_map/ppermute | solution.py:39
  44.5 2.3 %collective-permute-done.11 = f32[192,128]{1,0:T(8,128)S(1)} collective-permute-done((f32[192,128]{1,0:T(8,128)S(1)}, f32[192,128]{1,0:T(8,128)S(1)}, u32[]{:S(2)}, u32[]{:S(2)}) %collective-permute-start.11) | collective-permute-done | bytes 98336 | tf_op jit(solution)/shard_map/ppermute | solution.py:39
  48.1 1.7 %collective-permute-done.13 = f32[720,128]{1,0:T(8,128)S(1)} collective-permute-done((f32[720,128]{1,0:T(8,128)S(1)}, f32[720,128]{1,0:T(8,128)S(1)}, u32[]{:S(2)}, u32[]{:S(2)}) %collective-permute-start.13) | collective-permute-done | bytes 368672 | tf_op jit(solution)/shard_map/ppermute | solution.py:39
  49.8 6.5 %next_forces.2 = (f32[48,128]{1,0:T(8,128)S(1)}, f32[48,128]{1,0:T(8,128)S(1)}, f32[48,128]{1,0:T(8,128)S(1)}) custom-call(f32[1536,128]{1,0:T(8,128)S(1)} %constant_dynamic-update-slice_fusion.24.gathered, f32[48,128]{1,0:T(8,128)S(1)} %copy-done, f32[48,128]{1,0:T(8,128)S(1)} %get-tuple-element.16.force, s32[32,128]{1,0:T(8,128)S(1)} %get-tuple-element.17.units), custom_call_target="tpu_custom_call" | custom-call | tf_op jit(solution)/shard_map/next_forces/pallas_call | solution.py:356
  58.0 3.6 %collective-permute-start.16 = (f32[48,128]{1,0:T(8,128)S(1)}, f32[48,128]{1,0:T(8,128)S(1)}, u32[]{:S(2)}, u32[]{:S(2)}) collective-permute-start(f32[48,128]{1,0:T(8,128)S(1)} %get-tuple-element.18), channel_id=1, source_target_pairs={{0,24},{1,25},{2,26},{3,27},{4,28},{5,29},{6,30},{7,31},{8,16},{9,... | collective-permute-start | bytes 73736 | tf_op jit(solution)/shard_map/ppermute | solution.py:39
  62.2 2.0 %collective-permute-done.16 = f32[48,128]{1,0:T(8,128)S(1)} collective-permute-done((f32[48,128]{1,0:T(8,128)S(1)}, f32[48,128]{1,0:T(8,128)S(1)}, u32[]{:S(2)}, u32[]{:S(2)}) %collective-permute-start.16) | collective-permute-done | bytes 24608 | tf_op jit(solution)/shard_map/ppermute | solution.py:39
  64.2 2.0 %collective-permute-start.17 = (f32[192,128]{1,0:T(8,128)S(1)}, f32[192,128]{1,0:T(8,128)S(1)}, u32[]{:S(2)}, u32[]{:S(2)}) collective-permute-start(f32[192,128]{1,0:T(8,128)S(1)} %get-tuple-element.72), channel_id=1, source_target_pairs={{0,2},{1,3},{2,0},{3,1},{4,6},{5,7},{6,4},{7,5},{8,10},{9,11},{10,... | collective-permute-start | bytes 294920 | tf_op jit(solution)/shard_map/ppermute | solution.py:39
  68.8 2.7 %collective-permute-done.18 = f32[192,128]{1,0:T(8,128)S(1)} collective-permute-done((f32[192,128]{1,0:T(8,128)S(1)}, f32[192,128]{1,0:T(8,128)S(1)}, u32[]{:S(2)}, u32[]{:S(2)}) %collective-permute-start.18) | collective-permute-done | bytes 98336 | tf_op jit(solution)/shard_map/ppermute | solution.py:39
  72.4 1.7 %collective-permute-done.20 = f32[720,128]{1,0:T(8,128)S(1)} collective-permute-done((f32[720,128]{1,0:T(8,128)S(1)}, f32[720,128]{1,0:T(8,128)S(1)}, u32[]{:S(2)}, u32[]{:S(2)}) %collective-permute-start.20) | collective-permute-done | bytes 368672 | tf_op jit(solution)/shard_map/ppermute | solution.py:39
  74.1 6.5 %next_forces.3 = (f32[48,128]{1,0:T(8,128)S(1)}, f32[48,128]{1,0:T(8,128)S(1)}, f32[48,128]{1,0:T(8,128)S(1)}) custom-call(f32[1536,128]{1,0:T(8,128)S(1)} %constant_dynamic-update-slice_fusion.40.gathered, f32[48,128]{1,0:T(8,128)S(1)} %get-tuple-element.19.velocity, f32[48,128]{1,0:T(8,128)S(1)} %get-tuple-element.20.force, ...), custom_call_target="tpu_custom_call" | custom-call | tf_op jit(solution)/shard_map/next_forces/pallas_call | solution.py:356
  82.4 2.9 %collective-permute-start.23 = (f32[48,128]{1,0:T(8,128)S(1)}, f32[48,128]{1,0:T(8,128)S(1)}, u32[]{:S(2)}, u32[]{:S(2)}) collective-permute-start(f32[48,128]{1,0:T(8,128)S(1)} %get-tuple-element.21), channel_id=1, source_target_pairs={{0,24},{1,25},{2,26},{3,27},{4,28},{5,29},{6,30},{7,31},{8,16},{9,... | collective-permute-start | bytes 73736 | tf_op jit(solution)/shard_map/ppermute | solution.py:39
  88.1 2.5 %collective-permute-start.24 = (f32[192,128]{1,0:T(8,128)S(1)}, f32[192,128]{1,0:T(8,128)S(1)}, u32[]{:S(2)}, u32[]{:S(2)}) collective-permute-start(f32[192,128]{1,0:T(8,128)S(1)} %get-tuple-element.67), channel_id=1, source_target_pairs={{0,2},{1,3},{2,0},{3,1},{4,6},{5,7},{6,4},{7,5},{8,10},{9,11},{10,... | collective-permute-start | bytes 294920 | tf_op jit(solution)/shard_map/ppermute | solution.py:39
  93.1 2.8 %collective-permute-done.25 = f32[192,128]{1,0:T(8,128)S(1)} collective-permute-done((f32[192,128]{1,0:T(8,128)S(1)}, f32[192,128]{1,0:T(8,128)S(1)}, u32[]{:S(2)}, u32[]{:S(2)}) %collective-permute-start.25) | collective-permute-done | bytes 98336 | tf_op jit(solution)/shard_map/ppermute | solution.py:39
  96.9 1.7 %collective-permute-done.27 = f32[720,128]{1,0:T(8,128)S(1)} collective-permute-done((f32[720,128]{1,0:T(8,128)S(1)}, f32[720,128]{1,0:T(8,128)S(1)}, u32[]{:S(2)}, u32[]{:S(2)}) %collective-permute-start.27) | collective-permute-done | bytes 368672 | tf_op jit(solution)/shard_map/ppermute | solution.py:39
  98.6 7.1 %last_forces.1 = (f32[3,2048]{1,0:T(4,128)}, f32[3,2048]{1,0:T(4,128)}) custom-call(f32[1536,128]{1,0:T(8,128)S(1)} %constant_dynamic-update-slice_fusion.56.gathered, f32[48,128]{1,0:T(8,128)S(1)} %get-tuple-element.22.velocity, f32[48,128]{1,0:T(8,128)S(1)} %get-tuple-element.23.force, s32[32,128]{1,0:T(8,128)S(1)} %get-tuple-element.17.units), custom_call_target="tpu_custom_call" | custom-call | tf_op jit(solution)/shard_map/last_forces/pallas_call | solution.py:356
  (77 shorter events, 26.7 us)
Async XLA Ops:
  2.7 5.1 %collective-permute-start = (f32[56,128]{1,0:T(8,128)}, f32[56,128]{1,0:T(8,128)S(1)}, u32[]{:S(2)}, u32[]{:S(2)}) collective-permute-start(f32[56,128]{1,0:T(8,128)} %get-tuple-element.13), channel_id=1, source_target_pairs={{0,1},{1,0},{2,3},{3,2},{4,5},{5,4},{6,7},{7,6},{8,9},{9,8},{10,11... | collective-permute-start | bytes 86024 | tf_op jit(solution)/shard_map/ppermute | solution.py:39
  3.2 10.3 %collective-permute-start.2 = (f32[56,128]{1,0:T(8,128)}, f32[56,128]{1,0:T(8,128)S(1)}, u32[]{:S(2)}, u32[]{:S(2)}) collective-permute-start(f32[56,128]{1,0:T(8,128)} %get-tuple-element.13), channel_id=1, source_target_pairs={{0,24},{1,25},{2,26},{3,27},{4,28},{5,29},{6,30},{7,31},{8,16},{9,... | collective-permute-start | bytes 86024 | tf_op jit(solution)/shard_map/ppermute | solution.py:39
  8.6 4.8 %collective-permute-start.1 = (f32[112,128]{1,0:T(8,128)S(1)}, f32[112,128]{1,0:T(8,128)S(1)}, u32[]{:S(2)}, u32[]{:S(2)}) collective-permute-start(f32[112,128]{1,0:T(8,128)S(1)} %pad_maximum_fusion), channel_id=1, source_target_pairs={{0,8},{1,17},{2,10},{3,19},{4,12},{5,21},{6,14},{7,23},{8,0},{9,25... | collective-permute-start | bytes 172040 | tf_op jit(solution)/shard_map/ppermute | solution.py:39
  13.4 4.9 %collective-permute-start.3 = (f32[224,128]{1,0:T(8,128)S(1)}, f32[224,128]{1,0:T(8,128)S(1)}, u32[]{:S(2)}, u32[]{:S(2)}) collective-permute-start(f32[224,128]{1,0:T(8,128)S(1)} %get-tuple-element.62), channel_id=1, source_target_pairs={{0,2},{1,3},{2,0},{3,1},{4,6},{5,7},{6,4},{7,5},{8,10},{9,11},{10,... | collective-permute-start | bytes 344072 | tf_op jit(solution)/shard_map/ppermute | solution.py:39
  15.0 5.4 %collective-permute-start.4 = (f32[224,128]{1,0:T(8,128)S(1)}, f32[224,128]{1,0:T(8,128)S(1)}, u32[]{:S(2)}, u32[]{:S(2)}) collective-permute-start(f32[224,128]{1,0:T(8,128)S(1)} %get-tuple-element.62), channel_id=1, source_target_pairs={{0,4},{1,5},{2,6},{3,7},{4,0},{5,1},{6,2},{7,3},{8,12},{9,13},{10,... | collective-permute-start | bytes 344072 | tf_op jit(solution)/shard_map/ppermute | solution.py:39
  16.5 5.7 %collective-permute-start.5 = (f32[224,128]{1,0:T(8,128)S(1)}, f32[224,128]{1,0:T(8,128)S(1)}, u32[]{:S(2)}, u32[]{:S(2)}) collective-permute-start(f32[224,128]{1,0:T(8,128)S(1)} %get-tuple-element.62), channel_id=1, source_target_pairs={{0,6},{1,7},{2,4},{3,5},{4,2},{5,3},{6,0},{7,1},{8,14},{9,15},{10,... | collective-permute-start | bytes 344072 | tf_op jit(solution)/shard_map/ppermute | solution.py:39
  22.2 1.8 %collective-permute-start.6 = (f32[840,128]{1,0:T(8,128)S(1)}, f32[840,128]{1,0:T(8,128)S(1)}, u32[]{:S(2)}, u32[]{:S(2)}) collective-permute-start(f32[840,128]{1,0:T(8,128)S(1)} %get-tuple-element.24), channel_id=1, source_target_pairs={{0,1},{1,0},{2,3},{3,2},{4,5},{5,4},{6,7},{7,6},{8,9},{9,8},{10,11... | collective-permute-start | bytes 1290248 | tf_op jit(solution)/shard_map/ppermute | solution.py:39
  34.1 4.6 %collective-permute-start.8 = (f32[96,128]{1,0:T(8,128)S(1)}, f32[96,128]{1,0:T(8,128)S(1)}, u32[]{:S(2)}, u32[]{:S(2)}) collective-permute-start(f32[96,128]{1,0:T(8,128)S(1)} %pad_maximum_fusion.1), channel_id=1, source_target_pairs={{0,8},{1,17},{2,10},{3,19},{4,12},{5,21},{6,14},{7,23},{8,0},{9,25... | collective-permute-start | bytes 147464 | tf_op jit(solution)/shard_map/ppermute | solution.py:39
  34.1 5.7 %collective-permute-start.9 = (f32[48,128]{1,0:T(8,128)S(1)}, f32[48,128]{1,0:T(8,128)S(1)}, u32[]{:S(2)}, u32[]{:S(2)}) collective-permute-start(f32[48,128]{1,0:T(8,128)S(1)} %get-tuple-element.15), channel_id=1, source_target_pairs={{0,24},{1,25},{2,26},{3,27},{4,28},{5,29},{6,30},{7,31},{8,16},{9,... | collective-permute-start | bytes 73736 | tf_op jit(solution)/shard_map/ppermute | solution.py:39
  39.8 4.6 %collective-permute-start.10 = (f32[192,128]{1,0:T(8,128)S(1)}, f32[192,128]{1,0:T(8,128)S(1)}, u32[]{:S(2)}, u32[]{:S(2)}) collective-permute-start(f32[192,128]{1,0:T(8,128)S(1)} %get-tuple-element.77), channel_id=1, source_target_pairs={{0,2},{1,3},{2,0},{3,1},{4,6},{5,7},{6,4},{7,5},{8,10},{9,11},{10,... | collective-permute-start | bytes 294920 | tf_op jit(solution)/shard_map/ppermute | solution.py:39
  41.7 5.0 %collective-permute-start.11 = (f32[192,128]{1,0:T(8,128)S(1)}, f32[192,128]{1,0:T(8,128)S(1)}, u32[]{:S(2)}, u32[]{:S(2)}) collective-permute-start(f32[192,128]{1,0:T(8,128)S(1)} %get-tuple-element.77), channel_id=1, source_target_pairs={{0,4},{1,5},{2,6},{3,7},{4,0},{5,1},{6,2},{7,3},{8,12},{9,13},{10,... | collective-permute-start | bytes 294920 | tf_op jit(solution)/shard_map/ppermute | solution.py:39
  42.5 5.6 %collective-permute-start.12 = (f32[192,128]{1,0:T(8,128)S(1)}, f32[192,128]{1,0:T(8,128)S(1)}, u32[]{:S(2)}, u32[]{:S(2)}) collective-permute-start(f32[192,128]{1,0:T(8,128)S(1)} %get-tuple-element.77), channel_id=1, source_target_pairs={{0,6},{1,7},{2,4},{3,5},{4,2},{5,3},{6,0},{7,1},{8,14},{9,15},{10,... | collective-permute-start | bytes 294920 | tf_op jit(solution)/shard_map/ppermute | solution.py:39
  57.6 4.6 %collective-permute-start.15 = (f32[96,128]{1,0:T(8,128)S(1)}, f32[96,128]{1,0:T(8,128)S(1)}, u32[]{:S(2)}, u32[]{:S(2)}) collective-permute-start(f32[96,128]{1,0:T(8,128)S(1)} %pad_maximum_fusion.2), channel_id=1, source_target_pairs={{0,8},{1,17},{2,10},{3,19},{4,12},{5,21},{6,14},{7,23},{8,0},{9,25... | collective-permute-start | bytes 147464 | tf_op jit(solution)/shard_map/ppermute | solution.py:39
  58.0 6.2 %collective-permute-start.16 = (f32[48,128]{1,0:T(8,128)S(1)}, f32[48,128]{1,0:T(8,128)S(1)}, u32[]{:S(2)}, u32[]{:S(2)}) collective-permute-start(f32[48,128]{1,0:T(8,128)S(1)} %get-tuple-element.18), channel_id=1, source_target_pairs={{0,24},{1,25},{2,26},{3,27},{4,28},{5,29},{6,30},{7,31},{8,16},{9,... | collective-permute-start | bytes 73736 | tf_op jit(solution)/shard_map/ppermute | solution.py:39
  64.2 4.6 %collective-permute-start.17 = (f32[192,128]{1,0:T(8,128)S(1)}, f32[192,128]{1,0:T(8,128)S(1)}, u32[]{:S(2)}, u32[]{:S(2)}) collective-permute-start(f32[192,128]{1,0:T(8,128)S(1)} %get-tuple-element.72), channel_id=1, source_target_pairs={{0,2},{1,3},{2,0},{3,1},{4,6},{5,7},{6,4},{7,5},{8,10},{9,11},{10,... | collective-permute-start | bytes 294920 | tf_op jit(solution)/shard_map/ppermute | solution.py:39
  66.1 5.4 %collective-permute-start.18 = (f32[192,128]{1,0:T(8,128)S(1)}, f32[192,128]{1,0:T(8,128)S(1)}, u32[]{:S(2)}, u32[]{:S(2)}) collective-permute-start(f32[192,128]{1,0:T(8,128)S(1)} %get-tuple-element.72), channel_id=1, source_target_pairs={{0,4},{1,5},{2,6},{3,7},{4,0},{5,1},{6,2},{7,3},{8,12},{9,13},{10,... | collective-permute-start | bytes 294920 | tf_op jit(solution)/shard_map/ppermute | solution.py:39
  66.6 5.7 %collective-permute-start.19 = (f32[192,128]{1,0:T(8,128)S(1)}, f32[192,128]{1,0:T(8,128)S(1)}, u32[]{:S(2)}, u32[]{:S(2)}) collective-permute-start(f32[192,128]{1,0:T(8,128)S(1)} %get-tuple-element.72), channel_id=1, source_target_pairs={{0,6},{1,7},{2,4},{3,5},{4,2},{5,3},{6,0},{7,1},{8,14},{9,15},{10,... | collective-permute-start | bytes 294920 | tf_op jit(solution)/shard_map/ppermute | solution.py:39
  72.4 1.8 %collective-permute-start.20 = (f32[720,128]{1,0:T(8,128)S(1)}, f32[720,128]{1,0:T(8,128)S(1)}, u32[]{:S(2)}, u32[]{:S(2)}) collective-permute-start(f32[720,128]{1,0:T(8,128)S(1)} %get-tuple-element.36), channel_id=1, source_target_pairs={{0,1},{1,0},{2,3},{3,2},{4,5},{5,4},{6,7},{7,6},{8,9},{9,8},{10,11... | collective-permute-start | bytes 1105928 | tf_op jit(solution)/shard_map/ppermute | solution.py:39
  81.9 4.6 %collective-permute-start.22 = (f32[96,128]{1,0:T(8,128)S(1)}, f32[96,128]{1,0:T(8,128)S(1)}, u32[]{:S(2)}, u32[]{:S(2)}) collective-permute-start(f32[96,128]{1,0:T(8,128)S(1)} %pad_maximum_fusion.3), channel_id=1, source_target_pairs={{0,8},{1,17},{2,10},{3,19},{4,12},{5,21},{6,14},{7,23},{8,0},{9,25... | collective-permute-start | bytes 147464 | tf_op jit(solution)/shard_map/ppermute | solution.py:39
  82.4 5.7 %collective-permute-start.23 = (f32[48,128]{1,0:T(8,128)S(1)}, f32[48,128]{1,0:T(8,128)S(1)}, u32[]{:S(2)}, u32[]{:S(2)}) collective-permute-start(f32[48,128]{1,0:T(8,128)S(1)} %get-tuple-element.21), channel_id=1, source_target_pairs={{0,24},{1,25},{2,26},{3,27},{4,28},{5,29},{6,30},{7,31},{8,16},{9,... | collective-permute-start | bytes 73736 | tf_op jit(solution)/shard_map/ppermute | solution.py:39
  88.1 5.1 %collective-permute-start.24 = (f32[192,128]{1,0:T(8,128)S(1)}, f32[192,128]{1,0:T(8,128)S(1)}, u32[]{:S(2)}, u32[]{:S(2)}) collective-permute-start(f32[192,128]{1,0:T(8,128)S(1)} %get-tuple-element.67), channel_id=1, source_target_pairs={{0,2},{1,3},{2,0},{3,1},{4,6},{5,7},{6,4},{7,5},{8,10},{9,11},{10,... | collective-permute-start | bytes 294920 | tf_op jit(solution)/shard_map/ppermute | solution.py:39
  90.5 5.4 %collective-permute-start.25 = (f32[192,128]{1,0:T(8,128)S(1)}, f32[192,128]{1,0:T(8,128)S(1)}, u32[]{:S(2)}, u32[]{:S(2)}) collective-permute-start(f32[192,128]{1,0:T(8,128)S(1)} %get-tuple-element.67), channel_id=1, source_target_pairs={{0,4},{1,5},{2,6},{3,7},{4,0},{5,1},{6,2},{7,3},{8,12},{9,13},{10,... | collective-permute-start | bytes 294920 | tf_op jit(solution)/shard_map/ppermute | solution.py:39
  91.0 5.7 %collective-permute-start.26 = (f32[192,128]{1,0:T(8,128)S(1)}, f32[192,128]{1,0:T(8,128)S(1)}, u32[]{:S(2)}, u32[]{:S(2)}) collective-permute-start(f32[192,128]{1,0:T(8,128)S(1)} %get-tuple-element.67), channel_id=1, source_target_pairs={{0,6},{1,7},{2,4},{3,5},{4,2},{5,3},{6,0},{7,1},{8,14},{9,15},{10,... | collective-permute-start | bytes 294920 | tf_op jit(solution)/shard_map/ppermute | solution.py:39
  96.8 1.8 %collective-permute-start.27 = (f32[720,128]{1,0:T(8,128)S(1)}, f32[720,128]{1,0:T(8,128)S(1)}, u32[]{:S(2)}, u32[]{:S(2)}) collective-permute-start(f32[720,128]{1,0:T(8,128)S(1)} %get-tuple-element.30), channel_id=1, source_target_pairs={{0,1},{1,0},{2,3},{3,2},{4,5},{5,4},{6,7},{7,6},{8,9},{9,8},{10,11... | collective-permute-start | bytes 1105928 | tf_op jit(solution)/shard_map/ppermute | solution.py:39
  (6 other events, 13.2 us)

commit v4 on v3

--- a/solution.py
+++ b/solution.py
@@ -39,10 +39,13 @@
     return lax.ppermute(block, AXES, [(d, d ^ mask(d)) for d in range(devices)])
 
 
-def gather(block, devices):
-    stages = stage_masks(devices)[:-1]
+def send(block, devices, mask):
+    return lax.ppermute(block, AXES, [(d, d ^ mask(d)) for d in range(devices)])
+
+
+def gather_near(block, devices):
     near, far, missing = block, None, [block]
-    for number, (low, count) in enumerate(stages):
+    for number, (low, count) in enumerate(stage_masks(devices)[:-2]):
         if number == 0 and count == 4:
             far = send(block, devices, lambda d: 1)
             both = jnp.concatenate([near, far], 0)
@@ -55,7 +58,20 @@
             missing = missing + parts
             near = jnp.concatenate([near] + parts, 0)
     rest = send(jnp.concatenate(missing, 0), devices, lambda d: 1)
-    return jnp.concatenate([near, rest] if far is None else [near, far, rest], 0)
+    return near, jnp.concatenate([near, rest] if far is None else [near, far, rest], 0)
+
+
+def gather_last(near, devices, beside=None):
+    low, count = stage_masks(devices)[-2]
+    parts = [send(near, devices, lambda d: step << low) for step in range(1, count)]
+    if beside is not None:
+        parts, beside = lax.optimization_barrier((parts, beside))
+    parts = jnp.concatenate(parts, 0)
+    return parts, send(parts, devices, lambda d: 1), beside
+
+
+def near_size(devices):
+    return devices // 2 // stage_masks(devices)[-2][1]
 
 
 def slot_of(owner, me, devices):
@@ -65,14 +81,16 @@
     size = 1
     for number, (low, count) in enumerate(stage_masks(devices)[:-1]):
         step = (relative >> low) & (count - 1)
-        if number == 0 and count == 4:
+        if number == 0 and count == 4 and len(stage_masks(devices)) > 2:
             fetcher = jnp.where((step == 1) | (step == 2), step - 1, holder)
             place = jnp.where(step == 0, place, jnp.where(step == 3, 3, 1 + (holder ^ fetcher)))
             holder = fetcher
         else:
             place = place + step * size
         size *= count
-    return place + (holder ^ (me & 1)) * size
+    near = near_size(devices)
+    other = holder ^ (me & 1)
+    return jnp.where(place < near, place + other * near, place + near + other * (size - near))
 
 
 def prepare_kernel(blocks, span, positions, velocities, pairs, total, out, velocity):
@@ -100,20 +118,26 @@
     return high, mid, rest - mid
 
 
-def evaluate(size, gathered, rows, units, points, lefts, sums, turned_kept, right_kept, weights_kept, partner_kept):
+def load_points(size, pieces, rows, points):
+    devices, blocks = size
+    stride = 4 * blocks
+    for ref, slots in pieces:
+        for n, slot in enumerate(slots):
+            norm = None
+            for c in range(3):
+                y = 0.5 * ref[pl.ds(n * rows + c * blocks, blocks), :]
+                points[pl.ds(slot * stride + c * blocks, blocks), :] = y
+                norm = y * y if norm is None else norm + y * y
+            points[pl.ds(slot * stride + 3 * blocks, blocks), :] = norm
+    dummy = devices * stride
+    points[pl.ds(dummy, 3 * blocks), :] = jnp.zeros((3 * blocks, LANES), jnp.float32)
+    points[pl.ds(dummy + 3 * blocks, blocks), :] = jnp.full((blocks, LANES), FAR, jnp.float32)
+
+
+def add_pairs(size, part, units, ready, points, lefts, sums, turned_kept, right_kept, weights_kept, partner_kept):
     devices, blocks = size
     stride = 4 * blocks
     dummy = devices * stride
-    for slot in range(devices):
-        norm = None
-        for c in range(3):
-            y = 0.5 * gathered[pl.ds(slot * rows + c * blocks, blocks), :]
-            points[pl.ds(slot * stride + c * blocks, blocks), :] = y
-            norm = y * y if norm is None else norm + y * y
-        points[pl.ds(slot * stride + 3 * blocks, blocks), :] = norm
-    points[pl.ds(dummy, 3 * blocks), :] = jnp.zeros((3 * blocks, LANES), jnp.float32)
-    points[pl.ds(dummy + 3 * blocks, blocks), :] = jnp.full((blocks, LANES), FAR, jnp.float32)
-
     place = lax.broadcasted_iota(jnp.int32, (8, LANES), 0)
     for b in range(blocks):
         tile = points[pl.ds(b, 8, stride=blocks), :]
@@ -124,6 +148,9 @@
         high, mid, low = split3(tile)
         lefts[b] = jnp.concatenate([high, high, high, mid, mid, low], 0).astype(jnp.bfloat16)
     sums[...] = jnp.zeros_like(sums)
+    ready()
+    steps = [units[units.shape[0] - 1, LANES - 1 - n] for n in range(2)]
+    begin, end = {0: (0, steps[0]), 1: (steps[0], steps[1]), None: (0, steps[1])}[part]
 
     def right_tile(word):
         tile = points[pl.ds(dummy - (word & BASE_MASK), 8, stride=blocks), :]
@@ -153,7 +180,7 @@
         sums[at, :] = sums[at, :] + (part[:, :LANES] + part[:, LANES:])
 
     for k in range(LEAD):
-        turned_kept[k], right_kept[k] = fetch(k)
+        turned_kept[k], right_kept[k] = fetch(begin * UNROLL + k)
     weights_kept[...] = jnp.zeros_like(weights_kept)
     partner_kept[...] = jnp.zeros_like(partner_kept)
 
@@ -172,22 +199,21 @@
             partner_kept[k], weights_kept[k] = weighed[UNROLL + k]
         return carry
 
-    count = units[units.shape[0] - 1, LANES - 1]
-    steps = (count + UNROLL - 1) >> (UNROLL.bit_length() - 1)
-    lax.fori_loop(0, steps, group, 0)
+    lax.fori_loop(begin, end, group, 0)
     for k in range(LAG):
-        add(jnp.maximum(steps * UNROLL - LAG + k, 0), partner_kept[k], weights_kept[k])
-
-    total = sums[pl.ds(4, blocks, stride=32), :]
+        add(jnp.maximum(end * UNROLL - LAG + k, 0), partner_kept[k], weights_kept[k])
+
+
+def forces_of(blocks, points, all_sums):
+    def entry(n):
+        at = pl.ds(n, blocks, stride=32)
+        return sum(sums[at, :] for sums in all_sums)
+
+    total = entry(4)
     forces = []
     for c in range(3):
         y = points[pl.ds(c * blocks, blocks), :]
-        mix = (
-            sums[pl.ds(c, blocks, stride=32), :]
-            + sums[pl.ds(8 + c, blocks, stride=32), :]
-            + sums[pl.ds(16 + c, blocks, stride=32), :]
-        )
-        forces.append((2.0 * STIFFNESS) * (y * total - mix))
+        forces.append((2.0 * STIFFNESS) * (y * total - (entry(c) + entry(8 + c) + entry(16 + c))))
     return forces
 
 
@@ -214,27 +240,42 @@
     valid = valid & (owner == me) & (by_row | distinct)
     other = jnp.where(by_row, right_owner, left_owner)
     place = jnp.where(by_row, right_place, left_place)
-    back = (devices - slot_of(other, me, devices)) * (4 * blocks) - place
-    mine = jnp.where(valid, mine, -1)
+    slot = slot_of(other, me, devices)
+    back = (devices - slot) * (4 * blocks) - place
+    group = jnp.where(valid, jnp.where(slot < 2 * near_size(devices), mine, mine + blocks), -1)
 
     ones = jnp.bfloat16
-    chosen = jnp.concatenate([(mine == b).astype(jnp.float32) for b in range(blocks)], 0)
+    groups = 2 * blocks
+    chosen = jnp.concatenate([(group == g).astype(jnp.float32) for g in range(groups)], 0)
     picked = chosen.astype(ones)
     one, two = lax.broadcasted_iota(jnp.int32, (LANES, LANES), 0), lax.broadcasted_iota(jnp.int32, (LANES, LANES), 1)
     before = matmul(picked, (one < two).astype(jnp.float32).astype(ones))
     totals = matmul(picked, jnp.ones((LANES, LANES), ones))
-    many = blocks * height
-    one, two = lax.broadcasted_iota(jnp.int32, (many, many), 0), lax.broadcasted_iota(jnp.int32, (many, many), 1)
-    earlier = ((one // height == two // height) & (two < one)).astype(jnp.float32).astype(ones)
-    above = matmul(earlier, totals.astype(ones))
-    offset = jnp.zeros((1, LANES), jnp.float32)
+    lane = lax.broadcasted_iota(jnp.int32, code.shape, 1)
+    table = jnp.zeros(code.shape, jnp.float32)
+    for g in range(groups):
+        table = jnp.where(lane == g, totals[g * height : (g + 1) * height], table)
+    row_one, row_two = [lax.broadcasted_iota(jnp.int32, (height, height), n) for n in range(2)]
+    above = matmul((row_two < row_one).astype(jnp.float32).astype(ones), table.astype(ones))
+    filled = jnp.broadcast_to(above[height - 1 :] + table[height - 1 :], (8, LANES)).astype(jnp.int32)
+    filled = filled + (filled & 1)
+    pieces = [(filled & 63).astype(jnp.float32).astype(ones), (filled >> 6).astype(jnp.float32).astype(ones)]
+
+    def total_over(mask):
+        mask = mask.astype(jnp.float32).astype(ones)
+        return matmul(pieces[0], mask) + 64.0 * matmul(pieces[1], mask)
+
+    in_near = one < blocks
+    step = 2 * UNROLL
+    near_steps = (total_over(in_near).astype(jnp.int32) + step - 1) >> (step.bit_length() - 1)
+    far_steps = (total_over(~in_near).astype(jnp.int32) + step - 1) >> (step.bit_length() - 1)
+    offset = total_over((one < two) & (in_near == (two < blocks)))
+    offset = offset + jnp.where(two[:8] < blocks, 0, near_steps * step).astype(jnp.float32)
+    start = above + offset[:1]
     position = jnp.zeros(code.shape, jnp.float32)
-    for b in range(blocks):
-        part = slice(b * height, (b + 1) * height)
-        position = position + chosen[part] * (before[part] + above[part] + offset)
-        last = (b + 1) * height - 1
-        filled = above[last : last + 1] + totals[last : last + 1]
-        offset = offset + filled + (filled.astype(jnp.int32) & 1).astype(jnp.float32)
+    for g in range(groups):
+        part = slice(g * height, (g + 1) * height)
+        position = position + chosen[part] * (before[part] + start[:, g : g + 1])
     position = position.astype(jnp.int32)
     high = jnp.where(valid, position >> 7, -1)
     low = position & (LANES - 1)
@@ -253,11 +294,18 @@
         )
     words = found.astype(jnp.int32)
     words = words[:rows] + words[rows : 2 * rows] * 64 + words[2 * rows :] * (BASE_MASK + 1)
-    end = (place == rows - 1) & (lax.broadcasted_iota(jnp.int32, (rows, LANES), 1) == LANES - 1)
-    out[...] = jnp.where(end, (offset * 0.5).astype(jnp.int32), words)
-
-
-def first_kernel(size, shape, gathered, velocity, x_next, force_out, units, codes, words, sem, *scratch):
+    lane = lax.broadcasted_iota(jnp.int32, (rows, LANES), 1)
+    words = jnp.where((place == rows - 1) & (lane == LANES - 1), near_steps[:1], words)
+    out[...] = jnp.where((place == rows - 1) & (lane == LANES - 2), (near_steps + far_steps)[:1], words)
+
+
+def slot_ranges(devices):
+    near = 2 * near_size(devices)
+    middle = near + (devices - near) // 2
+    return range(near), range(near, middle), range(middle, devices)
+
+
+def first_kernel(size, shape, near, middle, far, velocity, x_next, force_out, words, codes, units, sem, *scratch):
     devices, blocks = size
     nrow, ncol, span = shape
     rows = 3 * blocks + LIST_ROWS
@@ -265,31 +313,51 @@
     me = row * ncol + col
     holders = [row * ncol + c for c in range(ncol)] + [r * ncol + col for r in range(nrow)]
     codes[...] = jnp.full_like(codes, -1)
+    pieces = list(zip((near, middle, far), slot_ranges(devices)))
     for n, holder in enumerate(holders):
         slot = slot_of(holder, me, devices)
-        tile = gathered[pl.ds(pl.multiple_of(slot * rows + 3 * blocks, 8), LIST_ROWS), :]
-        codes[pl.ds(n * span, span), :] = tile[:span].astype(jnp.int32)
+        for ref, slots in pieces:
+
+            @pl.when((slot >= slots[0]) & (slot <= slots[-1]))
+            def _(ref=ref, slots=slots):
+                at = pl.multiple_of((slot - slots[0]) * rows + 3 * blocks, 8)
+                tile = ref[pl.ds(at, LIST_ROWS), :]
+                codes[pl.ds(n * span, span), :] = tile[:span].astype(jnp.int32)
+
     build_units(size, shape, codes, words)
     copy = pltpu.make_async_copy(words, units, sem)
     copy.start()
-    copy.wait()
-    forces = evaluate(size, gathered, rows, units, *scratch)
+    load_points(size, pieces, rows, scratch[0])
+    add_pairs(size, None, units, copy.wait, *scratch)
+    forces = forces_of(blocks, scratch[0], [scratch[2]])
     for c in range(3):
         at = pl.ds(c * blocks, blocks)
         force_out[at, :] = forces[c]
-        x_next[at, :] = gathered[at, :] + TIME_STEP * velocity[at, :] + (0.5 * TIME_STEP * TIME_STEP) * forces[c]
-
-
-def next_kernel(size, last, gathered, velocity, force, units, x_next, v_next, *rest):
-    devices, blocks = size
-    if last:
-        scratch = rest
-    else:
-        force_out, *scratch = rest
-    forces = evaluate(size, gathered, 3 * blocks, units, *scratch)
+        x_next[at, :] = near[at, :] + TIME_STEP * velocity[at, :] + (0.5 * TIME_STEP * TIME_STEP) * forces[c]
+
+
+def near_kernel(size, near, words, sums_out, units, sem, points, lefts, *kept):
+    devices, blocks = size
+    copy = pltpu.make_async_copy(words, units, sem)
+    copy.start()
+    load_points(size, [(near, slot_ranges(devices)[0])], 3 * blocks, points)
+    add_pairs(size, 0, units, copy.wait, points, lefts, sums_out, *kept)
+
+
+def next_kernel(size, last, near, middle, far, near_sums, velocity, force, words, x_next, v_next, *rest):
+    devices, blocks = size
+    if not last:
+        force_out, *rest = rest
+    units, sem, points, lefts, sums, *kept = rest
+    copy = pltpu.make_async_copy(words, units, sem)
+    copy.start()
+    _, *ranges = slot_ranges(devices)
+    load_points(size, [(near, range(1))] + list(zip((middle, far), ranges)), 3 * blocks, points)
+    add_pairs(size, 1, units, copy.wait, points, lefts, sums, *kept)
+    forces = forces_of(blocks, points, [near_sums, sums])
     for c in range(3):
         at = pl.ds(c * blocks, blocks)
-        x = gathered[at, :]
+        x = near[at, :]
         v = velocity[at, :] + (0.5 * TIME_STEP) * (force[at, :] + forces[c])
         if last:
             for b in range(blocks):
@@ -310,7 +378,7 @@
     slots = pairs.shape[0]
     size = (devices, blocks)
     span = slots // LANES
-    entries = (nrow + ncol) * slots + blocks + 2 * (UNROLL + LEAD)
+    entries = (nrow + ncol) * slots + 2 * blocks + 2 * (2 * UNROLL + LEAD)
     unit_rows = 8 * (entries // (8 * LANES) + 1)
     code_rows = 8 * (-(-(nrow + ncol) * span // 8))
     flat = jax.ShapeDtypeStruct((3 * blocks, LANES), jnp.float32)
@@ -318,16 +386,21 @@
     unit_list = jax.ShapeDtypeStruct((unit_rows, LANES), jnp.int32)
     vmem = pl.BlockSpec(memory_space=pltpu.VMEM)
     smem = pl.BlockSpec(memory_space=pltpu.SMEM)
-    scratch = [
-        pltpu.VMEM(((devices + 3) * 4 * blocks, LANES), jnp.float32),
-        pltpu.VMEM((blocks, 48, LANES), jnp.bfloat16),
-        pltpu.VMEM((blocks * 32, LANES), jnp.float32),
+    points = pltpu.VMEM(((devices + 3) * 4 * blocks, LANES), jnp.float32)
+    lefts = pltpu.VMEM((blocks, 48, LANES), jnp.bfloat16)
+    sums = pltpu.VMEM((blocks * 32, LANES), jnp.float32)
+    kept = [
         pltpu.VMEM((LEAD, 2 * LANES, 48), jnp.bfloat16),
         pltpu.VMEM((LEAD, 32, 2 * LANES), jnp.bfloat16),
         pltpu.VMEM((LAG, 2 * LANES, 2 * LANES), jnp.bfloat16),
         pltpu.VMEM((LAG, 32, 2 * LANES), jnp.bfloat16),
     ]
+    listed = [pltpu.SMEM((unit_rows, LANES), jnp.int32), pltpu.SemaphoreType.DMA]
     params = pltpu.CompilerParams(vmem_limit_bytes=48 * 1024 * 1024)
+
+    def cost(share):
+        flops = int(share * 4e9)
+        return pl.CostEstimate(flops=flops, bytes_accessed=1 << 20, transcendentals=0)
 
     packed, velocity = pl.pallas_call(
         functools.partial(prepare_kernel, blocks, nrow * blocks),
@@ -336,32 +409,40 @@
         out_specs=[vmem, vmem],
         name="prepare",
     )(positions, velocities, pairs.T, pair_counts)
-    gathered = gather(packed, devices)
-    current, force, units = pl.pallas_call(
+    near, both = gather_near(packed, devices)
+    current, force, words = pl.pallas_call(
         functools.partial(first_kernel, size, (nrow, ncol, span)),
         out_shape=[flat, flat, unit_list],
-        in_specs=[vmem, vmem],
-        out_specs=[vmem, vmem, smem],
-        scratch_shapes=[
-            pltpu.VMEM((code_rows, LANES), jnp.int32),
-            pltpu.VMEM((unit_rows, LANES), jnp.int32),
-            pltpu.SemaphoreType.DMA,
-        ]
-        + scratch,
+        in_specs=[vmem] * 4,
+        out_specs=[vmem] * 3,
+        scratch_shapes=[pltpu.VMEM((code_rows, LANES), jnp.int32)] + listed + [points, lefts, sums] + kept,
         compiler_params=params,
+        cost_estimate=cost(1.0),
         name="first_forces",
-    )(gathered, velocity)
+    )(both, *gather_last(near, devices)[:2], velocity)
     for turn in range(STEPS):
         last = turn == STEPS - 1
+        near, both = gather_near(current, devices)
+        near_sums = pl.pallas_call(
+            functools.partial(near_kernel, size),
+            out_shape=jax.ShapeDtypeStruct((blocks * 32, LANES), jnp.float32),
+            in_specs=[vmem] * 2,
+            out_specs=vmem,
+            scratch_shapes=listed + [points, lefts] + kept,
+            compiler_params=params,
+            cost_estimate=cost(0.25),
+            name="near_forces",
+        )(both, words)
         result = pl.pallas_call(
             functools.partial(next_kernel, size, last),
             out_shape=[whole] * 2 if last else [flat] * 3,
-            in_specs=[vmem, vmem, vmem, smem],
+            in_specs=[vmem] * 7,
             out_specs=[vmem] * (2 if last else 3),
-            scratch_shapes=scratch,
+            scratch_shapes=listed + [points, lefts, sums] + kept,
             compiler_params=params,
+            cost_estimate=cost(0.75),
             name="last_forces" if last else "next_forces",
-        )(gather(current, devices), velocity, force, units)
+        )(both, *gather_last(near, devices, near_sums), velocity, force, words)
         if last:
             current, velocity = result
         else:

time: 106 us -> 104 us (0.981); the launches traced: 106 us -> 102 us
  waiting for transfers between devices: 42.4 us -> 31.7 us
  Pallas kernels: 30.2 us -> 37.7 us
    ppermute x28 -> x32, waiting for transfers between devices: 42.4 us -> 31.7 us  [send(): return lax.ppermute(block, AXES, [(d, d ^ mask(d)) for d in range(devices)])]
    pallas_call x0 -> x3, Pallas kernels: none -> 9.84 us  [body(): pl.pallas_call(functools.partial(near_kernel, size), out_shape=jax.ShapeD...]
    pallas_call x3, Pallas kernels: 20 us -> 17 us  [body(): pl.pallas_call(functools.partial(next_kernel, size, last), out_shape=[who...]
    ppermute x28 -> x32, starting transfers between devices: 30.4 us -> 29.9 us  [send(): return lax.ppermute(block, AXES, [(d, d ^ mask(d)) for d in range(devices)])]
  transfers between devices with their start and end apart: 28 -> 32, of which waited for: 26 -> 13; matrix products, arithmetic and copies ran while one was open for 1% -> 1% of each run, Pallas kernels for 0% -> 10%
where the time goes in v4:
time: 104 us; the launch traced here: 102 us
  Pallas kernels  37.7 us (36%)
  waiting for transfers between devices  31.7 us (30%)
  starting transfers between devices  29.9 us (29%)
  between operations  1.88 us (2%)
    ppermute x32, waiting for transfers between devices, send(): return lax.ppermute(block, AXES, [(d, d ^ mask(d)) for d in range(devices)])  31.7 us
    ppermute x32, starting transfers between devices, send(): return lax.ppermute(block, AXES, [(d, d ^ mask(d)) for d in range(devices)])  29.9 us
    pallas_call x3, Pallas kernels, body(): pl.pallas_call(functools.partial(next_kernel, size, last), out_shape=[who...  17 us
    pallas_call x3, Pallas kernels, body(): pl.pallas_call(functools.partial(near_kernel, size), out_shape=jax.ShapeD...  9.84 us
    pallas_call x1, Pallas kernels, body(): pl.pallas_call(functools.partial(first_kernel, size, (nrow, ncol, span)),...  9.4 us
  transfers between devices with their start and end apart: 32, of which 13 were waited for; matrix products, arithmetic and copies ran while one was open for 1% of the time, Pallas kernels for 10%

profile of v4, /device:TPU:0, one launch (start us, length us, event | category | flops | bytes accessed | tf_op | source)
XLA Modules:
  0.0 102.3 jit_solution(12633193578570895261)
XLA Ops:
  1.3 1.4 %prepare.1 = (f32[56,128]{1,0:T(8,128)}, f32[48,128]{1,0:T(8,128)}) custom-call(f32[3,2048]{1,0:T(4,128)} %positions.1, f32[3,2048]{1,0:T(4,128)} %velocities.1, s32[2,256]{1,0:T(2,128)} %bitcast.3, s32[1,1]{1,0:T(1,128)S(6)} %copy.38.total), custom_call_target="tpu_custom_call" | custom-call | tf_op jit(solution)/shard_map/prepare/pallas_call | solution.py:405
  3.2 4.7 %collective-permute-start.2 = (f32[56,128]{1,0:T(8,128)}, f32[56,128]{1,0:T(8,128)S(1)}, u32[]{:S(2)}, u32[]{:S(2)}) collective-permute-start(f32[56,128]{1,0:T(8,128)} %get-tuple-element.25), channel_id=1, source_target_pairs={{0,24},{1,25},{2,26},{3,27},{4,28},{5,29},{6,30},{7,31},{8,16},{9,... | collective-permute-start | bytes 86024 | tf_op jit(solution)/shard_map/ppermute | solution.py:43
  8.6 4.8 %collective-permute-done.1 = f32[112,128]{1,0:T(8,128)S(1)} collective-permute-done((f32[112,128]{1,0:T(8,128)S(1)}, f32[112,128]{1,0:T(8,128)S(1)}, u32[]{:S(2)}, u32[]{:S(2)}) %collective-permute-start.1) | collective-permute-done | bytes 57376 | tf_op jit(solution)/shard_map/ppermute | solution.py:43
  13.4 1.6 %collective-permute-start.4 = (f32[224,128]{1,0:T(8,128)S(1)}, f32[224,128]{1,0:T(8,128)S(1)}, u32[]{:S(2)}, u32[]{:S(2)}) collective-permute-start(f32[224,128]{1,0:T(8,128)S(1)} %get-tuple-element.56), channel_id=1, source_target_pairs={{0,2},{1,3},{2,0},{3,1},{4,6},{5,7},{6,4},{7,5},{8,10},{9,11},{10,... | collective-permute-start | bytes 344072 | tf_op jit(solution)/shard_map/ppermute | solution.py:43
  15.0 1.4 %collective-permute-start.6 = (f32[224,128]{1,0:T(8,128)S(1)}, f32[224,128]{1,0:T(8,128)S(1)}, u32[]{:S(2)}, u32[]{:S(2)}) collective-permute-start(f32[224,128]{1,0:T(8,128)S(1)} %get-tuple-element.56), channel_id=1, source_target_pairs={{0,6},{1,7},{2,4},{3,5},{4,2},{5,3},{6,0},{7,1},{8,14},{9,15},{10,... | collective-permute-start | bytes 344072 | tf_op jit(solution)/shard_map/ppermute | solution.py:43
  17.0 2.5 %collective-permute-done.4 = f32[224,128]{1,0:T(8,128)S(1)} collective-permute-done((f32[224,128]{1,0:T(8,128)S(1)}, f32[224,128]{1,0:T(8,128)S(1)}, u32[]{:S(2)}, u32[]{:S(2)}) %collective-permute-start.4) | collective-permute-done | bytes 114720 | tf_op jit(solution)/shard_map/ppermute | solution.py:43
  19.5 2.1 %collective-permute-done.5 = f32[224,128]{1,0:T(8,128)S(1)} collective-permute-done((f32[224,128]{1,0:T(8,128)S(1)}, f32[224,128]{1,0:T(8,128)S(1)}, u32[]{:S(2)}, u32[]{:S(2)}) %collective-permute-start.5) | collective-permute-done | bytes 114720 | tf_op jit(solution)/shard_map/ppermute | solution.py:43
  23.6 9.4 %first_forces.1 = (f32[48,128]{1,0:T(8,128)S(1)}, f32[48,128]{1,0:T(8,128)S(1)}, s32[32,128]{1,0:T(8,128)S(1)}) custom-call(f32[448,128]{1,0:T(8,128)S(1)} %constant_dynamic-update-slice_fusion.near, f32[672,128]{1,0:T(8,128)S(1)} %constant_dynamic-update-slice_fusion.8.middle, f32[672,128]{1,0:T(8,128)S(1)} %collective-permute-done.7.far, f32[48,128]{1,0:T(8,128)S(1)} %copy-done), custom_call_target="tpu_custom_call" | custom-call | flops 4000000000 | bytes 1048576 | tf_op jit(solution)/shard_map/first_forces/pallas_call | solution.py:413
  33.2 3.0 %collective-permute-start.10 = (f32[48,128]{1,0:T(8,128)S(1)}, f32[48,128]{1,0:T(8,128)S(1)}, u32[]{:S(2)}, u32[]{:S(2)}) collective-permute-start(f32[48,128]{1,0:T(8,128)S(1)} %get-tuple-element.27), channel_id=1, source_target_pairs={{0,24},{1,25},{2,26},{3,27},{4,28},{5,29},{6,30},{7,31},{8,16},{9,... | collective-permute-start | bytes 73736 | tf_op jit(solution)/shard_map/ppermute | solution.py:43
  36.2 4.3 %collective-permute-done.9 = f32[96,128]{1,0:T(8,128)S(1)} collective-permute-done((f32[96,128]{1,0:T(8,128)S(1)}, f32[96,128]{1,0:T(8,128)S(1)}, u32[]{:S(2)}, u32[]{:S(2)}) %collective-permute-start.9) | collective-permute-done | bytes 49184 | tf_op jit(solution)/shard_map/ppermute | solution.py:43
  40.6 2.8 %collective-permute-start.14 = (f32[192,128]{1,0:T(8,128)S(1)}, f32[192,128]{1,0:T(8,128)S(1)}, u32[]{:S(2)}, u32[]{:S(2)}) collective-permute-start(f32[192,128]{1,0:T(8,128)S(1)} %get-tuple-element.68), channel_id=1, source_target_pairs={{0,6},{1,7},{2,4},{3,5},{4,2},{5,3},{6,0},{7,1},{8,14},{9,15},{10,... | collective-permute-start | bytes 294920 | tf_op jit(solution)/shard_map/ppermute | solution.py:43
  45.4 3.3 %near_forces.3.near_sums = f32[512,128]{1,0:T(8,128)S(1)} custom-call(f32[384,128]{1,0:T(8,128)S(1)} %constant_dynamic-update-slice_fusion.11.near, s32[32,128]{1,0:T(8,128)S(1)} %get-tuple-element.28.words), custom_call_target="tpu_custom_call" | custom-call | flops 1000000000 | bytes 1048576 | tf_op jit(solution)/shard_map/near_forces/pallas_call | solution.py:426
  49.0 1.4 %collective-permute-done.15.far = f32[576,128]{1,0:T(8,128)S(1)} collective-permute-done((f32[576,128]{1,0:T(8,128)S(1)}, f32[576,128]{1,0:T(8,128)S(1)}, u32[]{:S(2)}, u32[]{:S(2)}) %collective-permute-start.15) | collective-permute-done | bytes 294944 | tf_op jit(solution)/shard_map/ppermute | solution.py:43
  50.5 5.4 %next_forces.2 = (f32[48,128]{1,0:T(8,128)S(1)}, f32[48,128]{1,0:T(8,128)S(1)}, f32[48,128]{1,0:T(8,128)S(1)}) custom-call(f32[384,128]{1,0:T(8,128)S(1)} %constant_dynamic-update-slice_fusion.11.near, f32[576,128]{1,0:T(8,128)S(1)} %constant_dynamic-update-slice_fusion.19.middle, f32[576,128]{1,0:T(8,128)S(1)} %collective-permute-done.15.far, ...), custom_call_target="tpu_custom_call" | custom-call | flops 3000000000 | bytes 1048576 | tf_op jit(solution)/shard_map/next_forces/pallas_call | solution.py:436
  56.1 2.7 %collective-permute-start.18 = (f32[48,128]{1,0:T(8,128)S(1)}, f32[48,128]{1,0:T(8,128)S(1)}, u32[]{:S(2)}, u32[]{:S(2)}) collective-permute-start(f32[48,128]{1,0:T(8,128)S(1)} %get-tuple-element.34), channel_id=1, source_target_pairs={{0,24},{1,25},{2,26},{3,27},{4,28},{5,29},{6,30},{7,31},{8,16},{9,... | collective-permute-start | bytes 73736 | tf_op jit(solution)/shard_map/ppermute | solution.py:43
  58.9 4.3 %collective-permute-done.17 = f32[96,128]{1,0:T(8,128)S(1)} collective-permute-done((f32[96,128]{1,0:T(8,128)S(1)}, f32[96,128]{1,0:T(8,128)S(1)}, u32[]{:S(2)}, u32[]{:S(2)}) %collective-permute-start.17) | collective-permute-done | bytes 49184 | tf_op jit(solution)/shard_map/ppermute | solution.py:43
  63.2 2.6 %collective-permute-start.22 = (f32[192,128]{1,0:T(8,128)S(1)}, f32[192,128]{1,0:T(8,128)S(1)}, u32[]{:S(2)}, u32[]{:S(2)}) collective-permute-start(f32[192,128]{1,0:T(8,128)S(1)} %get-tuple-element.64), channel_id=1, source_target_pairs={{0,6},{1,7},{2,4},{3,5},{4,2},{5,3},{6,0},{7,1},{8,14},{9,15},{10,... | collective-permute-start | bytes 294920 | tf_op jit(solution)/shard_map/ppermute | solution.py:43
  68.0 3.3 %near_forces.4.near_sums = f32[512,128]{1,0:T(8,128)S(1)} custom-call(f32[384,128]{1,0:T(8,128)S(1)} %constant_dynamic-update-slice_fusion.22.near, s32[32,128]{1,0:T(8,128)S(1)} %get-tuple-element.28.words), custom_call_target="tpu_custom_call" | custom-call | flops 1000000000 | bytes 1048576 | tf_op jit(solution)/shard_map/near_forces/pallas_call | solution.py:426
  73.1 5.6 %next_forces.3 = (f32[48,128]{1,0:T(8,128)S(1)}, f32[48,128]{1,0:T(8,128)S(1)}, f32[48,128]{1,0:T(8,128)S(1)}) custom-call(f32[384,128]{1,0:T(8,128)S(1)} %constant_dynamic-update-slice_fusion.22.near, f32[576,128]{1,0:T(8,128)S(1)} %constant_dynamic-update-slice_fusion.30.middle, f32[576,128]{1,0:T(8,128)S(1)} %collective-permute-done.23.far, ...), custom_call_target="tpu_custom_call" | custom-call | flops 3000000000 | bytes 1048576 | tf_op jit(solution)/shard_map/next_forces/pallas_call | solution.py:436
  78.9 2.8 %collective-permute-start.26 = (f32[48,128]{1,0:T(8,128)S(1)}, f32[48,128]{1,0:T(8,128)S(1)}, u32[]{:S(2)}, u32[]{:S(2)}) collective-permute-start(f32[48,128]{1,0:T(8,128)S(1)} %get-tuple-element.41), channel_id=1, source_target_pairs={{0,24},{1,25},{2,26},{3,27},{4,28},{5,29},{6,30},{7,31},{8,16},{9,... | collective-permute-start | bytes 73736 | tf_op jit(solution)/shard_map/ppermute | solution.py:43
  81.8 4.3 %collective-permute-done.25 = f32[96,128]{1,0:T(8,128)S(1)} collective-permute-done((f32[96,128]{1,0:T(8,128)S(1)}, f32[96,128]{1,0:T(8,128)S(1)}, u32[]{:S(2)}, u32[]{:S(2)}) %collective-permute-start.25) | collective-permute-done | bytes 49184 | tf_op jit(solution)/shard_map/ppermute | solution.py:43
  86.1 3.0 %collective-permute-start.30 = (f32[192,128]{1,0:T(8,128)S(1)}, f32[192,128]{1,0:T(8,128)S(1)}, u32[]{:S(2)}, u32[]{:S(2)}) collective-permute-start(f32[192,128]{1,0:T(8,128)S(1)} %get-tuple-element.60), channel_id=1, source_target_pairs={{0,6},{1,7},{2,4},{3,5},{4,2},{5,3},{6,0},{7,1},{8,14},{9,15},{10,... | collective-permute-start | bytes 294920 | tf_op jit(solution)/shard_map/ppermute | solution.py:43
  91.1 3.3 %near_forces.5.near_sums = f32[512,128]{1,0:T(8,128)S(1)} custom-call(f32[384,128]{1,0:T(8,128)S(1)} %constant_dynamic-update-slice_fusion.33.near, s32[32,128]{1,0:T(8,128)S(1)} %get-tuple-element.28.words), custom_call_target="tpu_custom_call" | custom-call | flops 1000000000 | bytes 1048576 | tf_op jit(solution)/shard_map/near_forces/pallas_call | solution.py:426
  96.1 6.0 %last_forces.1 = (f32[3,2048]{1,0:T(4,128)}, f32[3,2048]{1,0:T(4,128)}) custom-call(f32[384,128]{1,0:T(8,128)S(1)} %constant_dynamic-update-slice_fusion.33.near, f32[576,128]{1,0:T(8,128)S(1)} %constant_dynamic-update-slice_fusion.41.middle, f32[576,128]{1,0:T(8,128)S(1)} %collective-permute-done.31.far, f32[512,128]{1,0:T(8,128)S(1)} %near_forces.5.near_sums, ...), custom_call_target="tpu_custom_call" | custom-call | flops 3000000000 | bytes 1048576 | tf_op jit(solution)/shard_map/last_forces/pallas_call | solution.py:436
  (92 shorter events, 14.4 us)
Async XLA Ops:
  2.7 5.1 %collective-permute-start = (f32[56,128]{1,0:T(8,128)}, f32[56,128]{1,0:T(8,128)S(1)}, u32[]{:S(2)}, u32[]{:S(2)}) collective-permute-start(f32[56,128]{1,0:T(8,128)} %get-tuple-element.25), channel_id=1, source_target_pairs={{0,1},{1,0},{2,3},{3,2},{4,5},{5,4},{6,7},{7,6},{8,9},{9,8},{10,11... | collective-permute-start | bytes 86024 | tf_op jit(solution)/shard_map/ppermute | solution.py:43
  3.2 10.3 %collective-permute-start.2 = (f32[56,128]{1,0:T(8,128)}, f32[56,128]{1,0:T(8,128)S(1)}, u32[]{:S(2)}, u32[]{:S(2)}) collective-permute-start(f32[56,128]{1,0:T(8,128)} %get-tuple-element.25), channel_id=1, source_target_pairs={{0,24},{1,25},{2,26},{3,27},{4,28},{5,29},{6,30},{7,31},{8,16},{9,... | collective-permute-start | bytes 86024 | tf_op jit(solution)/shard_map/ppermute | solution.py:43
  8.6 4.8 %collective-permute-start.1 = (f32[112,128]{1,0:T(8,128)S(1)}, f32[112,128]{1,0:T(8,128)S(1)}, u32[]{:S(2)}, u32[]{:S(2)}) collective-permute-start(f32[112,128]{1,0:T(8,128)S(1)} %pad_maximum_fusion.4), channel_id=1, source_target_pairs={{0,8},{1,17},{2,10},{3,19},{4,12},{5,21},{6,14},{7,23},{8,0},{9,25... | collective-permute-start | bytes 172040 | tf_op jit(solution)/shard_map/ppermute | solution.py:43
  13.4 6.1 %collective-permute-start.4 = (f32[224,128]{1,0:T(8,128)S(1)}, f32[224,128]{1,0:T(8,128)S(1)}, u32[]{:S(2)}, u32[]{:S(2)}) collective-permute-start(f32[224,128]{1,0:T(8,128)S(1)} %get-tuple-element.56), channel_id=1, source_target_pairs={{0,2},{1,3},{2,0},{3,1},{4,6},{5,7},{6,4},{7,5},{8,10},{9,11},{10,... | collective-permute-start | bytes 344072 | tf_op jit(solution)/shard_map/ppermute | solution.py:43
  15.0 6.6 %collective-permute-start.6 = (f32[224,128]{1,0:T(8,128)S(1)}, f32[224,128]{1,0:T(8,128)S(1)}, u32[]{:S(2)}, u32[]{:S(2)}) collective-permute-start(f32[224,128]{1,0:T(8,128)S(1)} %get-tuple-element.56), channel_id=1, source_target_pairs={{0,6},{1,7},{2,4},{3,5},{4,2},{5,3},{6,0},{7,1},{8,14},{9,15},{10,... | collective-permute-start | bytes 344072 | tf_op jit(solution)/shard_map/ppermute | solution.py:43
  16.5 5.2 %collective-permute-start.5 = (f32[224,128]{1,0:T(8,128)S(1)}, f32[224,128]{1,0:T(8,128)S(1)}, u32[]{:S(2)}, u32[]{:S(2)}) collective-permute-start(f32[224,128]{1,0:T(8,128)S(1)} %get-tuple-element.56), channel_id=1, source_target_pairs={{0,4},{1,5},{2,6},{3,7},{4,0},{5,1},{6,2},{7,3},{8,12},{9,13},{10,... | collective-permute-start | bytes 344072 | tf_op jit(solution)/shard_map/ppermute | solution.py:43
  33.0 3.2 %collective-permute-start.8 = (f32[48,128]{1,0:T(8,128)S(1)}, f32[48,128]{1,0:T(8,128)S(1)}, u32[]{:S(2)}, u32[]{:S(2)}) collective-permute-start(f32[48,128]{1,0:T(8,128)S(1)} %get-tuple-element.27), channel_id=1, source_target_pairs={{0,1},{1,0},{2,3},{3,2},{4,5},{5,4},{6,7},{7,6},{8,9},{9,8},{10,11... | collective-permute-start | bytes 73736 | tf_op jit(solution)/shard_map/ppermute | solution.py:43
  33.2 7.4 %collective-permute-start.10 = (f32[48,128]{1,0:T(8,128)S(1)}, f32[48,128]{1,0:T(8,128)S(1)}, u32[]{:S(2)}, u32[]{:S(2)}) collective-permute-start(f32[48,128]{1,0:T(8,128)S(1)} %get-tuple-element.27), channel_id=1, source_target_pairs={{0,24},{1,25},{2,26},{3,27},{4,28},{5,29},{6,30},{7,31},{8,16},{9,... | collective-permute-start | bytes 73736 | tf_op jit(solution)/shard_map/ppermute | solution.py:43
  36.2 4.4 %collective-permute-start.9 = (f32[96,128]{1,0:T(8,128)S(1)}, f32[96,128]{1,0:T(8,128)S(1)}, u32[]{:S(2)}, u32[]{:S(2)}) collective-permute-start(f32[96,128]{1,0:T(8,128)S(1)} %pad_maximum_fusion.5), channel_id=1, source_target_pairs={{0,8},{1,17},{2,10},{3,19},{4,12},{5,21},{6,14},{7,23},{8,0},{9,25... | collective-permute-start | bytes 147464 | tf_op jit(solution)/shard_map/ppermute | solution.py:43
  40.6 8.1 %collective-permute-start.14 = (f32[192,128]{1,0:T(8,128)S(1)}, f32[192,128]{1,0:T(8,128)S(1)}, u32[]{:S(2)}, u32[]{:S(2)}) collective-permute-start(f32[192,128]{1,0:T(8,128)S(1)} %get-tuple-element.68), channel_id=1, source_target_pairs={{0,6},{1,7},{2,4},{3,5},{4,2},{5,3},{6,0},{7,1},{8,14},{9,15},{10,... | collective-permute-start | bytes 294920 | tf_op jit(solution)/shard_map/ppermute | solution.py:43
  43.4 5.3 %collective-permute-start.13 = (f32[192,128]{1,0:T(8,128)S(1)}, f32[192,128]{1,0:T(8,128)S(1)}, u32[]{:S(2)}, u32[]{:S(2)}) collective-permute-start(f32[192,128]{1,0:T(8,128)S(1)} %get-tuple-element.68), channel_id=1, source_target_pairs={{0,4},{1,5},{2,6},{3,7},{4,0},{5,1},{6,2},{7,3},{8,12},{9,13},{10,... | collective-permute-start | bytes 294920 | tf_op jit(solution)/shard_map/ppermute | solution.py:43
  43.4 5.4 %collective-permute-start.12 = (f32[192,128]{1,0:T(8,128)S(1)}, f32[192,128]{1,0:T(8,128)S(1)}, u32[]{:S(2)}, u32[]{:S(2)}) collective-permute-start(f32[192,128]{1,0:T(8,128)S(1)} %get-tuple-element.68), channel_id=1, source_target_pairs={{0,2},{1,3},{2,0},{3,1},{4,6},{5,7},{6,4},{7,5},{8,10},{9,11},{10,... | collective-permute-start | bytes 294920 | tf_op jit(solution)/shard_map/ppermute | solution.py:43
  55.9 2.9 %collective-permute-start.16 = (f32[48,128]{1,0:T(8,128)S(1)}, f32[48,128]{1,0:T(8,128)S(1)}, u32[]{:S(2)}, u32[]{:S(2)}) collective-permute-start(f32[48,128]{1,0:T(8,128)S(1)} %get-tuple-element.34), channel_id=1, source_target_pairs={{0,1},{1,0},{2,3},{3,2},{4,5},{5,4},{6,7},{7,6},{8,9},{9,8},{10,11... | collective-permute-start | bytes 73736 | tf_op jit(solution)/shard_map/ppermute | solution.py:43
  56.1 7.1 %collective-permute-start.18 = (f32[48,128]{1,0:T(8,128)S(1)}, f32[48,128]{1,0:T(8,128)S(1)}, u32[]{:S(2)}, u32[]{:S(2)}) collective-permute-start(f32[48,128]{1,0:T(8,128)S(1)} %get-tuple-element.34), channel_id=1, source_target_pairs={{0,24},{1,25},{2,26},{3,27},{4,28},{5,29},{6,30},{7,31},{8,16},{9,... | collective-permute-start | bytes 73736 | tf_op jit(solution)/shard_map/ppermute | solution.py:43
  58.8 4.4 %collective-permute-start.17 = (f32[96,128]{1,0:T(8,128)S(1)}, f32[96,128]{1,0:T(8,128)S(1)}, u32[]{:S(2)}, u32[]{:S(2)}) collective-permute-start(f32[96,128]{1,0:T(8,128)S(1)} %pad_maximum_fusion.6), channel_id=1, source_target_pairs={{0,8},{1,17},{2,10},{3,19},{4,12},{5,21},{6,14},{7,23},{8,0},{9,25... | collective-permute-start | bytes 147464 | tf_op jit(solution)/shard_map/ppermute | solution.py:43
  63.2 8.1 %collective-permute-start.22 = (f32[192,128]{1,0:T(8,128)S(1)}, f32[192,128]{1,0:T(8,128)S(1)}, u32[]{:S(2)}, u32[]{:S(2)}) collective-permute-start(f32[192,128]{1,0:T(8,128)S(1)} %get-tuple-element.64), channel_id=1, source_target_pairs={{0,6},{1,7},{2,4},{3,5},{4,2},{5,3},{6,0},{7,1},{8,14},{9,15},{10,... | collective-permute-start | bytes 294920 | tf_op jit(solution)/shard_map/ppermute | solution.py:43
  65.8 5.5 %collective-permute-start.21 = (f32[192,128]{1,0:T(8,128)S(1)}, f32[192,128]{1,0:T(8,128)S(1)}, u32[]{:S(2)}, u32[]{:S(2)}) collective-permute-start(f32[192,128]{1,0:T(8,128)S(1)} %get-tuple-element.64), channel_id=1, source_target_pairs={{0,4},{1,5},{2,6},{3,7},{4,0},{5,1},{6,2},{7,3},{8,12},{9,13},{10,... | collective-permute-start | bytes 294920 | tf_op jit(solution)/shard_map/ppermute | solution.py:43
  65.8 5.5 %collective-permute-start.20 = (f32[192,128]{1,0:T(8,128)S(1)}, f32[192,128]{1,0:T(8,128)S(1)}, u32[]{:S(2)}, u32[]{:S(2)}) collective-permute-start(f32[192,128]{1,0:T(8,128)S(1)} %get-tuple-element.64), channel_id=1, source_target_pairs={{0,2},{1,3},{2,0},{3,1},{4,6},{5,7},{6,4},{7,5},{8,10},{9,11},{10,... | collective-permute-start | bytes 294920 | tf_op jit(solution)/shard_map/ppermute | solution.py:43
  78.7 3.0 %collective-permute-start.24 = (f32[48,128]{1,0:T(8,128)S(1)}, f32[48,128]{1,0:T(8,128)S(1)}, u32[]{:S(2)}, u32[]{:S(2)}) collective-permute-start(f32[48,128]{1,0:T(8,128)S(1)} %get-tuple-element.41), channel_id=1, source_target_pairs={{0,1},{1,0},{2,3},{3,2},{4,5},{5,4},{6,7},{7,6},{8,9},{9,8},{10,11... | collective-permute-start | bytes 73736 | tf_op jit(solution)/shard_map/ppermute | solution.py:43
  78.9 7.2 %collective-permute-start.26 = (f32[48,128]{1,0:T(8,128)S(1)}, f32[48,128]{1,0:T(8,128)S(1)}, u32[]{:S(2)}, u32[]{:S(2)}) collective-permute-start(f32[48,128]{1,0:T(8,128)S(1)} %get-tuple-element.41), channel_id=1, source_target_pairs={{0,24},{1,25},{2,26},{3,27},{4,28},{5,29},{6,30},{7,31},{8,16},{9,... | collective-permute-start | bytes 73736 | tf_op jit(solution)/shard_map/ppermute | solution.py:43
  81.7 4.4 %collective-permute-start.25 = (f32[96,128]{1,0:T(8,128)S(1)}, f32[96,128]{1,0:T(8,128)S(1)}, u32[]{:S(2)}, u32[]{:S(2)}) collective-permute-start(f32[96,128]{1,0:T(8,128)S(1)} %pad_maximum_fusion.7), channel_id=1, source_target_pairs={{0,8},{1,17},{2,10},{3,19},{4,12},{5,21},{6,14},{7,23},{8,0},{9,25... | collective-permute-start | bytes 147464 | tf_op jit(solution)/shard_map/ppermute | solution.py:43
  86.1 8.2 %collective-permute-start.30 = (f32[192,128]{1,0:T(8,128)S(1)}, f32[192,128]{1,0:T(8,128)S(1)}, u32[]{:S(2)}, u32[]{:S(2)}) collective-permute-start(f32[192,128]{1,0:T(8,128)S(1)} %get-tuple-element.60), channel_id=1, source_target_pairs={{0,6},{1,7},{2,4},{3,5},{4,2},{5,3},{6,0},{7,1},{8,14},{9,15},{10,... | collective-permute-start | bytes 294920 | tf_op jit(solution)/shard_map/ppermute | solution.py:43
  89.1 5.2 %collective-permute-start.29 = (f32[192,128]{1,0:T(8,128)S(1)}, f32[192,128]{1,0:T(8,128)S(1)}, u32[]{:S(2)}, u32[]{:S(2)}) collective-permute-start(f32[192,128]{1,0:T(8,128)S(1)} %get-tuple-element.60), channel_id=1, source_target_pairs={{0,4},{1,5},{2,6},{3,7},{4,0},{5,1},{6,2},{7,3},{8,12},{9,13},{10,... | collective-permute-start | bytes 294920 | tf_op jit(solution)/shard_map/ppermute | solution.py:43
  89.1 5.2 %collective-permute-start.28 = (f32[192,128]{1,0:T(8,128)S(1)}, f32[192,128]{1,0:T(8,128)S(1)}, u32[]{:S(2)}, u32[]{:S(2)}) collective-permute-start(f32[192,128]{1,0:T(8,128)S(1)} %get-tuple-element.60), channel_id=1, source_target_pairs={{0,2},{1,3},{2,0},{3,1},{4,6},{5,7},{6,4},{7,5},{8,10},{9,11},{10,... | collective-permute-start | bytes 294920 | tf_op jit(solution)/shard_map/ppermute | solution.py:43
  (10 other events, 19.5 us)

commit v5 on v4

--- a/solution.py
+++ b/solution.py
@@ -15,9 +15,9 @@
 
 LANES = 128
 LIST_ROWS = 8
-UNROLL = 32
-LEAD = 4
-LAG = 8
+STEP = 16
+LEAD = 2
+LAG = 6
 BASE_BITS = 14
 BASE_MASK = (1 << BASE_BITS) - 1
 FAR = 1.0e6
@@ -61,13 +61,14 @@
     return near, jnp.concatenate([near, rest] if far is None else [near, far, rest], 0)
 
 
-def gather_last(near, devices, beside=None):
+def gather_last(near, devices):
     low, count = stage_masks(devices)[-2]
-    parts = [send(near, devices, lambda d: step << low) for step in range(1, count)]
-    if beside is not None:
-        parts, beside = lax.optimization_barrier((parts, beside))
+    return [send(near, devices, lambda d: step << low) for step in range(1, count)]
+
+
+def exchange(parts, devices):
     parts = jnp.concatenate(parts, 0)
-    return parts, send(parts, devices, lambda d: 1), beside
+    return parts, send(parts, devices, lambda d: 1)
 
 
 def near_size(devices):
@@ -121,8 +122,8 @@
 def load_points(size, pieces, rows, points):
     devices, blocks = size
     stride = 4 * blocks
-    for ref, slots in pieces:
-        for n, slot in enumerate(slots):
+    for ref, first, slots in pieces:
+        for n, slot in enumerate(slots, first):
             norm = None
             for c in range(3):
                 y = 0.5 * ref[pl.ds(n * rows + c * blocks, blocks), :]
@@ -149,7 +150,7 @@
         lefts[b] = jnp.concatenate([high, high, high, mid, mid, low], 0).astype(jnp.bfloat16)
     sums[...] = jnp.zeros_like(sums)
     ready()
-    steps = [units[units.shape[0] - 1, LANES - 1 - n] for n in range(2)]
+    steps = [units[0, n] for n in range(2)]
     begin, end = {0: (0, steps[0]), 1: (steps[0], steps[1]), None: (0, steps[1])}[part]
 
     def right_tile(word):
@@ -159,7 +160,7 @@
         return jnp.concatenate([high, mid, low, high, mid, high], 0).astype(jnp.bfloat16)
 
     def word(unit, n):
-        at = 2 * unit + n
+        at = 2 * unit + n + LANES
         return units[at >> 7, at & (LANES - 1)]
 
     def block_of(unit):
@@ -180,28 +181,52 @@
         sums[at, :] = sums[at, :] + (part[:, :LANES] + part[:, LANES:])
 
     for k in range(LEAD):
-        turned_kept[k], right_kept[k] = fetch(begin * UNROLL + k)
+        turned_kept[k], right_kept[k] = fetch(begin * STEP + k)
     weights_kept[...] = jnp.zeros_like(weights_kept)
     partner_kept[...] = jnp.zeros_like(partner_kept)
 
-    def group(number, carry):
-        first = number * UNROLL
+    def group(first, many):
         fetched = [(turned_kept[k], right_kept[k]) for k in range(LEAD)]
         weighed = [(partner_kept[k], weights_kept[k]) for k in range(LAG)]
-        for k in range(UNROLL):
+        for k in range(many):
             add(jnp.maximum(first + k - LAG, 0), *weighed[k])
             turned, right = fetched[k]
             weighed.append((right, weigh(first + k, turned)))
             fetched.append(fetch(first + k + LEAD))
         for k in range(LEAD):
-            turned_kept[k], right_kept[k] = fetched[UNROLL + k]
+            turned_kept[k], right_kept[k] = fetched[many + k]
         for k in range(LAG):
-            partner_kept[k], weights_kept[k] = weighed[UNROLL + k]
+            partner_kept[k], weights_kept[k] = weighed[many + k]
+
+    def double(number, carry):
+        group((begin + 2 * number) * STEP, 2 * STEP)
         return carry
 
-    lax.fori_loop(begin, end, group, 0)
+    lax.fori_loop(0, (end - begin) >> 1, double, 0)
+
+    @pl.when(((end - begin) & 1) == 1)
+    def _():
+        group((end - 1) * STEP, STEP)
+
     for k in range(LAG):
-        add(jnp.maximum(end * UNROLL - LAG + k, 0), partner_kept[k], weights_kept[k])
+        add(jnp.maximum(end * STEP - LAG + k, 0), partner_kept[k], weights_kept[k])
+
+
+def start_list(words, units, sem):
+    copy = pltpu.make_async_copy(words.at[pl.ds(0, 8)], units.at[pl.ds(0, 8)], sem)
+    copy.start()
+
+    def ready():
+        copy.wait()
+
+        @pl.when(LANES + 2 * (units[0, 1] * STEP + LEAD) > 8 * LANES)
+        def _():
+            more = pl.ds(8, units.shape[0] - 8)
+            rest = pltpu.make_async_copy(words.at[more], units.at[more], sem)
+            rest.start()
+            rest.wait()
+
+    return ready
 
 
 def forces_of(blocks, points, all_sums):
@@ -242,7 +267,7 @@
     place = jnp.where(by_row, right_place, left_place)
     slot = slot_of(other, me, devices)
     back = (devices - slot) * (4 * blocks) - place
-    group = jnp.where(valid, jnp.where(slot < 2 * near_size(devices), mine, mine + blocks), -1)
+    group = jnp.where(valid, jnp.where(slot < slot_ranges(devices)[2][0], mine, mine + blocks), -1)
 
     ones = jnp.bfloat16
     groups = 2 * blocks
@@ -266,7 +291,7 @@
         return matmul(pieces[0], mask) + 64.0 * matmul(pieces[1], mask)
 
     in_near = one < blocks
-    step = 2 * UNROLL
+    step = 2 * STEP
     near_steps = (total_over(in_near).astype(jnp.int32) + step - 1) >> (step.bit_length() - 1)
     far_steps = (total_over(~in_near).astype(jnp.int32) + step - 1) >> (step.bit_length() - 1)
     offset = total_over((one < two) & (in_near == (two < blocks)))
@@ -276,7 +301,7 @@
     for g in range(groups):
         part = slice(g * height, (g + 1) * height)
         position = position + chosen[part] * (before[part] + start[:, g : g + 1])
-    position = position.astype(jnp.int32)
+    position = position.astype(jnp.int32) + LANES
     high = jnp.where(valid, position >> 7, -1)
     low = position & (LANES - 1)
 
@@ -295,17 +320,17 @@
     words = found.astype(jnp.int32)
     words = words[:rows] + words[rows : 2 * rows] * 64 + words[2 * rows :] * (BASE_MASK + 1)
     lane = lax.broadcasted_iota(jnp.int32, (rows, LANES), 1)
-    words = jnp.where((place == rows - 1) & (lane == LANES - 1), near_steps[:1], words)
-    out[...] = jnp.where((place == rows - 1) & (lane == LANES - 2), (near_steps + far_steps)[:1], words)
+    words = jnp.where((place == 0) & (lane == 0), near_steps[:1], words)
+    out[...] = jnp.where((place == 0) & (lane == 1), (near_steps + far_steps)[:1], words)
 
 
 def slot_ranges(devices):
-    near = 2 * near_size(devices)
-    middle = near + (devices - near) // 2
-    return range(near), range(near, middle), range(middle, devices)
-
-
-def first_kernel(size, shape, near, middle, far, velocity, x_next, force_out, words, codes, units, sem, *scratch):
+    near = near_size(devices)
+    middle = near + devices // 2
+    return range(2 * near), range(2 * near, 3 * near), range(3 * near, middle), range(middle, devices)
+
+
+def first_kernel(size, shape, gathered, velocity, x_next, force_out, words, codes, units, sem, *scratch):
     devices, blocks = size
     nrow, ncol, span = shape
     rows = 3 * blocks + LIST_ROWS
@@ -313,35 +338,27 @@
     me = row * ncol + col
     holders = [row * ncol + c for c in range(ncol)] + [r * ncol + col for r in range(nrow)]
     codes[...] = jnp.full_like(codes, -1)
-    pieces = list(zip((near, middle, far), slot_ranges(devices)))
     for n, holder in enumerate(holders):
-        slot = slot_of(holder, me, devices)
-        for ref, slots in pieces:
-
-            @pl.when((slot >= slots[0]) & (slot <= slots[-1]))
-            def _(ref=ref, slots=slots):
-                at = pl.multiple_of((slot - slots[0]) * rows + 3 * blocks, 8)
-                tile = ref[pl.ds(at, LIST_ROWS), :]
-                codes[pl.ds(n * span, span), :] = tile[:span].astype(jnp.int32)
+        at = pl.multiple_of(slot_of(holder, me, devices) * rows + 3 * blocks, 8)
+        codes[pl.ds(n * span, span), :] = gathered[pl.ds(at, LIST_ROWS), :][:span].astype(jnp.int32)
 
     build_units(size, shape, codes, words)
-    copy = pltpu.make_async_copy(words, units, sem)
-    copy.start()
-    load_points(size, pieces, rows, scratch[0])
-    add_pairs(size, None, units, copy.wait, *scratch)
+    ready = start_list(words, units, sem)
+    load_points(size, [(gathered, 0, range(devices))], rows, scratch[0])
+    add_pairs(size, None, units, ready, *scratch)
     forces = forces_of(blocks, scratch[0], [scratch[2]])
     for c in range(3):
         at = pl.ds(c * blocks, blocks)
         force_out[at, :] = forces[c]
-        x_next[at, :] = near[at, :] + TIME_STEP * velocity[at, :] + (0.5 * TIME_STEP * TIME_STEP) * forces[c]
-
-
-def near_kernel(size, near, words, sums_out, units, sem, points, lefts, *kept):
-    devices, blocks = size
-    copy = pltpu.make_async_copy(words, units, sem)
-    copy.start()
-    load_points(size, [(near, slot_ranges(devices)[0])], 3 * blocks, points)
-    add_pairs(size, 0, units, copy.wait, points, lefts, sums_out, *kept)
+        x_next[at, :] = gathered[at, :] + TIME_STEP * velocity[at, :] + (0.5 * TIME_STEP * TIME_STEP) * forces[c]
+
+
+def near_kernel(size, near, part, words, sums_out, units, sem, points, lefts, *kept):
+    devices, blocks = size
+    ready = start_list(words, units, sem)
+    ranges = slot_ranges(devices)
+    load_points(size, [(near, 0, ranges[0]), (part, 0, ranges[1])], 3 * blocks, points)
+    add_pairs(size, 0, units, ready, points, lefts, sums_out, *kept)
 
 
 def next_kernel(size, last, near, middle, far, near_sums, velocity, force, words, x_next, v_next, *rest):
@@ -349,11 +366,11 @@
     if not last:
         force_out, *rest = rest
     units, sem, points, lefts, sums, *kept = rest
-    copy = pltpu.make_async_copy(words, units, sem)
-    copy.start()
-    _, *ranges = slot_ranges(devices)
-    load_points(size, [(near, range(1))] + list(zip((middle, far), ranges)), 3 * blocks, points)
-    add_pairs(size, 1, units, copy.wait, points, lefts, sums, *kept)
+    ready = start_list(words, units, sem)
+    ranges = slot_ranges(devices)
+    pieces = [(near, 0, range(1)), (middle, len(ranges[1]), ranges[2]), (far, 0, ranges[3])]
+    load_points(size, pieces, 3 * blocks, points)
+    add_pairs(size, 1, units, ready, points, lefts, sums, *kept)
     forces = forces_of(blocks, points, [near_sums, sums])
     for c in range(3):
         at = pl.ds(c * blocks, blocks)
@@ -378,7 +395,7 @@
     slots = pairs.shape[0]
     size = (devices, blocks)
     span = slots // LANES
-    entries = (nrow + ncol) * slots + 2 * blocks + 2 * (2 * UNROLL + LEAD)
+    entries = LANES + (nrow + ncol) * slots + 2 * blocks + 2 * (3 * STEP + LEAD)
     unit_rows = 8 * (entries // (8 * LANES) + 1)
     code_rows = 8 * (-(-(nrow + ncol) * span // 8))
     flat = jax.ShapeDtypeStruct((3 * blocks, LANES), jnp.float32)
@@ -413,26 +430,28 @@
     current, force, words = pl.pallas_call(
         functools.partial(first_kernel, size, (nrow, ncol, span)),
         out_shape=[flat, flat, unit_list],
-        in_specs=[vmem] * 4,
+        in_specs=[vmem] * 2,
         out_specs=[vmem] * 3,
         scratch_shapes=[pltpu.VMEM((code_rows, LANES), jnp.int32)] + listed + [points, lefts, sums] + kept,
         compiler_params=params,
         cost_estimate=cost(1.0),
         name="first_forces",
-    )(both, *gather_last(near, devices)[:2], velocity)
+    )(jnp.concatenate([both, *exchange(gather_last(near, devices), devices)], 0), velocity)
     for turn in range(STEPS):
         last = turn == STEPS - 1
         near, both = gather_near(current, devices)
+        parts = gather_last(near, devices)
         near_sums = pl.pallas_call(
             functools.partial(near_kernel, size),
             out_shape=jax.ShapeDtypeStruct((blocks * 32, LANES), jnp.float32),
-            in_specs=[vmem] * 2,
+            in_specs=[vmem] * 3,
             out_specs=vmem,
             scratch_shapes=listed + [points, lefts] + kept,
             compiler_params=params,
             cost_estimate=cost(0.25),
             name="near_forces",
-        )(both, words)
+        )(both, parts[0], words)
+        parts, near_sums = lax.optimization_barrier((parts, near_sums))
         result = pl.pallas_call(
             functools.partial(next_kernel, size, last),
             out_shape=[whole] * 2 if last else [flat] * 3,
@@ -442,7 +461,7 @@
             compiler_params=params,
             cost_estimate=cost(0.75),
             name="last_forces" if last else "next_forces",
-        )(both, *gather_last(near, devices, near_sums), velocity, force, words)
+        )(both, *exchange(parts, devices), near_sums, velocity, force, words)
         if last:
             current, velocity = result
         else:

time: 104 us -> 100 us (0.962); the launches traced: 102 us -> 99.9 us
  Pallas kernels: 37.7 us -> 30.8 us
  waiting for transfers between devices: 31.7 us -> 37.1 us
    ppermute x32, waiting for transfers between devices: 31.7 us -> 37.1 us  [send(): return lax.ppermute(block, AXES, [(d, d ^ mask(d)) for d in range(devices)])]
    pallas_call x3, Pallas kernels: 17 us -> 12.9 us  [body(): pl.pallas_call(functools.partial(next_kernel, size, last), out_shape=[who...]
    pallas_call x1, Pallas kernels: 9.4 us -> 7.64 us  [body(): pl.pallas_call(functools.partial(first_kernel, size, (nrow, ncol, span)),...]
  transfers between devices with their start and end apart: 32 -> 32, of which waited for: 13 -> 17; matrix products, arithmetic and copies ran while one was open for 1% -> 1% of each run, Pallas kernels for 10% -> 9%
where the time goes in v5:
time: 100 us; the launch traced here: 99.9 us
  waiting for transfers between devices  37.1 us (37%)
  Pallas kernels  30.8 us (31%)
  starting transfers between devices  29 us (29%)
  between operations  1.89 us (2%)
    ppermute x32, waiting for transfers between devices, send(): return lax.ppermute(block, AXES, [(d, d ^ mask(d)) for d in range(devices)])  37.1 us
    ppermute x32, starting transfers between devices, send(): return lax.ppermute(block, AXES, [(d, d ^ mask(d)) for d in range(devices)])  29 us
    pallas_call x3, Pallas kernels, body(): pl.pallas_call(functools.partial(next_kernel, size, last), out_shape=[who...  12.9 us
    pallas_call x3, Pallas kernels, body(): pl.pallas_call(functools.partial(near_kernel, size), out_shape=jax.ShapeD...  8.81 us
    pallas_call x1, Pallas kernels, body(): pl.pallas_call(functools.partial(first_kernel, size, (nrow, ncol, span)),...  7.64 us
  transfers between devices with their start and end apart: 32, of which 17 were waited for; matrix products, arithmetic and copies ran while one was open for 1% of the time, Pallas kernels for 9%

profile of v5, /device:TPU:0, one launch (start us, length us, event | category | flops | bytes accessed | tf_op | source)
XLA Modules:
  0.0 99.9 jit_solution(1956349474695818380)
XLA Ops:
  3.2 4.7 %collective-permute-start.2 = (f32[56,128]{1,0:T(8,128)}, f32[56,128]{1,0:T(8,128)S(1)}, u32[]{:S(2)}, u32[]{:S(2)}) collective-permute-start(f32[56,128]{1,0:T(8,128)} %get-tuple-element.25), channel_id=1, source_target_pairs={{0,24},{1,25},{2,26},{3,27},{4,28},{5,29},{6,30},{7,31},{8,16},{9,... | collective-permute-start | bytes 86024 | tf_op jit(solution)/shard_map/ppermute | solution.py:43
  8.6 4.8 %collective-permute-done.1 = f32[112,128]{1,0:T(8,128)S(1)} collective-permute-done((f32[112,128]{1,0:T(8,128)S(1)}, f32[112,128]{1,0:T(8,128)S(1)}, u32[]{:S(2)}, u32[]{:S(2)}) %collective-permute-start.1) | collective-permute-done | bytes 57376 | tf_op jit(solution)/shard_map/ppermute | solution.py:43
  13.4 1.6 %collective-permute-start.4 = (f32[224,128]{1,0:T(8,128)S(1)}, f32[224,128]{1,0:T(8,128)S(1)}, u32[]{:S(2)}, u32[]{:S(2)}) collective-permute-start(f32[224,128]{1,0:T(8,128)S(1)} %get-tuple-element.56), channel_id=1, source_target_pairs={{0,2},{1,3},{2,0},{3,1},{4,6},{5,7},{6,4},{7,5},{8,10},{9,11},{10,... | collective-permute-start | bytes 344072 | tf_op jit(solution)/shard_map/ppermute | solution.py:43
  18.3 2.1 %collective-permute-done.5 = f32[224,128]{1,0:T(8,128)S(1)} collective-permute-done((f32[224,128]{1,0:T(8,128)S(1)}, f32[224,128]{1,0:T(8,128)S(1)}, u32[]{:S(2)}, u32[]{:S(2)}) %collective-permute-start.5) | collective-permute-done | bytes 114720 | tf_op jit(solution)/shard_map/ppermute | solution.py:43
  20.4 1.8 %collective-permute-done.6 = f32[224,128]{1,0:T(8,128)S(1)} collective-permute-done((f32[224,128]{1,0:T(8,128)S(1)}, f32[224,128]{1,0:T(8,128)S(1)}, u32[]{:S(2)}, u32[]{:S(2)}) %collective-permute-start.6) | collective-permute-done | bytes 114720 | tf_op jit(solution)/shard_map/ppermute | solution.py:43
  22.4 1.6 %collective-permute-done.7 = f32[672,128]{1,0:T(8,128)S(1)} collective-permute-done((f32[672,128]{1,0:T(8,128)S(1)}, f32[672,128]{1,0:T(8,128)S(1)}, u32[]{:S(2)}, u32[]{:S(2)}) %collective-permute-start.7) | collective-permute-done | bytes 344096 | tf_op jit(solution)/shard_map/ppermute | solution.py:43
  24.0 7.6 %first_forces.1 = (f32[48,128]{1,0:T(8,128)S(1)}, f32[48,128]{1,0:T(8,128)S(1)}, s32[32,128]{1,0:T(8,128)S(1)}) custom-call(f32[1792,128]{1,0:T(8,128)S(1)} %constant_dynamic-update-slice_fusion.3.gathered, f32[48,128]{1,0:T(8,128)S(1)} %copy-done), custom_call_target="tpu_custom_call" | custom-call | flops 4000000000 | bytes 1048576 | tf_op jit(solution)/shard_map/first_forces/pallas_call | solution.py:430
  31.9 1.9 %collective-permute-start.10 = (f32[48,128]{1,0:T(8,128)S(1)}, f32[48,128]{1,0:T(8,128)S(1)}, u32[]{:S(2)}, u32[]{:S(2)}) collective-permute-start(f32[48,128]{1,0:T(8,128)S(1)} %get-tuple-element.27), channel_id=1, source_target_pairs={{0,24},{1,25},{2,26},{3,27},{4,28},{5,29},{6,30},{7,31},{8,16},{9,... | collective-permute-start | bytes 73736 | tf_op jit(solution)/shard_map/ppermute | solution.py:43
  33.9 4.7 %collective-permute-done.9 = f32[96,128]{1,0:T(8,128)S(1)} collective-permute-done((f32[96,128]{1,0:T(8,128)S(1)}, f32[96,128]{1,0:T(8,128)S(1)}, u32[]{:S(2)}, u32[]{:S(2)}) %collective-permute-start.9) | collective-permute-done | bytes 49184 | tf_op jit(solution)/shard_map/ppermute | solution.py:43
  38.6 1.7 %collective-permute-start.12 = (f32[192,128]{1,0:T(8,128)S(1)}, f32[192,128]{1,0:T(8,128)S(1)}, u32[]{:S(2)}, u32[]{:S(2)}) collective-permute-start(f32[192,128]{1,0:T(8,128)S(1)} %get-tuple-element.68), channel_id=1, source_target_pairs={{0,2},{1,3},{2,0},{3,1},{4,6},{5,7},{6,4},{7,5},{8,10},{9,11},{10,... | collective-permute-start | bytes 294920 | tf_op jit(solution)/shard_map/ppermute | solution.py:43
  40.3 2.2 %collective-permute-start.13 = (f32[192,128]{1,0:T(8,128)S(1)}, f32[192,128]{1,0:T(8,128)S(1)}, u32[]{:S(2)}, u32[]{:S(2)}) collective-permute-start(f32[192,128]{1,0:T(8,128)S(1)} %get-tuple-element.68), channel_id=1, source_target_pairs={{0,4},{1,5},{2,6},{3,7},{4,0},{5,1},{6,2},{7,3},{8,12},{9,13},{10,... | collective-permute-start | bytes 294920 | tf_op jit(solution)/shard_map/ppermute | solution.py:43
  43.9 2.9 %near_forces.3.near_sums = f32[512,128]{1,0:T(8,128)S(1)} custom-call(f32[384,128]{1,0:T(8,128)S(1)} %constant_dynamic-update-slice_fusion.12.near, f32[192,128]{1,0:T(8,128)S(1)} %collective-permute-done.12.part, s32[32,128]{1,0:T(8,128)S(1)} %get-tuple-element.28.words), custom_call_target="tpu_custom_call" | custom-call | flops 1000000000 | bytes 1048576 | tf_op jit(solution)/shard_map/near_forces/pallas_call | solution.py:444
  49.7 4.1 %next_forces.2 = (f32[48,128]{1,0:T(8,128)S(1)}, f32[48,128]{1,0:T(8,128)S(1)}, f32[48,128]{1,0:T(8,128)S(1)}) custom-call(f32[384,128]{1,0:T(8,128)S(1)} %constant_dynamic-update-slice_fusion.12.near, f32[576,128]{1,0:T(8,128)S(1)} %constant_dynamic-update-slice_fusion.20.middle, f32[576,128]{1,0:T(8,128)S(1)} %collective-permute-done.15.far, ...), custom_call_target="tpu_custom_call" | custom-call | flops 3000000000 | bytes 1048576 | tf_op jit(solution)/shard_map/next_forces/pallas_call | solution.py:455
  54.0 1.9 %collective-permute-start.18 = (f32[48,128]{1,0:T(8,128)S(1)}, f32[48,128]{1,0:T(8,128)S(1)}, u32[]{:S(2)}, u32[]{:S(2)}) collective-permute-start(f32[48,128]{1,0:T(8,128)S(1)} %get-tuple-element.34), channel_id=1, source_target_pairs={{0,24},{1,25},{2,26},{3,27},{4,28},{5,29},{6,30},{7,31},{8,16},{9,... | collective-permute-start | bytes 73736 | tf_op jit(solution)/shard_map/ppermute | solution.py:43
  55.9 4.8 %collective-permute-done.17 = f32[96,128]{1,0:T(8,128)S(1)} collective-permute-done((f32[96,128]{1,0:T(8,128)S(1)}, f32[96,128]{1,0:T(8,128)S(1)}, u32[]{:S(2)}, u32[]{:S(2)}) %collective-permute-start.17) | collective-permute-done | bytes 49184 | tf_op jit(solution)/shard_map/ppermute | solution.py:43
  60.7 2.3 %collective-permute-start.20 = (f32[192,128]{1,0:T(8,128)S(1)}, f32[192,128]{1,0:T(8,128)S(1)}, u32[]{:S(2)}, u32[]{:S(2)}) collective-permute-start(f32[192,128]{1,0:T(8,128)S(1)} %get-tuple-element.64), channel_id=1, source_target_pairs={{0,2},{1,3},{2,0},{3,1},{4,6},{5,7},{6,4},{7,5},{8,10},{9,11},{10,... | collective-permute-start | bytes 294920 | tf_op jit(solution)/shard_map/ppermute | solution.py:43
  65.8 2.9 %near_forces.4.near_sums = f32[512,128]{1,0:T(8,128)S(1)} custom-call(f32[384,128]{1,0:T(8,128)S(1)} %constant_dynamic-update-slice_fusion.23.near, f32[192,128]{1,0:T(8,128)S(1)} %collective-permute-done.20.part, s32[32,128]{1,0:T(8,128)S(1)} %get-tuple-element.28.words), custom_call_target="tpu_custom_call" | custom-call | flops 1000000000 | bytes 1048576 | tf_op jit(solution)/shard_map/near_forces/pallas_call | solution.py:444
  71.4 4.2 %next_forces.3 = (f32[48,128]{1,0:T(8,128)S(1)}, f32[48,128]{1,0:T(8,128)S(1)}, f32[48,128]{1,0:T(8,128)S(1)}) custom-call(f32[384,128]{1,0:T(8,128)S(1)} %constant_dynamic-update-slice_fusion.23.near, f32[576,128]{1,0:T(8,128)S(1)} %constant_dynamic-update-slice_fusion.31.middle, f32[576,128]{1,0:T(8,128)S(1)} %collective-permute-done.23.far, ...), custom_call_target="tpu_custom_call" | custom-call | flops 3000000000 | bytes 1048576 | tf_op jit(solution)/shard_map/next_forces/pallas_call | solution.py:455
  75.8 3.2 %collective-permute-start.26 = (f32[48,128]{1,0:T(8,128)S(1)}, f32[48,128]{1,0:T(8,128)S(1)}, u32[]{:S(2)}, u32[]{:S(2)}) collective-permute-start(f32[48,128]{1,0:T(8,128)S(1)} %get-tuple-element.41), channel_id=1, source_target_pairs={{0,24},{1,25},{2,26},{3,27},{4,28},{5,29},{6,30},{7,31},{8,16},{9,... | collective-permute-start | bytes 73736 | tf_op jit(solution)/shard_map/ppermute | solution.py:43
  79.1 4.3 %collective-permute-done.25 = f32[96,128]{1,0:T(8,128)S(1)} collective-permute-done((f32[96,128]{1,0:T(8,128)S(1)}, f32[96,128]{1,0:T(8,128)S(1)}, u32[]{:S(2)}, u32[]{:S(2)}) %collective-permute-start.25) | collective-permute-done | bytes 49184 | tf_op jit(solution)/shard_map/ppermute | solution.py:43
  84.4 3.4 %collective-permute-start.29 = (f32[192,128]{1,0:T(8,128)S(1)}, f32[192,128]{1,0:T(8,128)S(1)}, u32[]{:S(2)}, u32[]{:S(2)}) collective-permute-start(f32[192,128]{1,0:T(8,128)S(1)} %get-tuple-element.60), channel_id=1, source_target_pairs={{0,4},{1,5},{2,6},{3,7},{4,0},{5,1},{6,2},{7,3},{8,12},{9,13},{10,... | collective-permute-start | bytes 294920 | tf_op jit(solution)/shard_map/ppermute | solution.py:43
  89.2 2.9 %near_forces.5.near_sums = f32[512,128]{1,0:T(8,128)S(1)} custom-call(f32[384,128]{1,0:T(8,128)S(1)} %constant_dynamic-update-slice_fusion.34.near, f32[192,128]{1,0:T(8,128)S(1)} %collective-permute-done.28.part, s32[32,128]{1,0:T(8,128)S(1)} %get-tuple-element.28.words), custom_call_target="tpu_custom_call" | custom-call | flops 1000000000 | bytes 1048576 | tf_op jit(solution)/shard_map/near_forces/pallas_call | solution.py:444
  93.5 1.6 %collective-permute-done.31.far = f32[576,128]{1,0:T(8,128)S(1)} collective-permute-done((f32[576,128]{1,0:T(8,128)S(1)}, f32[576,128]{1,0:T(8,128)S(1)}, u32[]{:S(2)}, u32[]{:S(2)}) %collective-permute-start.31) | collective-permute-done | bytes 294944 | tf_op jit(solution)/shard_map/ppermute | solution.py:43
  95.1 4.7 %last_forces.1 = (f32[3,2048]{1,0:T(4,128)}, f32[3,2048]{1,0:T(4,128)}) custom-call(f32[384,128]{1,0:T(8,128)S(1)} %constant_dynamic-update-slice_fusion.34.near, f32[576,128]{1,0:T(8,128)S(1)} %constant_dynamic-update-slice_fusion.42.middle, f32[576,128]{1,0:T(8,128)S(1)} %collective-permute-done.31.far, f32[512,128]{1,0:T(8,128)S(1)} %near_forces.5.near_sums, ...), custom_call_target="tpu_custom_call" | custom-call | flops 3000000000 | bytes 1048576 | tf_op jit(solution)/shard_map/last_forces/pallas_call | solution.py:455
  (94 shorter events, 20.2 us)
Async XLA Ops:
  2.7 5.1 %collective-permute-start = (f32[56,128]{1,0:T(8,128)}, f32[56,128]{1,0:T(8,128)S(1)}, u32[]{:S(2)}, u32[]{:S(2)}) collective-permute-start(f32[56,128]{1,0:T(8,128)} %get-tuple-element.25), channel_id=1, source_target_pairs={{0,1},{1,0},{2,3},{3,2},{4,5},{5,4},{6,7},{7,6},{8,9},{9,8},{10,11... | collective-permute-start | bytes 86024 | tf_op jit(solution)/shard_map/ppermute | solution.py:43
  3.2 10.3 %collective-permute-start.2 = (f32[56,128]{1,0:T(8,128)}, f32[56,128]{1,0:T(8,128)S(1)}, u32[]{:S(2)}, u32[]{:S(2)}) collective-permute-start(f32[56,128]{1,0:T(8,128)} %get-tuple-element.25), channel_id=1, source_target_pairs={{0,24},{1,25},{2,26},{3,27},{4,28},{5,29},{6,30},{7,31},{8,16},{9,... | collective-permute-start | bytes 86024 | tf_op jit(solution)/shard_map/ppermute | solution.py:43
  8.6 4.8 %collective-permute-start.1 = (f32[112,128]{1,0:T(8,128)S(1)}, f32[112,128]{1,0:T(8,128)S(1)}, u32[]{:S(2)}, u32[]{:S(2)}) collective-permute-start(f32[112,128]{1,0:T(8,128)S(1)} %pad_maximum_fusion.5), channel_id=1, source_target_pairs={{0,8},{1,17},{2,10},{3,19},{4,12},{5,21},{6,14},{7,23},{8,0},{9,25... | collective-permute-start | bytes 172040 | tf_op jit(solution)/shard_map/ppermute | solution.py:43
  13.4 4.9 %collective-permute-start.4 = (f32[224,128]{1,0:T(8,128)S(1)}, f32[224,128]{1,0:T(8,128)S(1)}, u32[]{:S(2)}, u32[]{:S(2)}) collective-permute-start(f32[224,128]{1,0:T(8,128)S(1)} %get-tuple-element.56), channel_id=1, source_target_pairs={{0,2},{1,3},{2,0},{3,1},{4,6},{5,7},{6,4},{7,5},{8,10},{9,11},{10,... | collective-permute-start | bytes 344072 | tf_op jit(solution)/shard_map/ppermute | solution.py:43
  15.0 5.4 %collective-permute-start.5 = (f32[224,128]{1,0:T(8,128)S(1)}, f32[224,128]{1,0:T(8,128)S(1)}, u32[]{:S(2)}, u32[]{:S(2)}) collective-permute-start(f32[224,128]{1,0:T(8,128)S(1)} %get-tuple-element.56), channel_id=1, source_target_pairs={{0,4},{1,5},{2,6},{3,7},{4,0},{5,1},{6,2},{7,3},{8,12},{9,13},{10,... | collective-permute-start | bytes 344072 | tf_op jit(solution)/shard_map/ppermute | solution.py:43
  16.5 5.7 %collective-permute-start.6 = (f32[224,128]{1,0:T(8,128)S(1)}, f32[224,128]{1,0:T(8,128)S(1)}, u32[]{:S(2)}, u32[]{:S(2)}) collective-permute-start(f32[224,128]{1,0:T(8,128)S(1)} %get-tuple-element.56), channel_id=1, source_target_pairs={{0,6},{1,7},{2,4},{3,5},{4,2},{5,3},{6,0},{7,1},{8,14},{9,15},{10,... | collective-permute-start | bytes 344072 | tf_op jit(solution)/shard_map/ppermute | solution.py:43
  31.6 2.1 %collective-permute-start.8 = (f32[48,128]{1,0:T(8,128)S(1)}, f32[48,128]{1,0:T(8,128)S(1)}, u32[]{:S(2)}, u32[]{:S(2)}) collective-permute-start(f32[48,128]{1,0:T(8,128)S(1)} %get-tuple-element.27), channel_id=1, source_target_pairs={{0,1},{1,0},{2,3},{3,2},{4,5},{5,4},{6,7},{7,6},{8,9},{9,8},{10,11... | collective-permute-start | bytes 73736 | tf_op jit(solution)/shard_map/ppermute | solution.py:43
  31.9 6.8 %collective-permute-start.10 = (f32[48,128]{1,0:T(8,128)S(1)}, f32[48,128]{1,0:T(8,128)S(1)}, u32[]{:S(2)}, u32[]{:S(2)}) collective-permute-start(f32[48,128]{1,0:T(8,128)S(1)} %get-tuple-element.27), channel_id=1, source_target_pairs={{0,24},{1,25},{2,26},{3,27},{4,28},{5,29},{6,30},{7,31},{8,16},{9,... | collective-permute-start | bytes 73736 | tf_op jit(solution)/shard_map/ppermute | solution.py:43
  33.8 4.8 %collective-permute-start.9 = (f32[96,128]{1,0:T(8,128)S(1)}, f32[96,128]{1,0:T(8,128)S(1)}, u32[]{:S(2)}, u32[]{:S(2)}) collective-permute-start(f32[96,128]{1,0:T(8,128)S(1)} %pad_maximum_fusion.6), channel_id=1, source_target_pairs={{0,8},{1,17},{2,10},{3,19},{4,12},{5,21},{6,14},{7,23},{8,0},{9,25... | collective-permute-start | bytes 147464 | tf_op jit(solution)/shard_map/ppermute | solution.py:43
  38.6 5.2 %collective-permute-start.12 = (f32[192,128]{1,0:T(8,128)S(1)}, f32[192,128]{1,0:T(8,128)S(1)}, u32[]{:S(2)}, u32[]{:S(2)}) collective-permute-start(f32[192,128]{1,0:T(8,128)S(1)} %get-tuple-element.68), channel_id=1, source_target_pairs={{0,2},{1,3},{2,0},{3,1},{4,6},{5,7},{6,4},{7,5},{8,10},{9,11},{10,... | collective-permute-start | bytes 294920 | tf_op jit(solution)/shard_map/ppermute | solution.py:43
  40.3 6.5 %collective-permute-start.13 = (f32[192,128]{1,0:T(8,128)S(1)}, f32[192,128]{1,0:T(8,128)S(1)}, u32[]{:S(2)}, u32[]{:S(2)}) collective-permute-start(f32[192,128]{1,0:T(8,128)S(1)} %get-tuple-element.68), channel_id=1, source_target_pairs={{0,4},{1,5},{2,6},{3,7},{4,0},{5,1},{6,2},{7,3},{8,12},{9,13},{10,... | collective-permute-start | bytes 294920 | tf_op jit(solution)/shard_map/ppermute | solution.py:43
  42.5 5.5 %collective-permute-start.14 = (f32[192,128]{1,0:T(8,128)S(1)}, f32[192,128]{1,0:T(8,128)S(1)}, u32[]{:S(2)}, u32[]{:S(2)}) collective-permute-start(f32[192,128]{1,0:T(8,128)S(1)} %get-tuple-element.68), channel_id=1, source_target_pairs={{0,6},{1,7},{2,4},{3,5},{4,2},{5,3},{6,0},{7,1},{8,14},{9,15},{10,... | collective-permute-start | bytes 294920 | tf_op jit(solution)/shard_map/ppermute | solution.py:43
  53.8 2.1 %collective-permute-start.16 = (f32[48,128]{1,0:T(8,128)S(1)}, f32[48,128]{1,0:T(8,128)S(1)}, u32[]{:S(2)}, u32[]{:S(2)}) collective-permute-start(f32[48,128]{1,0:T(8,128)S(1)} %get-tuple-element.34), channel_id=1, source_target_pairs={{0,1},{1,0},{2,3},{3,2},{4,5},{5,4},{6,7},{7,6},{8,9},{9,8},{10,11... | collective-permute-start | bytes 73736 | tf_op jit(solution)/shard_map/ppermute | solution.py:43
  54.0 6.7 %collective-permute-start.18 = (f32[48,128]{1,0:T(8,128)S(1)}, f32[48,128]{1,0:T(8,128)S(1)}, u32[]{:S(2)}, u32[]{:S(2)}) collective-permute-start(f32[48,128]{1,0:T(8,128)S(1)} %get-tuple-element.34), channel_id=1, source_target_pairs={{0,24},{1,25},{2,26},{3,27},{4,28},{5,29},{6,30},{7,31},{8,16},{9,... | collective-permute-start | bytes 73736 | tf_op jit(solution)/shard_map/ppermute | solution.py:43
  55.9 4.8 %collective-permute-start.17 = (f32[96,128]{1,0:T(8,128)S(1)}, f32[96,128]{1,0:T(8,128)S(1)}, u32[]{:S(2)}, u32[]{:S(2)}) collective-permute-start(f32[96,128]{1,0:T(8,128)S(1)} %pad_maximum_fusion.7), channel_id=1, source_target_pairs={{0,8},{1,17},{2,10},{3,19},{4,12},{5,21},{6,14},{7,23},{8,0},{9,25... | collective-permute-start | bytes 147464 | tf_op jit(solution)/shard_map/ppermute | solution.py:43
  60.7 5.1 %collective-permute-start.20 = (f32[192,128]{1,0:T(8,128)S(1)}, f32[192,128]{1,0:T(8,128)S(1)}, u32[]{:S(2)}, u32[]{:S(2)}) collective-permute-start(f32[192,128]{1,0:T(8,128)S(1)} %get-tuple-element.64), channel_id=1, source_target_pairs={{0,2},{1,3},{2,0},{3,1},{4,6},{5,7},{6,4},{7,5},{8,10},{9,11},{10,... | collective-permute-start | bytes 294920 | tf_op jit(solution)/shard_map/ppermute | solution.py:43
  63.0 5.8 %collective-permute-start.21 = (f32[192,128]{1,0:T(8,128)S(1)}, f32[192,128]{1,0:T(8,128)S(1)}, u32[]{:S(2)}, u32[]{:S(2)}) collective-permute-start(f32[192,128]{1,0:T(8,128)S(1)} %get-tuple-element.64), channel_id=1, source_target_pairs={{0,4},{1,5},{2,6},{3,7},{4,0},{5,1},{6,2},{7,3},{8,12},{9,13},{10,... | collective-permute-start | bytes 294920 | tf_op jit(solution)/shard_map/ppermute | solution.py:43
  64.2 5.5 %collective-permute-start.22 = (f32[192,128]{1,0:T(8,128)S(1)}, f32[192,128]{1,0:T(8,128)S(1)}, u32[]{:S(2)}, u32[]{:S(2)}) collective-permute-start(f32[192,128]{1,0:T(8,128)S(1)} %get-tuple-element.64), channel_id=1, source_target_pairs={{0,6},{1,7},{2,4},{3,5},{4,2},{5,3},{6,0},{7,1},{8,14},{9,15},{10,... | collective-permute-start | bytes 294920 | tf_op jit(solution)/shard_map/ppermute | solution.py:43
  75.6 3.4 %collective-permute-start.24 = (f32[48,128]{1,0:T(8,128)S(1)}, f32[48,128]{1,0:T(8,128)S(1)}, u32[]{:S(2)}, u32[]{:S(2)}) collective-permute-start(f32[48,128]{1,0:T(8,128)S(1)} %get-tuple-element.41), channel_id=1, source_target_pairs={{0,1},{1,0},{2,3},{3,2},{4,5},{5,4},{6,7},{7,6},{8,9},{9,8},{10,11... | collective-permute-start | bytes 73736 | tf_op jit(solution)/shard_map/ppermute | solution.py:43
  75.8 7.6 %collective-permute-start.26 = (f32[48,128]{1,0:T(8,128)S(1)}, f32[48,128]{1,0:T(8,128)S(1)}, u32[]{:S(2)}, u32[]{:S(2)}) collective-permute-start(f32[48,128]{1,0:T(8,128)S(1)} %get-tuple-element.41), channel_id=1, source_target_pairs={{0,24},{1,25},{2,26},{3,27},{4,28},{5,29},{6,30},{7,31},{8,16},{9,... | collective-permute-start | bytes 73736 | tf_op jit(solution)/shard_map/ppermute | solution.py:43
  79.0 4.4 %collective-permute-start.25 = (f32[96,128]{1,0:T(8,128)S(1)}, f32[96,128]{1,0:T(8,128)S(1)}, u32[]{:S(2)}, u32[]{:S(2)}) collective-permute-start(f32[96,128]{1,0:T(8,128)S(1)} %pad_maximum_fusion.8), channel_id=1, source_target_pairs={{0,8},{1,17},{2,10},{3,19},{4,12},{5,21},{6,14},{7,23},{8,0},{9,25... | collective-permute-start | bytes 147464 | tf_op jit(solution)/shard_map/ppermute | solution.py:43
  83.5 5.8 %collective-permute-start.28 = (f32[192,128]{1,0:T(8,128)S(1)}, f32[192,128]{1,0:T(8,128)S(1)}, u32[]{:S(2)}, u32[]{:S(2)}) collective-permute-start(f32[192,128]{1,0:T(8,128)S(1)} %get-tuple-element.60), channel_id=1, source_target_pairs={{0,2},{1,3},{2,0},{3,1},{4,6},{5,7},{6,4},{7,5},{8,10},{9,11},{10,... | collective-permute-start | bytes 294920 | tf_op jit(solution)/shard_map/ppermute | solution.py:43
  84.4 7.7 %collective-permute-start.29 = (f32[192,128]{1,0:T(8,128)S(1)}, f32[192,128]{1,0:T(8,128)S(1)}, u32[]{:S(2)}, u32[]{:S(2)}) collective-permute-start(f32[192,128]{1,0:T(8,128)S(1)} %get-tuple-element.60), channel_id=1, source_target_pairs={{0,4},{1,5},{2,6},{3,7},{4,0},{5,1},{6,2},{7,3},{8,12},{9,13},{10,... | collective-permute-start | bytes 294920 | tf_op jit(solution)/shard_map/ppermute | solution.py:43
  87.9 5.5 %collective-permute-start.30 = (f32[192,128]{1,0:T(8,128)S(1)}, f32[192,128]{1,0:T(8,128)S(1)}, u32[]{:S(2)}, u32[]{:S(2)}) collective-permute-start(f32[192,128]{1,0:T(8,128)S(1)} %get-tuple-element.60), channel_id=1, source_target_pairs={{0,6},{1,7},{2,4},{3,5},{4,2},{5,3},{6,0},{7,1},{8,14},{9,15},{10,... | collective-permute-start | bytes 294920 | tf_op jit(solution)/shard_map/ppermute | solution.py:43
  (10 other events, 19.4 us)

commit v6 on v5

--- a/solution.py
+++ b/solution.py
@@ -15,6 +15,7 @@
 
 LANES = 128
 LIST_ROWS = 8
+SUM_ROWS = 16
 STEP = 16
 LEAD = 2
 LAG = 6
@@ -157,7 +158,8 @@
         tile = points[pl.ds(dummy - (word & BASE_MASK), 8, stride=blocks), :]
         tile = jnp.where(place < 4, tile, jnp.where(place == 4, 1.0, 0.0))
         high, mid, low = split3(tile)
-        return jnp.concatenate([high, mid, low, high, mid, high], 0).astype(jnp.bfloat16)
+        stack = jnp.concatenate([high, mid, low, high, mid, high], 0).astype(jnp.bfloat16)
+        return stack, jnp.concatenate([high, mid + pltpu.roll(low, 4, 0)], 0).astype(jnp.bfloat16)
 
     def word(unit, n):
         at = 2 * unit + n + LANES
@@ -168,7 +170,7 @@
 
     def fetch(unit):
         rights = [right_tile(word(unit, n)) for n in range(2)]
-        return jnp.concatenate([r.T for r in rights], 0), jnp.concatenate([r[:32] for r in rights], 1)
+        return jnp.concatenate([r.T for r, _ in rights], 0), jnp.concatenate([r for _, r in rights], 1)
 
     def weigh(unit, turned):
         w = jnp.maximum(matmul(turned, lefts[block_of(unit)]), 0.0)
@@ -177,7 +179,7 @@
 
     def add(unit, right, w):
         part = matmul(right, w)
-        at = pl.ds(pl.multiple_of(block_of(unit) * 32, 32), 32)
+        at = pl.ds(pl.multiple_of(block_of(unit) * SUM_ROWS, SUM_ROWS), SUM_ROWS)
         sums[at, :] = sums[at, :] + (part[:, :LANES] + part[:, LANES:])
 
     for k in range(LEAD):
@@ -231,14 +233,14 @@
 
 def forces_of(blocks, points, all_sums):
     def entry(n):
-        at = pl.ds(n, blocks, stride=32)
+        at = pl.ds(n, blocks, stride=SUM_ROWS)
         return sum(sums[at, :] for sums in all_sums)
 
     total = entry(4)
     forces = []
     for c in range(3):
         y = points[pl.ds(c * blocks, blocks), :]
-        forces.append((2.0 * STIFFNESS) * (y * total - (entry(c) + entry(8 + c) + entry(16 + c))))
+        forces.append((2.0 * STIFFNESS) * (y * total - (entry(c) + entry(8 + c) + entry(12 + c))))
     return forces
 
 
@@ -405,12 +407,12 @@
     smem = pl.BlockSpec(memory_space=pltpu.SMEM)
     points = pltpu.VMEM(((devices + 3) * 4 * blocks, LANES), jnp.float32)
     lefts = pltpu.VMEM((blocks, 48, LANES), jnp.bfloat16)
-    sums = pltpu.VMEM((blocks * 32, LANES), jnp.float32)
+    sums = pltpu.VMEM((blocks * SUM_ROWS, LANES), jnp.float32)
     kept = [
         pltpu.VMEM((LEAD, 2 * LANES, 48), jnp.bfloat16),
-        pltpu.VMEM((LEAD, 32, 2 * LANES), jnp.bfloat16),
+        pltpu.VMEM((LEAD, SUM_ROWS, 2 * LANES), jnp.bfloat16),
         pltpu.VMEM((LAG, 2 * LANES, 2 * LANES), jnp.bfloat16),
-        pltpu.VMEM((LAG, 32, 2 * LANES), jnp.bfloat16),
+        pltpu.VMEM((LAG, SUM_ROWS, 2 * LANES), jnp.bfloat16),
     ]
     listed = [pltpu.SMEM((unit_rows, LANES), jnp.int32), pltpu.SemaphoreType.DMA]
     params = pltpu.CompilerParams(vmem_limit_bytes=48 * 1024 * 1024)
@@ -443,7 +445,7 @@
         parts = gather_last(near, devices)
         near_sums = pl.pallas_call(
             functools.partial(near_kernel, size),
-            out_shape=jax.ShapeDtypeStruct((blocks * 32, LANES), jnp.float32),
+            out_shape=jax.ShapeDtypeStruct((blocks * SUM_ROWS, LANES), jnp.float32),
             in_specs=[vmem] * 3,
             out_specs=vmem,
             scratch_shapes=listed + [points, lefts] + kept,

time: 100 us -> 99.4 us (level); the launches traced: 99.9 us -> 98.1 us
  starting transfers between devices: 29 us -> 27 us
    ppermute x32, starting transfers between devices: 29 us -> 27 us  [send(): return lax.ppermute(block, AXES, [(d, d ^ mask(d)) for d in range(devices)])]
    pallas_call x3, Pallas kernels: 8.81 us -> 7.47 us  [body(): pl.pallas_call(functools.partial(near_kernel, size), out_shape=jax.ShapeD...]
    pallas_call x3, Pallas kernels: 12.9 us -> 14.3 us  [body(): pl.pallas_call(functools.partial(next_kernel, size, last), out_shape=[who...]
  transfers between devices with their start and end apart: 32 -> 32, of which waited for: 17 -> 18; matrix products, arithmetic and copies ran while one was open for 1% -> 1% of each run, Pallas kernels for 9% -> 8%
where the time goes in v6:
time: 99.4 us; the launch traced here: 98.1 us
  waiting for transfers between devices  37.4 us (38%)
  Pallas kernels  30.7 us (31%)
  starting transfers between devices  27 us (27%)
  between operations  1.85 us (2%)
    ppermute x32, waiting for transfers between devices, send(): return lax.ppermute(block, AXES, [(d, d ^ mask(d)) for d in range(devices)])  37.4 us
    ppermute x32, starting transfers between devices, send(): return lax.ppermute(block, AXES, [(d, d ^ mask(d)) for d in range(devices)])  27 us
    pallas_call x3, Pallas kernels, body(): pl.pallas_call(functools.partial(next_kernel, size, last), out_shape=[who...  14.3 us
    pallas_call x1, Pallas kernels, body(): pl.pallas_call(functools.partial(first_kernel, size, (nrow, ncol, span)),...  7.55 us
    pallas_call x3, Pallas kernels, body(): pl.pallas_call(functools.partial(near_kernel, size), out_shape=jax.ShapeD...  7.47 us
  transfers between devices with their start and end apart: 32, of which 18 were waited for; matrix products, arithmetic and copies ran while one was open for 1% of the time, Pallas kernels for 8%

profile of v6, /device:TPU:0, one launch (start us, length us, event | category | flops | bytes accessed | tf_op | source)
XLA Modules:
  0.0 98.1 jit_solution(16572532963338996392)
XLA Ops:
  3.2 4.7 %collective-permute-start.2 = (f32[56,128]{1,0:T(8,128)}, f32[56,128]{1,0:T(8,128)S(1)}, u32[]{:S(2)}, u32[]{:S(2)}) collective-permute-start(f32[56,128]{1,0:T(8,128)} %get-tuple-element.25), channel_id=1, source_target_pairs={{0,24},{1,25},{2,26},{3,27},{4,28},{5,29},{6,30},{7,31},{8,16},{9,... | collective-permute-start | bytes 86024 | tf_op jit(solution)/shard_map/ppermute | solution.py:44
  8.6 4.8 %collective-permute-done.1 = f32[112,128]{1,0:T(8,128)S(1)} collective-permute-done((f32[112,128]{1,0:T(8,128)S(1)}, f32[112,128]{1,0:T(8,128)S(1)}, u32[]{:S(2)}, u32[]{:S(2)}) %collective-permute-start.1) | collective-permute-done | bytes 57376 | tf_op jit(solution)/shard_map/ppermute | solution.py:44
  13.4 1.6 %collective-permute-start.4 = (f32[224,128]{1,0:T(8,128)S(1)}, f32[224,128]{1,0:T(8,128)S(1)}, u32[]{:S(2)}, u32[]{:S(2)}) collective-permute-start(f32[224,128]{1,0:T(8,128)S(1)} %get-tuple-element.56), channel_id=1, source_target_pairs={{0,2},{1,3},{2,0},{3,1},{4,6},{5,7},{6,4},{7,5},{8,10},{9,11},{10,... | collective-permute-start | bytes 344072 | tf_op jit(solution)/shard_map/ppermute | solution.py:44
  18.3 2.1 %collective-permute-done.5 = f32[224,128]{1,0:T(8,128)S(1)} collective-permute-done((f32[224,128]{1,0:T(8,128)S(1)}, f32[224,128]{1,0:T(8,128)S(1)}, u32[]{:S(2)}, u32[]{:S(2)}) %collective-permute-start.5) | collective-permute-done | bytes 114720 | tf_op jit(solution)/shard_map/ppermute | solution.py:44
  20.4 1.8 %collective-permute-done.6 = f32[224,128]{1,0:T(8,128)S(1)} collective-permute-done((f32[224,128]{1,0:T(8,128)S(1)}, f32[224,128]{1,0:T(8,128)S(1)}, u32[]{:S(2)}, u32[]{:S(2)}) %collective-permute-start.6) | collective-permute-done | bytes 114720 | tf_op jit(solution)/shard_map/ppermute | solution.py:44
  22.4 1.6 %collective-permute-done.7 = f32[672,128]{1,0:T(8,128)S(1)} collective-permute-done((f32[672,128]{1,0:T(8,128)S(1)}, f32[672,128]{1,0:T(8,128)S(1)}, u32[]{:S(2)}, u32[]{:S(2)}) %collective-permute-start.7) | collective-permute-done | bytes 344096 | tf_op jit(solution)/shard_map/ppermute | solution.py:44
  24.0 7.5 %first_forces.1 = (f32[48,128]{1,0:T(8,128)S(1)}, f32[48,128]{1,0:T(8,128)S(1)}, s32[32,128]{1,0:T(8,128)S(1)}) custom-call(f32[1792,128]{1,0:T(8,128)S(1)} %constant_dynamic-update-slice_fusion.3.gathered, f32[48,128]{1,0:T(8,128)S(1)} %copy-done), custom_call_target="tpu_custom_call" | custom-call | flops 4000000000 | bytes 1048576 | tf_op jit(solution)/shard_map/first_forces/pallas_call | solution.py:432
  33.5 4.1 %collective-permute-done.9 = f32[96,128]{1,0:T(8,128)S(1)} collective-permute-done((f32[96,128]{1,0:T(8,128)S(1)}, f32[96,128]{1,0:T(8,128)S(1)}, u32[]{:S(2)}, u32[]{:S(2)}) %collective-permute-start.9) | collective-permute-done | bytes 49184 | tf_op jit(solution)/shard_map/ppermute | solution.py:44
  39.2 3.0 %collective-permute-start.13 = (f32[192,128]{1,0:T(8,128)S(1)}, f32[192,128]{1,0:T(8,128)S(1)}, u32[]{:S(2)}, u32[]{:S(2)}) collective-permute-start(f32[192,128]{1,0:T(8,128)S(1)} %get-tuple-element.68), channel_id=1, source_target_pairs={{0,4},{1,5},{2,6},{3,7},{4,0},{5,1},{6,2},{7,3},{8,12},{9,13},{10,... | collective-permute-start | bytes 294920 | tf_op jit(solution)/shard_map/ppermute | solution.py:44
  43.5 2.5 %near_forces.3.near_sums = f32[256,128]{1,0:T(8,128)S(1)} custom-call(f32[384,128]{1,0:T(8,128)S(1)} %constant_dynamic-update-slice_fusion.12.near, f32[192,128]{1,0:T(8,128)S(1)} %collective-permute-done.12.part, s32[32,128]{1,0:T(8,128)S(1)} %get-tuple-element.28.words), custom_call_target="tpu_custom_call" | custom-call | flops 1000000000 | bytes 1048576 | tf_op jit(solution)/shard_map/near_forces/pallas_call | solution.py:446
  46.0 1.7 %collective-permute-done.14 = f32[192,128]{1,0:T(8,128)S(1)} collective-permute-done((f32[192,128]{1,0:T(8,128)S(1)}, f32[192,128]{1,0:T(8,128)S(1)}, u32[]{:S(2)}, u32[]{:S(2)}) %collective-permute-start.14) | collective-permute-done | bytes 98336 | tf_op jit(solution)/shard_map/ppermute | solution.py:44
  47.8 1.6 %collective-permute-done.15.far = f32[576,128]{1,0:T(8,128)S(1)} collective-permute-done((f32[576,128]{1,0:T(8,128)S(1)}, f32[576,128]{1,0:T(8,128)S(1)}, u32[]{:S(2)}, u32[]{:S(2)}) %collective-permute-start.15) | collective-permute-done | bytes 294944 | tf_op jit(solution)/shard_map/ppermute | solution.py:44
  49.4 4.5 %next_forces.2 = (f32[48,128]{1,0:T(8,128)S(1)}, f32[48,128]{1,0:T(8,128)S(1)}, f32[48,128]{1,0:T(8,128)S(1)}) custom-call(f32[384,128]{1,0:T(8,128)S(1)} %constant_dynamic-update-slice_fusion.12.near, f32[576,128]{1,0:T(8,128)S(1)} %constant_dynamic-update-slice_fusion.20.middle, f32[576,128]{1,0:T(8,128)S(1)} %collective-permute-done.15.far, ...), custom_call_target="tpu_custom_call" | custom-call | flops 3000000000 | bytes 1048576 | tf_op jit(solution)/shard_map/next_forces/pallas_call | solution.py:457
  55.1 4.7 %collective-permute-done.17 = f32[96,128]{1,0:T(8,128)S(1)} collective-permute-done((f32[96,128]{1,0:T(8,128)S(1)}, f32[96,128]{1,0:T(8,128)S(1)}, u32[]{:S(2)}, u32[]{:S(2)}) %collective-permute-start.17) | collective-permute-done | bytes 49184 | tf_op jit(solution)/shard_map/ppermute | solution.py:44
  60.3 2.9 %collective-permute-start.21 = (f32[192,128]{1,0:T(8,128)S(1)}, f32[192,128]{1,0:T(8,128)S(1)}, u32[]{:S(2)}, u32[]{:S(2)}) collective-permute-start(f32[192,128]{1,0:T(8,128)S(1)} %get-tuple-element.64), channel_id=1, source_target_pairs={{0,4},{1,5},{2,6},{3,7},{4,0},{5,1},{6,2},{7,3},{8,12},{9,13},{10,... | collective-permute-start | bytes 294920 | tf_op jit(solution)/shard_map/ppermute | solution.py:44
  65.3 2.5 %near_forces.4.near_sums = f32[256,128]{1,0:T(8,128)S(1)} custom-call(f32[384,128]{1,0:T(8,128)S(1)} %constant_dynamic-update-slice_fusion.23.near, f32[192,128]{1,0:T(8,128)S(1)} %collective-permute-done.20.part, s32[32,128]{1,0:T(8,128)S(1)} %get-tuple-element.28.words), custom_call_target="tpu_custom_call" | custom-call | flops 1000000000 | bytes 1048576 | tf_op jit(solution)/shard_map/near_forces/pallas_call | solution.py:446
  68.9 1.6 %collective-permute-done.23.far = f32[576,128]{1,0:T(8,128)S(1)} collective-permute-done((f32[576,128]{1,0:T(8,128)S(1)}, f32[576,128]{1,0:T(8,128)S(1)}, u32[]{:S(2)}, u32[]{:S(2)}) %collective-permute-start.23) | collective-permute-done | bytes 294944 | tf_op jit(solution)/shard_map/ppermute | solution.py:44
  70.4 4.7 %next_forces.3 = (f32[48,128]{1,0:T(8,128)S(1)}, f32[48,128]{1,0:T(8,128)S(1)}, f32[48,128]{1,0:T(8,128)S(1)}) custom-call(f32[384,128]{1,0:T(8,128)S(1)} %constant_dynamic-update-slice_fusion.23.near, f32[576,128]{1,0:T(8,128)S(1)} %constant_dynamic-update-slice_fusion.31.middle, f32[576,128]{1,0:T(8,128)S(1)} %collective-permute-done.23.far, ...), custom_call_target="tpu_custom_call" | custom-call | flops 3000000000 | bytes 1048576 | tf_op jit(solution)/shard_map/next_forces/pallas_call | solution.py:457
  75.2 2.0 %collective-permute-start.26 = (f32[48,128]{1,0:T(8,128)S(1)}, f32[48,128]{1,0:T(8,128)S(1)}, u32[]{:S(2)}, u32[]{:S(2)}) collective-permute-start(f32[48,128]{1,0:T(8,128)S(1)} %get-tuple-element.41), channel_id=1, source_target_pairs={{0,24},{1,25},{2,26},{3,27},{4,28},{5,29},{6,30},{7,31},{8,16},{9,... | collective-permute-start | bytes 73736 | tf_op jit(solution)/shard_map/ppermute | solution.py:44
  77.3 4.7 %collective-permute-done.25 = f32[96,128]{1,0:T(8,128)S(1)} collective-permute-done((f32[96,128]{1,0:T(8,128)S(1)}, f32[96,128]{1,0:T(8,128)S(1)}, u32[]{:S(2)}, u32[]{:S(2)}) %collective-permute-start.25) | collective-permute-done | bytes 49184 | tf_op jit(solution)/shard_map/ppermute | solution.py:44
  82.3 3.3 %collective-permute-start.29 = (f32[192,128]{1,0:T(8,128)S(1)}, f32[192,128]{1,0:T(8,128)S(1)}, u32[]{:S(2)}, u32[]{:S(2)}) collective-permute-start(f32[192,128]{1,0:T(8,128)S(1)} %get-tuple-element.60), channel_id=1, source_target_pairs={{0,4},{1,5},{2,6},{3,7},{4,0},{5,1},{6,2},{7,3},{8,12},{9,13},{10,... | collective-permute-start | bytes 294920 | tf_op jit(solution)/shard_map/ppermute | solution.py:44
  87.9 2.5 %near_forces.5.near_sums = f32[256,128]{1,0:T(8,128)S(1)} custom-call(f32[384,128]{1,0:T(8,128)S(1)} %constant_dynamic-update-slice_fusion.34.near, f32[192,128]{1,0:T(8,128)S(1)} %collective-permute-done.28.part, s32[32,128]{1,0:T(8,128)S(1)} %get-tuple-element.28.words), custom_call_target="tpu_custom_call" | custom-call | flops 1000000000 | bytes 1048576 | tf_op jit(solution)/shard_map/near_forces/pallas_call | solution.py:446
  91.3 1.6 %collective-permute-done.31.far = f32[576,128]{1,0:T(8,128)S(1)} collective-permute-done((f32[576,128]{1,0:T(8,128)S(1)}, f32[576,128]{1,0:T(8,128)S(1)}, u32[]{:S(2)}, u32[]{:S(2)}) %collective-permute-start.31) | collective-permute-done | bytes 294944 | tf_op jit(solution)/shard_map/ppermute | solution.py:44
  92.9 5.1 %last_forces.1 = (f32[3,2048]{1,0:T(4,128)}, f32[3,2048]{1,0:T(4,128)}) custom-call(f32[384,128]{1,0:T(8,128)S(1)} %constant_dynamic-update-slice_fusion.34.near, f32[576,128]{1,0:T(8,128)S(1)} %constant_dynamic-update-slice_fusion.42.middle, f32[576,128]{1,0:T(8,128)S(1)} %collective-permute-done.31.far, f32[256,128]{1,0:T(8,128)S(1)} %near_forces.5.near_sums, ...), custom_call_target="tpu_custom_call" | custom-call | flops 3000000000 | bytes 1048576 | tf_op jit(solution)/shard_map/last_forces/pallas_call | solution.py:457
  (94 shorter events, 19.5 us)
Async XLA Ops:
  2.7 5.1 %collective-permute-start = (f32[56,128]{1,0:T(8,128)}, f32[56,128]{1,0:T(8,128)S(1)}, u32[]{:S(2)}, u32[]{:S(2)}) collective-permute-start(f32[56,128]{1,0:T(8,128)} %get-tuple-element.25), channel_id=1, source_target_pairs={{0,1},{1,0},{2,3},{3,2},{4,5},{5,4},{6,7},{7,6},{8,9},{9,8},{10,11... | collective-permute-start | bytes 86024 | tf_op jit(solution)/shard_map/ppermute | solution.py:44
  3.2 10.3 %collective-permute-start.2 = (f32[56,128]{1,0:T(8,128)}, f32[56,128]{1,0:T(8,128)S(1)}, u32[]{:S(2)}, u32[]{:S(2)}) collective-permute-start(f32[56,128]{1,0:T(8,128)} %get-tuple-element.25), channel_id=1, source_target_pairs={{0,24},{1,25},{2,26},{3,27},{4,28},{5,29},{6,30},{7,31},{8,16},{9,... | collective-permute-start | bytes 86024 | tf_op jit(solution)/shard_map/ppermute | solution.py:44
  8.6 4.8 %collective-permute-start.1 = (f32[112,128]{1,0:T(8,128)S(1)}, f32[112,128]{1,0:T(8,128)S(1)}, u32[]{:S(2)}, u32[]{:S(2)}) collective-permute-start(f32[112,128]{1,0:T(8,128)S(1)} %pad_maximum_fusion.5), channel_id=1, source_target_pairs={{0,8},{1,17},{2,10},{3,19},{4,12},{5,21},{6,14},{7,23},{8,0},{9,25... | collective-permute-start | bytes 172040 | tf_op jit(solution)/shard_map/ppermute | solution.py:44
  13.4 4.9 %collective-permute-start.4 = (f32[224,128]{1,0:T(8,128)S(1)}, f32[224,128]{1,0:T(8,128)S(1)}, u32[]{:S(2)}, u32[]{:S(2)}) collective-permute-start(f32[224,128]{1,0:T(8,128)S(1)} %get-tuple-element.56), channel_id=1, source_target_pairs={{0,2},{1,3},{2,0},{3,1},{4,6},{5,7},{6,4},{7,5},{8,10},{9,11},{10,... | collective-permute-start | bytes 344072 | tf_op jit(solution)/shard_map/ppermute | solution.py:44
  15.0 5.4 %collective-permute-start.5 = (f32[224,128]{1,0:T(8,128)S(1)}, f32[224,128]{1,0:T(8,128)S(1)}, u32[]{:S(2)}, u32[]{:S(2)}) collective-permute-start(f32[224,128]{1,0:T(8,128)S(1)} %get-tuple-element.56), channel_id=1, source_target_pairs={{0,4},{1,5},{2,6},{3,7},{4,0},{5,1},{6,2},{7,3},{8,12},{9,13},{10,... | collective-permute-start | bytes 344072 | tf_op jit(solution)/shard_map/ppermute | solution.py:44
  16.5 5.7 %collective-permute-start.6 = (f32[224,128]{1,0:T(8,128)S(1)}, f32[224,128]{1,0:T(8,128)S(1)}, u32[]{:S(2)}, u32[]{:S(2)}) collective-permute-start(f32[224,128]{1,0:T(8,128)S(1)} %get-tuple-element.56), channel_id=1, source_target_pairs={{0,6},{1,7},{2,4},{3,5},{4,2},{5,3},{6,0},{7,1},{8,14},{9,15},{10,... | collective-permute-start | bytes 344072 | tf_op jit(solution)/shard_map/ppermute | solution.py:44
  22.2 1.7 %collective-permute-start.7 = (f32[672,128]{1,0:T(8,128)S(1)}, f32[672,128]{1,0:T(8,128)S(1)}, u32[]{:S(2)}, u32[]{:S(2)}) collective-permute-start(f32[672,128]{1,0:T(8,128)S(1)} %pad_maximum_fusion), channel_id=1, source_target_pairs={{0,1},{1,0},{2,3},{3,2},{4,5},{5,4},{6,7},{7,6},{8,9},{9,8},{10,11... | collective-permute-start | bytes 1032200 | tf_op jit(solution)/shard_map/ppermute | solution.py:44
  31.8 5.9 %collective-permute-start.10 = (f32[48,128]{1,0:T(8,128)S(1)}, f32[48,128]{1,0:T(8,128)S(1)}, u32[]{:S(2)}, u32[]{:S(2)}) collective-permute-start(f32[48,128]{1,0:T(8,128)S(1)} %get-tuple-element.27), channel_id=1, source_target_pairs={{0,24},{1,25},{2,26},{3,27},{4,28},{5,29},{6,30},{7,31},{8,16},{9,... | collective-permute-start | bytes 73736 | tf_op jit(solution)/shard_map/ppermute | solution.py:44
  33.1 4.5 %collective-permute-start.9 = (f32[96,128]{1,0:T(8,128)S(1)}, f32[96,128]{1,0:T(8,128)S(1)}, u32[]{:S(2)}, u32[]{:S(2)}) collective-permute-start(f32[96,128]{1,0:T(8,128)S(1)} %pad_maximum_fusion.6), channel_id=1, source_target_pairs={{0,8},{1,17},{2,10},{3,19},{4,12},{5,21},{6,14},{7,23},{8,0},{9,25... | collective-permute-start | bytes 147464 | tf_op jit(solution)/shard_map/ppermute | solution.py:44
  37.7 5.8 %collective-permute-start.12 = (f32[192,128]{1,0:T(8,128)S(1)}, f32[192,128]{1,0:T(8,128)S(1)}, u32[]{:S(2)}, u32[]{:S(2)}) collective-permute-start(f32[192,128]{1,0:T(8,128)S(1)} %get-tuple-element.68), channel_id=1, source_target_pairs={{0,2},{1,3},{2,0},{3,1},{4,6},{5,7},{6,4},{7,5},{8,10},{9,11},{10,... | collective-permute-start | bytes 294920 | tf_op jit(solution)/shard_map/ppermute | solution.py:44
  39.2 6.8 %collective-permute-start.13 = (f32[192,128]{1,0:T(8,128)S(1)}, f32[192,128]{1,0:T(8,128)S(1)}, u32[]{:S(2)}, u32[]{:S(2)}) collective-permute-start(f32[192,128]{1,0:T(8,128)S(1)} %get-tuple-element.68), channel_id=1, source_target_pairs={{0,4},{1,5},{2,6},{3,7},{4,0},{5,1},{6,2},{7,3},{8,12},{9,13},{10,... | collective-permute-start | bytes 294920 | tf_op jit(solution)/shard_map/ppermute | solution.py:44
  42.1 5.5 %collective-permute-start.14 = (f32[192,128]{1,0:T(8,128)S(1)}, f32[192,128]{1,0:T(8,128)S(1)}, u32[]{:S(2)}, u32[]{:S(2)}) collective-permute-start(f32[192,128]{1,0:T(8,128)S(1)} %get-tuple-element.68), channel_id=1, source_target_pairs={{0,6},{1,7},{2,4},{3,5},{4,2},{5,3},{6,0},{7,1},{8,14},{9,15},{10,... | collective-permute-start | bytes 294920 | tf_op jit(solution)/shard_map/ppermute | solution.py:44
  47.7 1.6 %collective-permute-start.15 = (f32[576,128]{1,0:T(8,128)S(1)}, f32[576,128]{1,0:T(8,128)S(1)}, u32[]{:S(2)}, u32[]{:S(2)}) collective-permute-start(f32[576,128]{1,0:T(8,128)S(1)} %constant_dynamic-update-slice_fusion.20.middle), channel_id=1, source_target_pairs={{0,1},{1,0},{2,3},{3,2},{4,5},{5,4},{6,7},{7,6},{8,9},{9,8},{10,11... | collective-permute-start | bytes 884744 | tf_op jit(solution)/shard_map/ppermute | solution.py:44
  53.9 6.0 %collective-permute-start.18 = (f32[48,128]{1,0:T(8,128)S(1)}, f32[48,128]{1,0:T(8,128)S(1)}, u32[]{:S(2)}, u32[]{:S(2)}) collective-permute-start(f32[48,128]{1,0:T(8,128)S(1)} %get-tuple-element.34), channel_id=1, source_target_pairs={{0,24},{1,25},{2,26},{3,27},{4,28},{5,29},{6,30},{7,31},{8,16},{9,... | collective-permute-start | bytes 73736 | tf_op jit(solution)/shard_map/ppermute | solution.py:44
  55.1 4.8 %collective-permute-start.17 = (f32[96,128]{1,0:T(8,128)S(1)}, f32[96,128]{1,0:T(8,128)S(1)}, u32[]{:S(2)}, u32[]{:S(2)}) collective-permute-start(f32[96,128]{1,0:T(8,128)S(1)} %pad_maximum_fusion.7), channel_id=1, source_target_pairs={{0,8},{1,17},{2,10},{3,19},{4,12},{5,21},{6,14},{7,23},{8,0},{9,25... | collective-permute-start | bytes 147464 | tf_op jit(solution)/shard_map/ppermute | solution.py:44
  59.9 5.4 %collective-permute-start.20 = (f32[192,128]{1,0:T(8,128)S(1)}, f32[192,128]{1,0:T(8,128)S(1)}, u32[]{:S(2)}, u32[]{:S(2)}) collective-permute-start(f32[192,128]{1,0:T(8,128)S(1)} %get-tuple-element.64), channel_id=1, source_target_pairs={{0,2},{1,3},{2,0},{3,1},{4,6},{5,7},{6,4},{7,5},{8,10},{9,11},{10,... | collective-permute-start | bytes 294920 | tf_op jit(solution)/shard_map/ppermute | solution.py:44
  60.3 7.5 %collective-permute-start.21 = (f32[192,128]{1,0:T(8,128)S(1)}, f32[192,128]{1,0:T(8,128)S(1)}, u32[]{:S(2)}, u32[]{:S(2)}) collective-permute-start(f32[192,128]{1,0:T(8,128)S(1)} %get-tuple-element.64), channel_id=1, source_target_pairs={{0,4},{1,5},{2,6},{3,7},{4,0},{5,1},{6,2},{7,3},{8,12},{9,13},{10,... | collective-permute-start | bytes 294920 | tf_op jit(solution)/shard_map/ppermute | solution.py:44
  63.2 5.6 %collective-permute-start.22 = (f32[192,128]{1,0:T(8,128)S(1)}, f32[192,128]{1,0:T(8,128)S(1)}, u32[]{:S(2)}, u32[]{:S(2)}) collective-permute-start(f32[192,128]{1,0:T(8,128)S(1)} %get-tuple-element.64), channel_id=1, source_target_pairs={{0,6},{1,7},{2,4},{3,5},{4,2},{5,3},{6,0},{7,1},{8,14},{9,15},{10,... | collective-permute-start | bytes 294920 | tf_op jit(solution)/shard_map/ppermute | solution.py:44
  75.1 2.1 %collective-permute-start.24 = (f32[48,128]{1,0:T(8,128)S(1)}, f32[48,128]{1,0:T(8,128)S(1)}, u32[]{:S(2)}, u32[]{:S(2)}) collective-permute-start(f32[48,128]{1,0:T(8,128)S(1)} %get-tuple-element.41), channel_id=1, source_target_pairs={{0,1},{1,0},{2,3},{3,2},{4,5},{5,4},{6,7},{7,6},{8,9},{9,8},{10,11... | collective-permute-start | bytes 73736 | tf_op jit(solution)/shard_map/ppermute | solution.py:44
  75.2 6.8 %collective-permute-start.26 = (f32[48,128]{1,0:T(8,128)S(1)}, f32[48,128]{1,0:T(8,128)S(1)}, u32[]{:S(2)}, u32[]{:S(2)}) collective-permute-start(f32[48,128]{1,0:T(8,128)S(1)} %get-tuple-element.41), channel_id=1, source_target_pairs={{0,24},{1,25},{2,26},{3,27},{4,28},{5,29},{6,30},{7,31},{8,16},{9,... | collective-permute-start | bytes 73736 | tf_op jit(solution)/shard_map/ppermute | solution.py:44
  77.2 4.8 %collective-permute-start.25 = (f32[96,128]{1,0:T(8,128)S(1)}, f32[96,128]{1,0:T(8,128)S(1)}, u32[]{:S(2)}, u32[]{:S(2)}) collective-permute-start(f32[96,128]{1,0:T(8,128)S(1)} %pad_maximum_fusion.8), channel_id=1, source_target_pairs={{0,8},{1,17},{2,10},{3,19},{4,12},{5,21},{6,14},{7,23},{8,0},{9,25... | collective-permute-start | bytes 147464 | tf_op jit(solution)/shard_map/ppermute | solution.py:44
  82.1 5.8 %collective-permute-start.28 = (f32[192,128]{1,0:T(8,128)S(1)}, f32[192,128]{1,0:T(8,128)S(1)}, u32[]{:S(2)}, u32[]{:S(2)}) collective-permute-start(f32[192,128]{1,0:T(8,128)S(1)} %get-tuple-element.60), channel_id=1, source_target_pairs={{0,2},{1,3},{2,0},{3,1},{4,6},{5,7},{6,4},{7,5},{8,10},{9,11},{10,... | collective-permute-start | bytes 294920 | tf_op jit(solution)/shard_map/ppermute | solution.py:44
  82.3 8.0 %collective-permute-start.29 = (f32[192,128]{1,0:T(8,128)S(1)}, f32[192,128]{1,0:T(8,128)S(1)}, u32[]{:S(2)}, u32[]{:S(2)}) collective-permute-start(f32[192,128]{1,0:T(8,128)S(1)} %get-tuple-element.60), channel_id=1, source_target_pairs={{0,4},{1,5},{2,6},{3,7},{4,0},{5,1},{6,2},{7,3},{8,12},{9,13},{10,... | collective-permute-start | bytes 294920 | tf_op jit(solution)/shard_map/ppermute | solution.py:44
  85.7 5.5 %collective-permute-start.30 = (f32[192,128]{1,0:T(8,128)S(1)}, f32[192,128]{1,0:T(8,128)S(1)}, u32[]{:S(2)}, u32[]{:S(2)}) collective-permute-start(f32[192,128]{1,0:T(8,128)S(1)} %get-tuple-element.60), channel_id=1, source_target_pairs={{0,6},{1,7},{2,4},{3,5},{4,2},{5,3},{6,0},{7,1},{8,14},{9,15},{10,... | collective-permute-start | bytes 294920 | tf_op jit(solution)/shard_map/ppermute | solution.py:44
  (10 other events, 18.8 us)

commit v7 on v6

--- a/solution.py
+++ b/solution.py
@@ -312,12 +312,15 @@
     lane = lax.broadcasted_iota(jnp.int32, (LANES, LANES), 0)
     place = lax.broadcasted_iota(jnp.int32, (rows, LANES), 0)
     found = jnp.zeros((3 * rows, LANES), jnp.float32)
-    for r in range(height):
-        here = high[r : r + 1] == place
-        weights = jnp.concatenate([jnp.where(here, p[r : r + 1], 0.0) for p in pieces], 0)
-        spots = (lane == low[r : r + 1]).astype(jnp.float32)
+    for pair in range(0, height, 2):
+        weights, spots = [], []
+        for r in (pair, pair + 1):
+            here = high[r : r + 1] == place
+            weights.append(jnp.concatenate([jnp.where(here, p[r : r + 1], 0.0) for p in pieces], 0))
+            spots.append((lane == low[r : r + 1]).astype(jnp.float32))
+        weights, spots = jnp.concatenate(weights, 1).astype(ones), jnp.concatenate(spots, 1).astype(ones)
         found = found + lax.dot_general(
-            weights.astype(ones), spots.astype(ones), (((1,), (1,)), ((), ())), preferred_element_type=jnp.float32
+            weights, spots, (((1,), (1,)), ((), ())), preferred_element_type=jnp.float32
         )
     words = found.astype(jnp.int32)
     words = words[:rows] + words[rows : 2 * rows] * 64 + words[2 * rows :] * (BASE_MASK + 1)

time: 99.4 us -> 98.8 us (level)
  waiting for transfers between devices: 37.4 us -> 34 us
  Pallas kernels: 30.7 us -> 32.2 us
  starting transfers between devices: 27 us -> 28 us
    ppermute x32, waiting for transfers between devices: 37.4 us -> 34 us  [send(): return lax.ppermute(block, AXES, [(d, d ^ mask(d)) for d in range(devices)])]
    pallas_call x3, Pallas kernels: 7.47 us -> 8.67 us  [body(): pl.pallas_call(functools.partial(near_kernel, size), out_shape=jax.ShapeD...]
  transfers between devices with their start and end apart: 32 -> 32, of which waited for: 18 -> 17; matrix products, arithmetic and copies ran while one was open for 1% -> 1% of each run, Pallas kernels for 8% -> 9%
where the time goes in v7:
time: 98.8 us; the launch traced here: 97.2 us
  waiting for transfers between devices  34 us (34%)
  Pallas kernels  32.2 us (33%)
  starting transfers between devices  28 us (28%)
  between operations  1.87 us (2%)
    ppermute x32, waiting for transfers between devices, send(): return lax.ppermute(block, AXES, [(d, d ^ mask(d)) for d in range(devices)])  34 us
    ppermute x32, starting transfers between devices, send(): return lax.ppermute(block, AXES, [(d, d ^ mask(d)) for d in range(devices)])  28 us
    pallas_call x3, Pallas kernels, body(): pl.pallas_call(functools.partial(next_kernel, size, last), out_shape=[who...  14.3 us
    pallas_call x3, Pallas kernels, body(): pl.pallas_call(functools.partial(near_kernel, size), out_shape=jax.ShapeD...  8.67 us
    pallas_call x1, Pallas kernels, body(): pl.pallas_call(functools.partial(first_kernel, size, (nrow, ncol, span)),...  7.84 us
  transfers between devices with their start and end apart: 32, of which 17 were waited for; matrix products, arithmetic and copies ran while one was open for 1% of the time, Pallas kernels for 9%

profile of v7, /device:TPU:0, one launch (start us, length us, event | category | flops | bytes accessed | tf_op | source)
XLA Modules:
  0.0 97.2 jit_solution(9260678338464993145)
XLA Ops:
  3.2 4.7 %collective-permute-start.2 = (f32[56,128]{1,0:T(8,128)}, f32[56,128]{1,0:T(8,128)S(1)}, u32[]{:S(2)}, u32[]{:S(2)}) collective-permute-start(f32[56,128]{1,0:T(8,128)} %get-tuple-element.25), channel_id=1, source_target_pairs={{0,24},{1,25},{2,26},{3,27},{4,28},{5,29},{6,30},{7,31},{8,16},{9,... | collective-permute-start | bytes 86024 | tf_op jit(solution)/shard_map/ppermute | solution.py:44
  8.6 4.8 %collective-permute-done.1 = f32[112,128]{1,0:T(8,128)S(1)} collective-permute-done((f32[112,128]{1,0:T(8,128)S(1)}, f32[112,128]{1,0:T(8,128)S(1)}, u32[]{:S(2)}, u32[]{:S(2)}) %collective-permute-start.1) | collective-permute-done | bytes 57376 | tf_op jit(solution)/shard_map/ppermute | solution.py:44
  13.4 1.6 %collective-permute-start.4 = (f32[224,128]{1,0:T(8,128)S(1)}, f32[224,128]{1,0:T(8,128)S(1)}, u32[]{:S(2)}, u32[]{:S(2)}) collective-permute-start(f32[224,128]{1,0:T(8,128)S(1)} %get-tuple-element.56), channel_id=1, source_target_pairs={{0,2},{1,3},{2,0},{3,1},{4,6},{5,7},{6,4},{7,5},{8,10},{9,11},{10,... | collective-permute-start | bytes 344072 | tf_op jit(solution)/shard_map/ppermute | solution.py:44
  18.3 2.1 %collective-permute-done.5 = f32[224,128]{1,0:T(8,128)S(1)} collective-permute-done((f32[224,128]{1,0:T(8,128)S(1)}, f32[224,128]{1,0:T(8,128)S(1)}, u32[]{:S(2)}, u32[]{:S(2)}) %collective-permute-start.5) | collective-permute-done | bytes 114720 | tf_op jit(solution)/shard_map/ppermute | solution.py:44
  20.4 1.8 %collective-permute-done.6 = f32[224,128]{1,0:T(8,128)S(1)} collective-permute-done((f32[224,128]{1,0:T(8,128)S(1)}, f32[224,128]{1,0:T(8,128)S(1)}, u32[]{:S(2)}, u32[]{:S(2)}) %collective-permute-start.6) | collective-permute-done | bytes 114720 | tf_op jit(solution)/shard_map/ppermute | solution.py:44
  22.4 1.6 %collective-permute-done.7 = f32[672,128]{1,0:T(8,128)S(1)} collective-permute-done((f32[672,128]{1,0:T(8,128)S(1)}, f32[672,128]{1,0:T(8,128)S(1)}, u32[]{:S(2)}, u32[]{:S(2)}) %collective-permute-start.7) | collective-permute-done | bytes 344096 | tf_op jit(solution)/shard_map/ppermute | solution.py:44
  24.0 7.8 %first_forces.1 = (f32[48,128]{1,0:T(8,128)S(1)}, f32[48,128]{1,0:T(8,128)S(1)}, s32[32,128]{1,0:T(8,128)S(1)}) custom-call(f32[1792,128]{1,0:T(8,128)S(1)} %constant_dynamic-update-slice_fusion.3.gathered, f32[48,128]{1,0:T(8,128)S(1)} %copy-done), custom_call_target="tpu_custom_call" | custom-call | flops 4000000000 | bytes 1048576 | tf_op jit(solution)/shard_map/first_forces/pallas_call | solution.py:435
  33.5 4.4 %collective-permute-done.9 = f32[96,128]{1,0:T(8,128)S(1)} collective-permute-done((f32[96,128]{1,0:T(8,128)S(1)}, f32[96,128]{1,0:T(8,128)S(1)}, u32[]{:S(2)}, u32[]{:S(2)}) %collective-permute-start.9) | collective-permute-done | bytes 49184 | tf_op jit(solution)/shard_map/ppermute | solution.py:44
  38.0 2.2 %collective-permute-start.12 = (f32[192,128]{1,0:T(8,128)S(1)}, f32[192,128]{1,0:T(8,128)S(1)}, u32[]{:S(2)}, u32[]{:S(2)}) collective-permute-start(f32[192,128]{1,0:T(8,128)S(1)} %get-tuple-element.68), channel_id=1, source_target_pairs={{0,2},{1,3},{2,0},{3,1},{4,6},{5,7},{6,4},{7,5},{8,10},{9,11},{10,... | collective-permute-start | bytes 294920 | tf_op jit(solution)/shard_map/ppermute | solution.py:44
  43.0 2.9 %near_forces.3.near_sums = f32[256,128]{1,0:T(8,128)S(1)} custom-call(f32[384,128]{1,0:T(8,128)S(1)} %constant_dynamic-update-slice_fusion.12.near, f32[192,128]{1,0:T(8,128)S(1)} %collective-permute-done.12.part, s32[32,128]{1,0:T(8,128)S(1)} %get-tuple-element.28.words), custom_call_target="tpu_custom_call" | custom-call | flops 1000000000 | bytes 1048576 | tf_op jit(solution)/shard_map/near_forces/pallas_call | solution.py:449
  46.4 1.6 %collective-permute-done.15.far = f32[576,128]{1,0:T(8,128)S(1)} collective-permute-done((f32[576,128]{1,0:T(8,128)S(1)}, f32[576,128]{1,0:T(8,128)S(1)}, u32[]{:S(2)}, u32[]{:S(2)}) %collective-permute-start.15) | collective-permute-done | bytes 294944 | tf_op jit(solution)/shard_map/ppermute | solution.py:44
  48.0 4.5 %next_forces.2 = (f32[48,128]{1,0:T(8,128)S(1)}, f32[48,128]{1,0:T(8,128)S(1)}, f32[48,128]{1,0:T(8,128)S(1)}) custom-call(f32[384,128]{1,0:T(8,128)S(1)} %constant_dynamic-update-slice_fusion.12.near, f32[576,128]{1,0:T(8,128)S(1)} %constant_dynamic-update-slice_fusion.20.middle, f32[576,128]{1,0:T(8,128)S(1)} %collective-permute-done.15.far, ...), custom_call_target="tpu_custom_call" | custom-call | flops 3000000000 | bytes 1048576 | tf_op jit(solution)/shard_map/next_forces/pallas_call | solution.py:460
  52.7 3.2 %collective-permute-start.18 = (f32[48,128]{1,0:T(8,128)S(1)}, f32[48,128]{1,0:T(8,128)S(1)}, u32[]{:S(2)}, u32[]{:S(2)}) collective-permute-start(f32[48,128]{1,0:T(8,128)S(1)} %get-tuple-element.34), channel_id=1, source_target_pairs={{0,24},{1,25},{2,26},{3,27},{4,28},{5,29},{6,30},{7,31},{8,16},{9,... | collective-permute-start | bytes 73736 | tf_op jit(solution)/shard_map/ppermute | solution.py:44
  56.0 4.3 %collective-permute-done.17 = f32[96,128]{1,0:T(8,128)S(1)} collective-permute-done((f32[96,128]{1,0:T(8,128)S(1)}, f32[96,128]{1,0:T(8,128)S(1)}, u32[]{:S(2)}, u32[]{:S(2)}) %collective-permute-start.17) | collective-permute-done | bytes 49184 | tf_op jit(solution)/shard_map/ppermute | solution.py:44
  61.9 2.0 %collective-permute-start.22 = (f32[192,128]{1,0:T(8,128)S(1)}, f32[192,128]{1,0:T(8,128)S(1)}, u32[]{:S(2)}, u32[]{:S(2)}) collective-permute-start(f32[192,128]{1,0:T(8,128)S(1)} %get-tuple-element.64), channel_id=1, source_target_pairs={{0,6},{1,7},{2,4},{3,5},{4,2},{5,3},{6,0},{7,1},{8,14},{9,15},{10,... | collective-permute-start | bytes 294920 | tf_op jit(solution)/shard_map/ppermute | solution.py:44
  65.2 2.9 %near_forces.4.near_sums = f32[256,128]{1,0:T(8,128)S(1)} custom-call(f32[384,128]{1,0:T(8,128)S(1)} %constant_dynamic-update-slice_fusion.23.near, f32[192,128]{1,0:T(8,128)S(1)} %collective-permute-done.20.part, s32[32,128]{1,0:T(8,128)S(1)} %get-tuple-element.28.words), custom_call_target="tpu_custom_call" | custom-call | flops 1000000000 | bytes 1048576 | tf_op jit(solution)/shard_map/near_forces/pallas_call | solution.py:449
  68.4 1.6 %collective-permute-done.23.far = f32[576,128]{1,0:T(8,128)S(1)} collective-permute-done((f32[576,128]{1,0:T(8,128)S(1)}, f32[576,128]{1,0:T(8,128)S(1)}, u32[]{:S(2)}, u32[]{:S(2)}) %collective-permute-start.23) | collective-permute-done | bytes 294944 | tf_op jit(solution)/shard_map/ppermute | solution.py:44
  70.0 4.7 %next_forces.3 = (f32[48,128]{1,0:T(8,128)S(1)}, f32[48,128]{1,0:T(8,128)S(1)}, f32[48,128]{1,0:T(8,128)S(1)}) custom-call(f32[384,128]{1,0:T(8,128)S(1)} %constant_dynamic-update-slice_fusion.23.near, f32[576,128]{1,0:T(8,128)S(1)} %constant_dynamic-update-slice_fusion.31.middle, f32[576,128]{1,0:T(8,128)S(1)} %collective-permute-done.23.far, ...), custom_call_target="tpu_custom_call" | custom-call | flops 3000000000 | bytes 1048576 | tf_op jit(solution)/shard_map/next_forces/pallas_call | solution.py:460
  74.9 2.7 %collective-permute-start.26 = (f32[48,128]{1,0:T(8,128)S(1)}, f32[48,128]{1,0:T(8,128)S(1)}, u32[]{:S(2)}, u32[]{:S(2)}) collective-permute-start(f32[48,128]{1,0:T(8,128)S(1)} %get-tuple-element.41), channel_id=1, source_target_pairs={{0,24},{1,25},{2,26},{3,27},{4,28},{5,29},{6,30},{7,31},{8,16},{9,... | collective-permute-start | bytes 73736 | tf_op jit(solution)/shard_map/ppermute | solution.py:44
  77.7 4.3 %collective-permute-done.25 = f32[96,128]{1,0:T(8,128)S(1)} collective-permute-done((f32[96,128]{1,0:T(8,128)S(1)}, f32[96,128]{1,0:T(8,128)S(1)}, u32[]{:S(2)}, u32[]{:S(2)}) %collective-permute-start.25) | collective-permute-done | bytes 49184 | tf_op jit(solution)/shard_map/ppermute | solution.py:44
  82.1 2.1 %collective-permute-start.28 = (f32[192,128]{1,0:T(8,128)S(1)}, f32[192,128]{1,0:T(8,128)S(1)}, u32[]{:S(2)}, u32[]{:S(2)}) collective-permute-start(f32[192,128]{1,0:T(8,128)S(1)} %get-tuple-element.60), channel_id=1, source_target_pairs={{0,2},{1,3},{2,0},{3,1},{4,6},{5,7},{6,4},{7,5},{8,10},{9,11},{10,... | collective-permute-start | bytes 294920 | tf_op jit(solution)/shard_map/ppermute | solution.py:44
  87.3 2.9 %near_forces.5.near_sums = f32[256,128]{1,0:T(8,128)S(1)} custom-call(f32[384,128]{1,0:T(8,128)S(1)} %constant_dynamic-update-slice_fusion.34.near, f32[192,128]{1,0:T(8,128)S(1)} %collective-permute-done.28.part, s32[32,128]{1,0:T(8,128)S(1)} %get-tuple-element.28.words), custom_call_target="tpu_custom_call" | custom-call | flops 1000000000 | bytes 1048576 | tf_op jit(solution)/shard_map/near_forces/pallas_call | solution.py:449
  90.3 1.6 %collective-permute-done.31.far = f32[576,128]{1,0:T(8,128)S(1)} collective-permute-done((f32[576,128]{1,0:T(8,128)S(1)}, f32[576,128]{1,0:T(8,128)S(1)}, u32[]{:S(2)}, u32[]{:S(2)}) %collective-permute-start.31) | collective-permute-done | bytes 294944 | tf_op jit(solution)/shard_map/ppermute | solution.py:44
  91.9 5.1 %last_forces.1 = (f32[3,2048]{1,0:T(4,128)}, f32[3,2048]{1,0:T(4,128)}) custom-call(f32[384,128]{1,0:T(8,128)S(1)} %constant_dynamic-update-slice_fusion.34.near, f32[576,128]{1,0:T(8,128)S(1)} %constant_dynamic-update-slice_fusion.42.middle, f32[576,128]{1,0:T(8,128)S(1)} %collective-permute-done.31.far, f32[256,128]{1,0:T(8,128)S(1)} %near_forces.5.near_sums, ...), custom_call_target="tpu_custom_call" | custom-call | flops 3000000000 | bytes 1048576 | tf_op jit(solution)/shard_map/last_forces/pallas_call | solution.py:460
  (94 shorter events, 18.0 us)
Async XLA Ops:
  2.7 5.1 %collective-permute-start = (f32[56,128]{1,0:T(8,128)}, f32[56,128]{1,0:T(8,128)S(1)}, u32[]{:S(2)}, u32[]{:S(2)}) collective-permute-start(f32[56,128]{1,0:T(8,128)} %get-tuple-element.25), channel_id=1, source_target_pairs={{0,1},{1,0},{2,3},{3,2},{4,5},{5,4},{6,7},{7,6},{8,9},{9,8},{10,11... | collective-permute-start | bytes 86024 | tf_op jit(solution)/shard_map/ppermute | solution.py:44
  3.2 10.3 %collective-permute-start.2 = (f32[56,128]{1,0:T(8,128)}, f32[56,128]{1,0:T(8,128)S(1)}, u32[]{:S(2)}, u32[]{:S(2)}) collective-permute-start(f32[56,128]{1,0:T(8,128)} %get-tuple-element.25), channel_id=1, source_target_pairs={{0,24},{1,25},{2,26},{3,27},{4,28},{5,29},{6,30},{7,31},{8,16},{9,... | collective-permute-start | bytes 86024 | tf_op jit(solution)/shard_map/ppermute | solution.py:44
  8.6 4.8 %collective-permute-start.1 = (f32[112,128]{1,0:T(8,128)S(1)}, f32[112,128]{1,0:T(8,128)S(1)}, u32[]{:S(2)}, u32[]{:S(2)}) collective-permute-start(f32[112,128]{1,0:T(8,128)S(1)} %pad_maximum_fusion.5), channel_id=1, source_target_pairs={{0,8},{1,17},{2,10},{3,19},{4,12},{5,21},{6,14},{7,23},{8,0},{9,25... | collective-permute-start | bytes 172040 | tf_op jit(solution)/shard_map/ppermute | solution.py:44
  13.4 4.9 %collective-permute-start.4 = (f32[224,128]{1,0:T(8,128)S(1)}, f32[224,128]{1,0:T(8,128)S(1)}, u32[]{:S(2)}, u32[]{:S(2)}) collective-permute-start(f32[224,128]{1,0:T(8,128)S(1)} %get-tuple-element.56), channel_id=1, source_target_pairs={{0,2},{1,3},{2,0},{3,1},{4,6},{5,7},{6,4},{7,5},{8,10},{9,11},{10,... | collective-permute-start | bytes 344072 | tf_op jit(solution)/shard_map/ppermute | solution.py:44
  15.0 5.4 %collective-permute-start.5 = (f32[224,128]{1,0:T(8,128)S(1)}, f32[224,128]{1,0:T(8,128)S(1)}, u32[]{:S(2)}, u32[]{:S(2)}) collective-permute-start(f32[224,128]{1,0:T(8,128)S(1)} %get-tuple-element.56), channel_id=1, source_target_pairs={{0,4},{1,5},{2,6},{3,7},{4,0},{5,1},{6,2},{7,3},{8,12},{9,13},{10,... | collective-permute-start | bytes 344072 | tf_op jit(solution)/shard_map/ppermute | solution.py:44
  16.5 5.7 %collective-permute-start.6 = (f32[224,128]{1,0:T(8,128)S(1)}, f32[224,128]{1,0:T(8,128)S(1)}, u32[]{:S(2)}, u32[]{:S(2)}) collective-permute-start(f32[224,128]{1,0:T(8,128)S(1)} %get-tuple-element.56), channel_id=1, source_target_pairs={{0,6},{1,7},{2,4},{3,5},{4,2},{5,3},{6,0},{7,1},{8,14},{9,15},{10,... | collective-permute-start | bytes 344072 | tf_op jit(solution)/shard_map/ppermute | solution.py:44
  22.2 1.7 %collective-permute-start.7 = (f32[672,128]{1,0:T(8,128)S(1)}, f32[672,128]{1,0:T(8,128)S(1)}, u32[]{:S(2)}, u32[]{:S(2)}) collective-permute-start(f32[672,128]{1,0:T(8,128)S(1)} %pad_maximum_fusion), channel_id=1, source_target_pairs={{0,1},{1,0},{2,3},{3,2},{4,5},{5,4},{6,7},{7,6},{8,9},{9,8},{10,11... | collective-permute-start | bytes 1032200 | tf_op jit(solution)/shard_map/ppermute | solution.py:44
  32.0 5.9 %collective-permute-start.10 = (f32[48,128]{1,0:T(8,128)S(1)}, f32[48,128]{1,0:T(8,128)S(1)}, u32[]{:S(2)}, u32[]{:S(2)}) collective-permute-start(f32[48,128]{1,0:T(8,128)S(1)} %get-tuple-element.27), channel_id=1, source_target_pairs={{0,24},{1,25},{2,26},{3,27},{4,28},{5,29},{6,30},{7,31},{8,16},{9,... | collective-permute-start | bytes 73736 | tf_op jit(solution)/shard_map/ppermute | solution.py:44
  33.4 4.5 %collective-permute-start.9 = (f32[96,128]{1,0:T(8,128)S(1)}, f32[96,128]{1,0:T(8,128)S(1)}, u32[]{:S(2)}, u32[]{:S(2)}) collective-permute-start(f32[96,128]{1,0:T(8,128)S(1)} %pad_maximum_fusion.6), channel_id=1, source_target_pairs={{0,8},{1,17},{2,10},{3,19},{4,12},{5,21},{6,14},{7,23},{8,0},{9,25... | collective-permute-start | bytes 147464 | tf_op jit(solution)/shard_map/ppermute | solution.py:44
  38.0 5.1 %collective-permute-start.12 = (f32[192,128]{1,0:T(8,128)S(1)}, f32[192,128]{1,0:T(8,128)S(1)}, u32[]{:S(2)}, u32[]{:S(2)}) collective-permute-start(f32[192,128]{1,0:T(8,128)S(1)} %get-tuple-element.68), channel_id=1, source_target_pairs={{0,2},{1,3},{2,0},{3,1},{4,6},{5,7},{6,4},{7,5},{8,10},{9,11},{10,... | collective-permute-start | bytes 294920 | tf_op jit(solution)/shard_map/ppermute | solution.py:44
  40.2 5.7 %collective-permute-start.13 = (f32[192,128]{1,0:T(8,128)S(1)}, f32[192,128]{1,0:T(8,128)S(1)}, u32[]{:S(2)}, u32[]{:S(2)}) collective-permute-start(f32[192,128]{1,0:T(8,128)S(1)} %get-tuple-element.68), channel_id=1, source_target_pairs={{0,4},{1,5},{2,6},{3,7},{4,0},{5,1},{6,2},{7,3},{8,12},{9,13},{10,... | collective-permute-start | bytes 294920 | tf_op jit(solution)/shard_map/ppermute | solution.py:44
  40.8 5.5 %collective-permute-start.14 = (f32[192,128]{1,0:T(8,128)S(1)}, f32[192,128]{1,0:T(8,128)S(1)}, u32[]{:S(2)}, u32[]{:S(2)}) collective-permute-start(f32[192,128]{1,0:T(8,128)S(1)} %get-tuple-element.68), channel_id=1, source_target_pairs={{0,6},{1,7},{2,4},{3,5},{4,2},{5,3},{6,0},{7,1},{8,14},{9,15},{10,... | collective-permute-start | bytes 294920 | tf_op jit(solution)/shard_map/ppermute | solution.py:44
  52.5 3.4 %collective-permute-start.16 = (f32[48,128]{1,0:T(8,128)S(1)}, f32[48,128]{1,0:T(8,128)S(1)}, u32[]{:S(2)}, u32[]{:S(2)}) collective-permute-start(f32[48,128]{1,0:T(8,128)S(1)} %get-tuple-element.34), channel_id=1, source_target_pairs={{0,1},{1,0},{2,3},{3,2},{4,5},{5,4},{6,7},{7,6},{8,9},{9,8},{10,11... | collective-permute-start | bytes 73736 | tf_op jit(solution)/shard_map/ppermute | solution.py:44
  52.7 7.7 %collective-permute-start.18 = (f32[48,128]{1,0:T(8,128)S(1)}, f32[48,128]{1,0:T(8,128)S(1)}, u32[]{:S(2)}, u32[]{:S(2)}) collective-permute-start(f32[48,128]{1,0:T(8,128)S(1)} %get-tuple-element.34), channel_id=1, source_target_pairs={{0,24},{1,25},{2,26},{3,27},{4,28},{5,29},{6,30},{7,31},{8,16},{9,... | collective-permute-start | bytes 73736 | tf_op jit(solution)/shard_map/ppermute | solution.py:44
  55.9 4.4 %collective-permute-start.17 = (f32[96,128]{1,0:T(8,128)S(1)}, f32[96,128]{1,0:T(8,128)S(1)}, u32[]{:S(2)}, u32[]{:S(2)}) collective-permute-start(f32[96,128]{1,0:T(8,128)S(1)} %pad_maximum_fusion.7), channel_id=1, source_target_pairs={{0,8},{1,17},{2,10},{3,19},{4,12},{5,21},{6,14},{7,23},{8,0},{9,25... | collective-permute-start | bytes 147464 | tf_op jit(solution)/shard_map/ppermute | solution.py:44
  60.4 4.8 %collective-permute-start.20 = (f32[192,128]{1,0:T(8,128)S(1)}, f32[192,128]{1,0:T(8,128)S(1)}, u32[]{:S(2)}, u32[]{:S(2)}) collective-permute-start(f32[192,128]{1,0:T(8,128)S(1)} %get-tuple-element.64), channel_id=1, source_target_pairs={{0,2},{1,3},{2,0},{3,1},{4,6},{5,7},{6,4},{7,5},{8,10},{9,11},{10,... | collective-permute-start | bytes 294920 | tf_op jit(solution)/shard_map/ppermute | solution.py:44
  61.7 6.5 %collective-permute-start.21 = (f32[192,128]{1,0:T(8,128)S(1)}, f32[192,128]{1,0:T(8,128)S(1)}, u32[]{:S(2)}, u32[]{:S(2)}) collective-permute-start(f32[192,128]{1,0:T(8,128)S(1)} %get-tuple-element.64), channel_id=1, source_target_pairs={{0,4},{1,5},{2,6},{3,7},{4,0},{5,1},{6,2},{7,3},{8,12},{9,13},{10,... | collective-permute-start | bytes 294920 | tf_op jit(solution)/shard_map/ppermute | solution.py:44
  61.9 6.4 %collective-permute-start.22 = (f32[192,128]{1,0:T(8,128)S(1)}, f32[192,128]{1,0:T(8,128)S(1)}, u32[]{:S(2)}, u32[]{:S(2)}) collective-permute-start(f32[192,128]{1,0:T(8,128)S(1)} %get-tuple-element.64), channel_id=1, source_target_pairs={{0,6},{1,7},{2,4},{3,5},{4,2},{5,3},{6,0},{7,1},{8,14},{9,15},{10,... | collective-permute-start | bytes 294920 | tf_op jit(solution)/shard_map/ppermute | solution.py:44
  74.7 2.9 %collective-permute-start.24 = (f32[48,128]{1,0:T(8,128)S(1)}, f32[48,128]{1,0:T(8,128)S(1)}, u32[]{:S(2)}, u32[]{:S(2)}) collective-permute-start(f32[48,128]{1,0:T(8,128)S(1)} %get-tuple-element.41), channel_id=1, source_target_pairs={{0,1},{1,0},{2,3},{3,2},{4,5},{5,4},{6,7},{7,6},{8,9},{9,8},{10,11... | collective-permute-start | bytes 73736 | tf_op jit(solution)/shard_map/ppermute | solution.py:44
  74.9 7.2 %collective-permute-start.26 = (f32[48,128]{1,0:T(8,128)S(1)}, f32[48,128]{1,0:T(8,128)S(1)}, u32[]{:S(2)}, u32[]{:S(2)}) collective-permute-start(f32[48,128]{1,0:T(8,128)S(1)} %get-tuple-element.41), channel_id=1, source_target_pairs={{0,24},{1,25},{2,26},{3,27},{4,28},{5,29},{6,30},{7,31},{8,16},{9,... | collective-permute-start | bytes 73736 | tf_op jit(solution)/shard_map/ppermute | solution.py:44
  77.6 4.4 %collective-permute-start.25 = (f32[96,128]{1,0:T(8,128)S(1)}, f32[96,128]{1,0:T(8,128)S(1)}, u32[]{:S(2)}, u32[]{:S(2)}) collective-permute-start(f32[96,128]{1,0:T(8,128)S(1)} %pad_maximum_fusion.8), channel_id=1, source_target_pairs={{0,8},{1,17},{2,10},{3,19},{4,12},{5,21},{6,14},{7,23},{8,0},{9,25... | collective-permute-start | bytes 147464 | tf_op jit(solution)/shard_map/ppermute | solution.py:44
  82.1 5.2 %collective-permute-start.28 = (f32[192,128]{1,0:T(8,128)S(1)}, f32[192,128]{1,0:T(8,128)S(1)}, u32[]{:S(2)}, u32[]{:S(2)}) collective-permute-start(f32[192,128]{1,0:T(8,128)S(1)} %get-tuple-element.60), channel_id=1, source_target_pairs={{0,2},{1,3},{2,0},{3,1},{4,6},{5,7},{6,4},{7,5},{8,10},{9,11},{10,... | collective-permute-start | bytes 294920 | tf_op jit(solution)/shard_map/ppermute | solution.py:44
  84.1 6.0 %collective-permute-start.29 = (f32[192,128]{1,0:T(8,128)S(1)}, f32[192,128]{1,0:T(8,128)S(1)}, u32[]{:S(2)}, u32[]{:S(2)}) collective-permute-start(f32[192,128]{1,0:T(8,128)S(1)} %get-tuple-element.60), channel_id=1, source_target_pairs={{0,4},{1,5},{2,6},{3,7},{4,0},{5,1},{6,2},{7,3},{8,12},{9,13},{10,... | collective-permute-start | bytes 294920 | tf_op jit(solution)/shard_map/ppermute | solution.py:44
  84.1 6.1 %collective-permute-start.30 = (f32[192,128]{1,0:T(8,128)S(1)}, f32[192,128]{1,0:T(8,128)S(1)}, u32[]{:S(2)}, u32[]{:S(2)}) collective-permute-start(f32[192,128]{1,0:T(8,128)S(1)} %get-tuple-element.60), channel_id=1, source_target_pairs={{0,6},{1,7},{2,4},{3,5},{4,2},{5,3},{6,0},{7,1},{8,14},{9,15},{10,... | collective-permute-start | bytes 294920 | tf_op jit(solution)/shard_map/ppermute | solution.py:44
  (10 other events, 19.1 us)
